TPU v7x, 32 devices: a whole 2x2x4 slice. The times are simulated.
32 devices in a mesh: rep: 4 (over y, x), shard: 8 (over z, core).
Axes of the slice: x: 2, y: 2, z: 4, core: 2. Of those that a mesh axis runs over, the one named last changes fastest.
Arguments:
- latents: float32 [128, 16, 256], P(('rep', 'shard')), may hold values from -6 to 6
- target_noise: float32 [128, 16, 256], P(('rep', 'shard')), may hold values from -6 to 6
- labels: int32 [128], P(('rep', 'shard')), may hold values from 0 to 999
- time_steps: int32 [128], P(('rep', 'shard')), may hold values from 0 to 999
- inner_weights: float32 [2, 768, 10752], P(None, 'shard'), may hold values from -0.4330127 to 0.4330127
- outer_weights: float32 [2, 3086, 768], P(None, None, 'shard'), may hold values from -1.2 to 1.2
- embed_table: float32 [2043, 768], P(None, 'shard'), may hold values from -2 to 2
- final_mod: float32 [769, 1536], P(None, 'shard'), may hold values from -1.2 to 1.2
- head_weights: float32 [769, 16], replicated, may hold values from -0.21875 to 0.21875
- inner_moment: float32 [2, 768, 10752], P(None, 'shard'), may hold values from -3e-06 to 3e-06
- inner_square: float32 [2, 768, 10752], P(None, 'shard'), may hold values from 1e-15 to 1e-13
- outer_moment: float32 [2, 3086, 768], P(None, None, 'shard'), may hold values from -3e-06 to 3e-06
- outer_square: float32 [2, 3086, 768], P(None, None, 'shard'), may hold values from 1e-15 to 1e-13
- embed_moment: float32 [2043, 768], P(None, 'shard'), may hold values from -3e-06 to 3e-06
- embed_square: float32 [2043, 768], P(None, 'shard'), may hold values from 1e-15 to 1e-13
- final_moment: float32 [769, 1536], P(None, 'shard'), may hold values from -3e-06 to 3e-06
- final_square: float32 [769, 1536], P(None, 'shard'), may hold values from 1e-15 to 1e-13
- head_moment: float32 [769, 16], replicated, may hold values from -3e-06 to 3e-06
- head_square: float32 [769, 16], replicated, may hold values from 1e-15 to 1e-13
Outputs:
- mean_loss: float32 [], replicated
- grad_norm: float32 [], replicated
- inner_new: float32 [2, 768, 10752], P(None, 'shard')
- inner_moment_new: float32 [2, 768, 10752], P(None, 'shard')
- inner_square_new: float32 [2, 768, 10752], P(None, 'shard')
- inner_copy: bfloat16 [2, 768, 10752], P(None, 'shard')
- outer_new: float32 [2, 3086, 768], P(None, None, 'shard')
- outer_moment_new: float32 [2, 3086, 768], P(None, None, 'shard')
- outer_square_new: float32 [2, 3086, 768], P(None, None, 'shard')
- outer_copy: bfloat16 [2, 3086, 768], P(None, None, 'shard')
- embed_new: float32 [2043, 768], P(None, 'shard')
- embed_moment_new: float32 [2043, 768], P(None, 'shard')
- embed_square_new: float32 [2043, 768], P(None, 'shard')
- embed_copy: bfloat16 [2043, 768], P(None, 'shard')
- final_new: float32 [769, 1536], P(None, 'shard')
- final_moment_new: float32 [769, 1536], P(None, 'shard')
- final_square_new: float32 [769, 1536], P(None, 'shard')
- final_copy: bfloat16 [769, 1536], P(None, 'shard')
- head_new: float32 [769, 16], replicated
- head_moment_new: float32 [769, 16], replicated
- head_square_new: float32 [769, 16], replicated
- head_copy: bfloat16 [769, 16], replicated
All inputs are finite; a program needn't handle non-finite values.
Results may differ from a plain program's by a relative error of at most 0.0045.
The roundings to bfloat16 on the way count: a program that leaves them out, or rounds other values in their place, can miss the bound.
Values may be sent and summed in bfloat16 or wider, within the bound.
A program may use at most 384 MiB of HBM per device.

v0:
```python
import math

import jax
import jax.numpy as jnp
from jax import lax
from jax.sharding import PartitionSpec as P

D = 768
HEADS = 12
HDIM = 64
FF = 3072
FREQ = 256
NCLASS = 1000
P_SIZE = 16
GRID = 16
LAYERS = 2
LAT_DEV = 4
TOK = 256


norm_eps = 1e-06
clip_coef = 2.5
beta_one = 0.9
beta_two = 0.999
adam_eps = 1e-08
learn_rate = 0.01
weight_decay = 0.01
step_count = 10.0


def noise_levels():
    beta_line = 0.0001 + (0.02 - 0.0001) * jnp.arange(1000, dtype=jnp.float32) / 999.0
    cumulative = jnp.exp(jnp.cumsum(jnp.log(1.0 - beta_line)))
    return (jnp.sqrt(cumulative), jnp.sqrt(1.0 - cumulative))


def position_table(grid_side, feature_width):
    quarter = feature_width // 4
    omega_rate = jnp.exp(-math.log(10000.0) * jnp.arange(quarter, dtype=jnp.float32) / quarter)
    cell_ids = jnp.arange(grid_side * grid_side, dtype=jnp.int32)
    across = (cell_ids % grid_side).astype(jnp.float32)[:, None] * omega_rate[None, :]
    downward = (cell_ids // grid_side).astype(jnp.float32)[:, None] * omega_rate[None, :]
    return jnp.concatenate(
        [jnp.sin(across), jnp.cos(across), jnp.sin(downward), jnp.cos(downward)], axis=1
    )


def time_features(step_ids, feature_count):
    half_count = feature_count // 2
    frequency = jnp.exp(-math.log(10000.0) * jnp.arange(half_count, dtype=jnp.float32) / half_count)
    angles = step_ids.astype(jnp.float32)[:, None] * frequency[None, :]
    return jnp.concatenate([jnp.cos(angles), jnp.sin(angles)], axis=1)


def modulate(stream, shift_by, scale_by):
    center = stream - jnp.mean(stream, axis=-1, keepdims=True)
    spread = jnp.mean(center * center, axis=-1, keepdims=True)
    return (
        center * lax.rsqrt(spread + norm_eps) * (1.0 + scale_by[:, None, :]) + shift_by[:, None, :]
    )


def gelu_tanh(inputs):
    return jax.nn.gelu(inputs, approximate=True)


def adam_update(weights, gradient, moment, square, factor):
    scaled = gradient * factor
    moment_new = beta_one * moment + (1.0 - beta_one) * scaled
    square_new = beta_two * square + (1.0 - beta_two) * scaled * scaled
    moment_hat = moment_new / (1.0 - beta_one**step_count)
    square_hat = square_new / (1.0 - beta_two**step_count)
    updated = weights - learn_rate * (
        moment_hat / (jnp.sqrt(square_hat) + adam_eps) + weight_decay * weights
    )
    return (updated, moment_new, square_new, updated.astype(jnp.bfloat16))


def contract(pattern, left, right):
    return jnp.einsum(pattern, left, right, preferred_element_type=jnp.float32)


def split_heads(tensor):
    return tensor.reshape(tensor.shape[0], tensor.shape[1], HEADS, HDIM)


def attend(queries, keys_all, values_all):
    scores = contract("gqhe,gkhe->ghqk", split_heads(queries), split_heads(keys_all)) * HDIM ** (
        -0.5
    )
    highest_score = jnp.max(scores, axis=-1, keepdims=True)
    exponent = jnp.exp(scores - highest_score)
    row_total = jnp.sum(exponent, axis=-1, keepdims=True)
    probs = (exponent / row_total).astype(jnp.bfloat16)
    mixed = contract("ghqk,gkhe->gqhe", probs, split_heads(values_all))
    return (mixed.reshape(queries.shape).astype(jnp.bfloat16), highest_score + jnp.log(row_total))


def attend_back(queries, keys_all, values_all, log_total, grad_mixed):
    head_queries = split_heads(queries)
    head_keys = split_heads(keys_all)
    head_grad = split_heads(grad_mixed)
    scores = contract("gqhe,gkhe->ghqk", head_queries, head_keys) * HDIM ** (-0.5)
    probs = jnp.exp(scores - log_total)
    grad_probs = contract("gqhe,gkhe->ghqk", head_grad, split_heads(values_all))
    grad_values = contract("ghqk,gqhe->gkhe", probs.astype(jnp.bfloat16), head_grad)
    grad_scores = probs * (grad_probs - jnp.sum(probs * grad_probs, axis=-1, keepdims=True))
    scores_low = grad_scores.astype(jnp.bfloat16)
    grad_queries = contract("ghqk,gkhe->gqhe", scores_low, head_keys) * HDIM ** (-0.5)
    grad_keys = contract("ghqk,gqhe->gkhe", scores_low, head_queries) * HDIM ** (-0.5)
    return (
        grad_queries.reshape(queries.shape),
        grad_keys.reshape(queries.shape),
        grad_values.reshape(queries.shape),
    )


def layer_forward(stream, cond_act, inner_full, outer_full):
    blocks = FF // D
    bias_rows = outer_full[FF:].astype(jnp.float32)
    modul = contract("gd,de->ge", cond_act, inner_full[:, 4 * D + FF :]) + bias_rows[
        3 + blocks : 9 + blocks
    ].reshape(-1)
    shift_one, scale_one, gate_one, shift_two, scale_two, gate_two = jnp.split(modul, 6, axis=1)
    normed = modulate(stream, shift_one, scale_one).astype(jnp.bfloat16)
    projected = contract("gtd,de->gte", normed, inner_full[:, : 3 * D])
    queries = (projected[..., :D] + bias_rows[0]).astype(jnp.bfloat16)
    keys_all = projected[..., D : 2 * D].astype(jnp.bfloat16)
    values_all = (projected[..., 2 * D :] + bias_rows[1]).astype(jnp.bfloat16)
    mixed, log_total = attend(queries, keys_all, values_all)
    attn_out = contract("gtd,de->gte", mixed, inner_full[:, 3 * D : 4 * D]) + bias_rows[2]
    middle = stream + gate_one[:, None, :] * attn_out
    normed_two = modulate(middle, shift_two, scale_two).astype(jnp.bfloat16)
    upper = contract("gtd,de->gte", normed_two, inner_full[:, 4 * D : 4 * D + FF]) + bias_rows[
        3 : 3 + blocks
    ].reshape(-1)
    activ = gelu_tanh(upper).astype(jnp.bfloat16)
    down_out = contract("gtf,fd->gtd", activ, outer_full[:FF]) + bias_rows[9 + blocks]
    result = middle + gate_two[:, None, :] * down_out
    saved = (
        stream,
        modul,
        normed,
        queries,
        keys_all,
        values_all,
        log_total,
        mixed,
        attn_out,
        middle,
        normed_two,
        upper,
        activ,
        down_out,
    )
    return (result, saved)


def layer_backward(grad_stream, cond_act, inner_full, outer_full, saved):
    blocks = FF // D
    (
        stream,
        modul,
        normed,
        queries,
        keys_all,
        values_all,
        log_total,
        mixed,
        attn_out,
        middle,
        normed_two,
        upper,
        activ,
        down_out,
    ) = saved
    shift_one, scale_one, gate_one, shift_two, scale_two, gate_two = jnp.split(modul, 6, axis=1)
    grad_down = grad_stream * gate_two[:, None, :]
    grad_gate_two = jnp.sum(grad_stream * down_out, axis=1)
    down_low = grad_down.astype(jnp.bfloat16)
    second_grad = contract("gtf,gtd->fd", activ, down_low)
    grad_activ = contract("gtd,fd->gtf", down_low, outer_full[:FF])
    grad_upper = jax.vjp(gelu_tanh, upper)[1](grad_activ)[0]
    upper_low = grad_upper.astype(jnp.bfloat16)
    first_grad = contract("gtd,gtf->df", normed_two, upper_low)
    grad_normed_two = contract("gtf,df->gtd", upper_low, inner_full[:, 4 * D : 4 * D + FF])
    pull_two = jax.vjp(modulate, middle, shift_two, scale_two)[1]
    grad_middle_norm, grad_shift_two, grad_scale_two = pull_two(grad_normed_two)
    grad_middle = grad_stream + grad_middle_norm
    grad_attn = grad_middle * gate_one[:, None, :]
    grad_gate_one = jnp.sum(grad_middle * attn_out, axis=1)
    attn_low = grad_attn.astype(jnp.bfloat16)
    proj_grad = contract("gtd,gte->de", mixed, attn_low)
    grad_mixed = contract("gte,de->gtd", attn_low, inner_full[:, 3 * D : 4 * D]).astype(
        jnp.bfloat16
    )
    grad_queries, grad_keys, grad_values = attend_back(
        queries, keys_all, values_all, log_total, grad_mixed
    )
    queries_low = grad_queries.astype(jnp.bfloat16)
    values_low = grad_values.astype(jnp.bfloat16)
    qkv_low = jnp.concatenate([queries_low, grad_keys.astype(jnp.bfloat16), values_low], axis=-1)
    qkv_grad = contract("gtd,gte->de", normed, qkv_low)
    grad_normed = contract("gte,de->gtd", qkv_low, inner_full[:, : 3 * D])
    pull_one = jax.vjp(modulate, stream, shift_one, scale_one)[1]
    grad_stream_norm, grad_shift_one, grad_scale_one = pull_one(grad_normed)
    grad_input = grad_middle + grad_stream_norm
    grad_modul = jnp.concatenate(
        [
            grad_shift_one,
            grad_scale_one,
            grad_gate_one,
            grad_shift_two,
            grad_scale_two,
            grad_gate_two,
        ],
        axis=1,
    )
    modul_low = grad_modul.astype(jnp.bfloat16)
    ada_grad = contract("gd,ge->de", cond_act, modul_low)
    grad_cond = contract("ge,de->gd", modul_low, inner_full[:, 4 * D + FF :])
    query_bias = jnp.sum(queries_low.astype(jnp.float32), axis=(0, 1))
    value_bias = jnp.sum(values_low.astype(jnp.float32), axis=(0, 1))
    proj_bias = jnp.sum(grad_attn, axis=(0, 1))
    first_bias = jnp.sum(grad_upper, axis=(0, 1)).reshape(blocks, D)
    ada_bias = jnp.sum(grad_modul, axis=0).reshape(6, D)
    second_bias = jnp.sum(grad_down, axis=(0, 1))
    inner_grad = jnp.concatenate([qkv_grad, proj_grad, first_grad, ada_grad], axis=1)
    outer_grad = jnp.concatenate(
        [
            second_grad,
            query_bias[None],
            value_bias[None],
            proj_bias[None],
            first_bias,
            ada_bias,
            second_bias[None],
        ],
        axis=0,
    )
    return (grad_input, grad_cond, inner_grad, outer_grad)


def per_device(
    latents,
    target_noise,
    labels,
    time_steps,
    inner_weights,
    outer_weights,
    embed_table,
    final_mod,
    head_weights,
    inner_moment,
    inner_square,
    outer_moment,
    outer_square,
    embed_moment,
    embed_square,
    final_moment,
    final_square,
    head_moment,
    head_square,
):
    n_rep = lax.axis_size("rep")
    n_shard = lax.axis_size("shard")
    latent_total = LAT_DEV * n_rep * n_shard
    element_count = latent_total * TOK * P_SIZE
    signal_table, noise_table = noise_levels()
    level_ids = jnp.arange(1000, dtype=jnp.int32)
    picked = (time_steps[:, None] == level_ids[None, :]).astype(jnp.float32)
    signal_rate = jnp.sum(picked * signal_table[None, :], axis=1)
    noise_rate = jnp.sum(picked * noise_table[None, :], axis=1)
    patches = (
        signal_rate[:, None, None] * latents + noise_rate[:, None, None] * target_noise
    ).astype(jnp.bfloat16)
    embed_full, final_full = (
        lax.all_gather(embed_table.astype(jnp.bfloat16), "shard", axis=1, tiled=True),
        lax.all_gather(final_mod.astype(jnp.bfloat16), "shard", axis=1, tiled=True),
    )
    row_time = P_SIZE + 1
    row_second = P_SIZE + 2 + FREQ
    row_class = P_SIZE + 3 + FREQ + D
    stream = (
        contract("gpt,pd->gtd", patches, embed_full[:P_SIZE])
        + embed_full[P_SIZE].astype(jnp.float32)
        + position_table(GRID, D)[None]
    )
    features = time_features(time_steps, FREQ).astype(jnp.bfloat16)
    time_hidden = contract(
        "gf,fd->gd", features, embed_full[row_time : row_time + FREQ]
    ) + embed_full[row_time + FREQ].astype(jnp.float32)
    time_act = jax.nn.silu(time_hidden).astype(jnp.bfloat16)
    class_rows = jnp.take(embed_full[row_class:], labels, axis=0).astype(jnp.float32)
    second = contract("gd,de->ge", time_act, embed_full[row_second : row_second + D]) + embed_full[
        row_second + D
    ].astype(jnp.float32)
    condition = second + class_rows
    cond_act = jax.nn.silu(condition).astype(jnp.bfloat16)
    kept_weights = []
    kept_states = []
    for layer_idx in range(LAYERS):
        inner_full, outer_full = (
            lax.all_gather(
                inner_weights[layer_idx].astype(jnp.bfloat16), "shard", axis=0, tiled=True
            ),
            lax.all_gather(
                outer_weights[layer_idx].astype(jnp.bfloat16), "shard", axis=1, tiled=True
            ),
        )
        stream, saved = layer_forward(stream, cond_act, inner_full, outer_full)
        kept_weights.append((inner_full, outer_full))
        kept_states.append(saved)
    fin_mod = contract("gd,de->ge", cond_act, final_full[:D]) + final_full[D].astype(jnp.float32)
    fin_shift, fin_scale = jnp.split(fin_mod, 2, axis=1)
    fin_normed = modulate(stream, fin_shift, fin_scale).astype(jnp.bfloat16)
    head_low = head_weights.astype(jnp.bfloat16)
    output = contract("gtd,dp->gtp", fin_normed, head_low[:D]) + head_low[D].astype(jnp.float32)
    differ = output - jnp.swapaxes(target_noise, 1, 2)
    loss_part = jnp.sum(differ * differ) / element_count
    grad_output = 2.0 * (differ * (1.0 / element_count))
    head_bias = jnp.sum(grad_output, axis=(0, 1))
    output_low = grad_output.astype(jnp.bfloat16)
    head_grad = jnp.concatenate(
        [contract("gtd,gtp->dp", fin_normed, output_low), head_bias[None]], axis=0
    )
    grad_fin_normed = contract("gtp,dp->gtd", output_low, head_low[:D])
    pull_final = jax.vjp(modulate, stream, fin_shift, fin_scale)[1]
    grad_stream, grad_fin_shift, grad_fin_scale = pull_final(grad_fin_normed)
    grad_fin_mod = jnp.concatenate([grad_fin_shift, grad_fin_scale], axis=1)
    fin_low = grad_fin_mod.astype(jnp.bfloat16)
    final_grad = jnp.concatenate(
        [contract("gd,ge->de", cond_act, fin_low), jnp.sum(grad_fin_mod, axis=0)[None]], axis=0
    )
    grad_cond = contract("ge,de->gd", fin_low, final_full[:D])
    head_total, mean_loss = lax.psum((head_grad, loss_part), ("rep", "shard"))
    inner_parts = [None] * LAYERS
    outer_parts = [None] * LAYERS
    for layer_idx in range(LAYERS - 1, -1, -1):
        inner_full, outer_full = (
            lax.all_gather(
                inner_weights[layer_idx].astype(jnp.bfloat16), "shard", axis=0, tiled=True
            ),
            lax.all_gather(
                outer_weights[layer_idx].astype(jnp.bfloat16), "shard", axis=1, tiled=True
            ),
        )
        grad_stream, cond_part, inner_grad, outer_grad = layer_backward(
            grad_stream, cond_act, inner_full, outer_full, kept_states[layer_idx]
        )
        grad_cond = grad_cond + cond_part
        inner_part, outer_part = (
            lax.psum_scatter(inner_grad, "shard", scatter_dimension=0, tiled=True),
            lax.psum_scatter(outer_grad, "shard", scatter_dimension=1, tiled=True),
        )
        inner_part, outer_part = lax.psum((inner_part, outer_part), "rep")
        inner_parts[layer_idx] = inner_part
        outer_parts[layer_idx] = outer_part
    grad_condition = jax.vjp(jax.nn.silu, condition)[1](grad_cond)[0]
    second_bias = jnp.sum(grad_condition, axis=0)
    condition_low = grad_condition.astype(jnp.bfloat16)
    second_grad = contract("gd,ge->de", time_act, condition_low)
    grad_time_act = contract("ge,de->gd", condition_low, embed_full[row_second : row_second + D])
    grad_time = jax.vjp(jax.nn.silu, time_hidden)[1](grad_time_act)[0]
    time_bias = jnp.sum(grad_time, axis=0)
    time_grad = contract("gf,gd->fd", features, grad_time.astype(jnp.bfloat16))
    class_ids = jnp.arange(NCLASS, dtype=jnp.int32)
    one_hot = (labels[:, None] == class_ids[None, :]).astype(jnp.float32)
    class_grad = jnp.einsum("gc,gd->cd", one_hot, grad_condition, precision=lax.Precision.HIGHEST)
    patch_bias = jnp.sum(grad_stream, axis=(0, 1))
    patch_grad = contract("gpt,gtd->pd", patches, grad_stream.astype(jnp.bfloat16))
    embed_grad = jnp.concatenate(
        [
            patch_grad,
            patch_bias[None],
            time_grad,
            time_bias[None],
            second_grad,
            second_bias[None],
            class_grad,
        ],
        axis=0,
    )
    embed_part, final_part = (
        lax.psum_scatter(embed_grad, "shard", scatter_dimension=1, tiled=True),
        lax.psum_scatter(final_grad, "shard", scatter_dimension=1, tiled=True),
    )
    embed_part, final_part = lax.psum((embed_part, final_part), "rep")
    inner_all = jnp.stack(inner_parts)
    outer_all = jnp.stack(outer_parts)
    local_square = (
        jnp.sum(inner_all * inner_all)
        + jnp.sum(outer_all * outer_all)
        + jnp.sum(embed_part * embed_part)
        + jnp.sum(final_part * final_part)
    )
    shard_square = lax.psum(local_square, "shard")
    grad_norm = jnp.sqrt(shard_square + jnp.sum(head_total * head_total))
    limit = clip_coef * math.sqrt(D / element_count)
    factor = jnp.minimum(1.0, limit / grad_norm)
    inner_out = adam_update(inner_weights, inner_all, inner_moment, inner_square, factor)
    outer_out = adam_update(outer_weights, outer_all, outer_moment, outer_square, factor)
    embed_out = adam_update(embed_table, embed_part, embed_moment, embed_square, factor)
    final_out = adam_update(final_mod, final_part, final_moment, final_square, factor)
    head_out = adam_update(head_weights, head_total, head_moment, head_square, factor)
    return (
        mean_loss,
        grad_norm,
        inner_out[0],
        inner_out[1],
        inner_out[2],
        inner_out[3],
        outer_out[0],
        outer_out[1],
        outer_out[2],
        outer_out[3],
        embed_out[0],
        embed_out[1],
        embed_out[2],
        embed_out[3],
        final_out[0],
        final_out[1],
        final_out[2],
        final_out[3],
        head_out[0],
        head_out[1],
        head_out[2],
        head_out[3],
    )


def solution(mesh):
    in_specs = (
        P(("rep", "shard"), None, None),
        P(("rep", "shard"), None, None),
        P(("rep", "shard")),
        P(("rep", "shard")),
        P(None, "shard", None),
        P(None, None, "shard"),
        P(None, "shard"),
        P(None, "shard"),
        P(),
        P(None, "shard", None),
        P(None, "shard", None),
        P(None, None, "shard"),
        P(None, None, "shard"),
        P(None, "shard"),
        P(None, "shard"),
        P(None, "shard"),
        P(None, "shard"),
        P(),
        P(),
    )
    out_specs = (
        P(),
        P(),
        P(None, "shard", None),
        P(None, "shard", None),
        P(None, "shard", None),
        P(None, "shard", None),
        P(None, None, "shard"),
        P(None, None, "shard"),
        P(None, None, "shard"),
        P(None, None, "shard"),
        P(None, "shard"),
        P(None, "shard"),
        P(None, "shard"),
        P(None, "shard"),
        P(None, "shard"),
        P(None, "shard"),
        P(None, "shard"),
        P(None, "shard"),
        P(),
        P(),
        P(),
        P(),
    )
    return jax.shard_map(
        per_device, mesh=mesh, in_specs=in_specs, out_specs=out_specs, check_vma=False
    )
```

profile of v0, /device:TPU:0, one launch (start us, length us, event | category | flops | bytes accessed | tf_op | source)
XLA Modules:
  0.0 2123.4 jit_solution(17177163438149190118)
XLA Ops:
  24.8 23.2 %all-gather.13.cloned.1.call-done = bf16[769,1536]{0,1:T(8,128)(2,1)} async-done(((bf16[769,192]{0,1:T(8,128)(2,1)}), bf16[769,1536]{0,1:T(8,128)(2,1)}) %all-gather.13.cloned.1.call-update) | async-done | bytes 2362384 | tf_op jit(solution)/shard_map/all_gather | solution.py:279
  49.2 38.3 %all-gather.11.cloned.1.call-done = bf16[2043,768]{0,1:T(8,128)(2,1)} async-done(((bf16[2043,96]{0,1:T(8,128)(2,1)}), bf16[2043,768]{0,1:T(8,128)(2,1)}) %all-gather.11.cloned.1.call-update) | async-done | bytes 3138064 | tf_op jit(solution)/shard_map/all_gather | solution.py:278
  99.7 42.2 %all-gather.21.cloned.1.call-done = bf16[1,3086,768]{1,2,0:T(8,128)(2,1)} async-done(((bf16[1,3086,96]{1,2,0:T(8,128)(2,1)}), bf16[1,3086,768]{1,2,0:T(8,128)(2,1)}) %all-gather.21.cloned.1.call-update) | async-done | bytes 4740112 | tf_op jit(solution)/shard_map/all_gather | solution.py:307
  144.7 51.4 %all-gather.17.cloned.1.call-done = bf16[1,3086,768]{1,2,0:T(8,128)(2,1)} async-done(((bf16[1,3086,96]{1,2,0:T(8,128)(2,1)}), bf16[1,3086,768]{1,2,0:T(8,128)(2,1)}) %all-gather.17.cloned.1.call-update) | async-done | bytes 4740112 | tf_op jit(solution)/shard_map/all_gather | solution.py:307
  215.8 130.2 %all-gather.15.cloned.1.call-done = bf16[1,768,10752]{2,1,0:T(8,128)(2,1)} async-done(((bf16[1,96,10752]{2,1,0:T(8,128)(2,1)}), bf16[1,768,10752]{2,1,0:T(8,128)(2,1)}) %all-gather.15.cloned.1.call-update) | async-done | bytes 16515088 | tf_op jit(solution)/shard_map/all_gather | solution.py:304
  350.1 145.2 %all-gather.19.cloned.1.call-done = bf16[1,768,10752]{2,1,0:T(8,128)(2,1)} async-done(((bf16[1,96,10752]{2,1,0:T(8,128)(2,1)}), bf16[1,768,10752]{2,1,0:T(8,128)(2,1)}) %all-gather.19.cloned.1.call-update) | async-done | bytes 16515088 | tf_op jit(solution)/shard_map/all_gather | solution.py:304
  536.6 12.0 fusion.46
  548.7 12.5 fusion.168
  561.7 6.7 fusion.60
  595.5 11.0 fusion.48
  606.5 13.8 fusion.166
  628.6 19.1 fusion.175
  647.8 8.9 multiply_reduce_fusion.17
  670.3 9.3 convert_reduce_fusion
  679.7 9.0 multiply_reduce_fusion.1
  688.7 7.2 multiply_convert_fusion.1
  720.4 7.1 multiply_reduce_fusion.16
  732.4 15.4 fusion.174
  747.9 10.0 multiply_reduce_fusion.15
  769.4 8.8 convert_reduce_fusion.2
  780.7 8.9 multiply_reduce_fusion
  789.7 7.1 multiply_convert_fusion
  802.5 6.4 multiply_convert_fusion.4
  811.6 8.4 multiply_reduce_fusion.6
  843.5 22.2 %concatenate.54 = f32[2043,768]{1,0:T(8,128)} concatenate(f32[16,768]{1,0:T(8,128)S(1)} %fusion.79, f32[1,768]{1,0:T(1,128)S(1)} %broadcast_in_dim.79, f32[256,768]{1,0:T(8,128)} %fusion.121, f32[1,768]{1,0:T(1,128)S(1)} %broadcast_in_dim.80, f32[768,768]{1,0:T(8,128)} %fusion.129, f32[1,768]{1,0:T(1,128)S(1)} %broadcast_in_dim.81, f32[1000,768]{1,0:T(8,128)} %fusion.109), dimensions={0} | concatenate | bytes 12552192 | tf_op jit(solution)/shard_map/concatenate | solution.py:372
  865.8 6.6 copy.464
  873.3 14.3 convolution_bitcast_fusion
  887.7 25.3 %concatenate.52 = f32[3086,768]{1,0:T(8,128)} concatenate(f32[3072,768]{1,0:T(8,128)} %convolution_bitcast_fusion, f32[1,768]{1,0:T(1,128)S(1)} %broadcast_in_dim.73, f32[1,768]{1,0:T(1,128)S(1)} %broadcast_in_dim.74, f32[1,768]{1,0:T(1,128)S(1)} %broadcast_in_dim.75, f32[4,768]{1,0:T(4,128)S(1)} %reshape.404, f32[6,768]{1,0:T(8,128)S(1)} %reshape.405, f32[1,768]{1,0:T(1,128)S(1)} %broadcast_in_dim.76), dimensions={0} | concatenate | bytes 18960384 | tf_op jit(solution)/shard_map/concatenate | solution.py:229
  912.9 10.5 copy.462
  923.7 14.1 convolution_bitcast_fusion.1
  937.8 25.3 %concatenate.51 = f32[3086,768]{1,0:T(8,128)} concatenate(f32[3072,768]{1,0:T(8,128)} %convolution_bitcast_fusion.1, f32[1,768]{1,0:T(1,128)S(1)} %broadcast_in_dim.69, f32[1,768]{1,0:T(1,128)S(1)} %broadcast_in_dim.70, f32[1,768]{1,0:T(1,128)S(1)} %broadcast_in_dim.71, f32[4,768]{1,0:T(4,128)S(1)} %reshape.402, f32[6,768]{1,0:T(8,128)S(1)} %reshape.403, ...), dimensions={0} | concatenate | bytes 18960384 | tf_op jit(solution)/shard_map/concatenate | solution.py:229
  963.1 10.4 copy.460
  979.3 8.8 fusion.107
  988.1 7.2 convolution_bitcast_fusion.5
  995.4 8.3 convolution_bitcast_fusion.3
  1003.6 22.6 %pad_maximum_fusion = f32[768,10752]{1,0:T(8,128)} fusion(f32[768,4608]{1,0:T(8,128)} %fusion.107, f32[768,3072]{1,0:T(8,128)} %convolution_bitcast_fusion.3, f32[768,768]{1,0:T(8,128)} %convolution_bitcast_fusion.7, f32[768,2304]{1,0:T(8,128)} %convolution_bitcast_fusion.5), kind=kLoop, calls=%fused_computation.1 | loop fusion | flops 24772608 | bytes 66060288 | tf_op jit(solution)/shard_map/concatenate | solution.py:228
  1032.4 8.6 fusion.104
  1041.1 7.3 convolution_bitcast_fusion.4
  1048.5 8.4 convolution_bitcast_fusion.2
  1056.9 21.6 %pad_maximum_fusion.1 = f32[768,10752]{1,0:T(8,128)} fusion(f32[768,4608]{1,0:T(8,128)} %fusion.104, f32[768,3072]{1,0:T(8,128)} %convolution_bitcast_fusion.2, f32[768,768]{1,0:T(8,128)S(1)} %copy-done.46, f32[768,2304]{1,0:T(8,128)} %convolution_bitcast_fusion.4), kind=kLoop, calls=%fused_computation.2 | loop fusion | flops 24772608 | bytes 66060288 | tf_op jit(solution)/shard_map/concatenate | solution.py:228
  1080.9 68.0 %reduce-scatter.19.cloned.1.call-done = f32[96,3086]{1,0:T(8,128)} async-done(((f32[768,3086]{1,0:T(8,128)}), f32[96,3086]{1,0:T(8,128)}) %reduce-scatter.19.cloned.1.call-update) | async-done | bytes 1185040
  1148.9 321.4 %reduce-scatter.15.cloned.1.call-done = f32[96,10752]{1,0:T(8,128)} async-done(((f32[768,10752]{1,0:T(8,128)}), f32[96,10752]{1,0:T(8,128)}) %reduce-scatter.15.cloned.1.call-update) | async-done | bytes 4128784 | tf_op jit(solution)/shard_map/reduce_scatter | solution.py:353
  1470.3 321.4 %reduce-scatter.17.cloned.1.call-done = f32[96,10752]{1,0:T(8,128)} async-done(((f32[768,10752]{1,0:T(8,128)}), f32[96,10752]{1,0:T(8,128)}) %reduce-scatter.17.cloned.1.call-update) | async-done | bytes 4128784 | tf_op jit(solution)/shard_map/reduce_scatter | solution.py:353
  1800.2 39.3 %all-reduce.1 = (f32[]{:T(128)}, f32[769,16]{0,1:T(8,128)S(1)}) all-reduce(f32[]{:T(128)S(6)} %div.265, f32[769,16]{0,1:T(8,128)S(1)} %pad_maximum_fusion.10), channel_id=1, replica_groups=mesh['rep'=4,'shard'=8] {'rep','shard'}, use_global_device_ids=true, to_apply=%region_19.20 | all-reduce | flops 12305 | bytes 98440 | tf_op jit(solution)/shard_map/psum | solution.py:336
  1839.5 195.7 %all-reduce.5.cloned.1.call-done = (f32[1,96,10752]{2,1,0:T(8,128)}, f32[1,96,10752]{2,1,0:T(8,128)}, f32[1,3086,96]{1,2,0:T(8,128)}, f32[1,3086,96]{1,2,0:T(8,1...) async-done(((f32[1,96,10752]{2,1,0:T(8,128)}, f32[1,96,10752]{2,1,0:T(8,128)}, f32[1,3086,96]{1,2,0:T(8,128)}, f32[1,3086,96]{1,2,0:T(8,128)}, f32[2043,96]{0,1:T(8,128)}, ...) | async-done | bytes 12002704 | tf_op jit(solution)/shard_map/psum | solution.py:356
  2053.8 16.8 psum.70
  2088.2 6.6 fusion.160
  2094.8 20.7 fusion.162
  (598 shorter events, 277.5 us)
Async XLA Ops:
  7.2 40.8 %all-gather.13.cloned.1.call-start = ((), (), s32[]{:S(2)}) async-start(), calls=%async_computation.7 | async-start | bytes 3096576 | tf_op jit(solution)/shard_map/all_gather | solution.py:279
  9.3 78.2 %all-gather.11.cloned.1.call-start = ((), (), s32[]{:S(2)}) async-start(), calls=%async_computation.6 | async-start | bytes 3538944 | tf_op jit(solution)/shard_map/all_gather | solution.py:278
  11.3 130.6 %all-gather.21.cloned.1.call-start = ((), (), s32[]{:S(2)}) async-start(), calls=%async_computation.13 | async-start | bytes 5529600 | tf_op jit(solution)/shard_map/all_gather | solution.py:307
  12.6 183.5 %all-gather.17.cloned.1.call-start = ((), (), s32[]{:S(2)}) async-start(), calls=%async_computation.11 | async-start | bytes 5529600 | tf_op jit(solution)/shard_map/all_gather | solution.py:307
  13.2 332.8 %all-gather.15.cloned.1.call-start = ((), (), s32[]{:S(2)}) async-start(), calls=%async_computation.10 | async-start | bytes 18579456 | tf_op jit(solution)/shard_map/all_gather | solution.py:304
  19.3 476.0 %all-gather.19.cloned.1.call-start = ((), (), s32[]{:S(2)}) async-start(), calls=%async_computation.12 | async-start | bytes 18579456 | tf_op jit(solution)/shard_map/all_gather | solution.py:304
  19.9 1058.7 %reduce-scatter.25.cloned.1.call-start = ((), (), s32[]{:S(2)}) async-start(), calls=%async_computation.17 | async-start | bytes 6193152
  24.6 71.9 %copy-start.161 = (bf16[4,128]{1,0:T(4,128)(2,1)}, bf16[4,128]{1,0:T(4,128)(2,1)S(1)}, u32[]{:S(2)}) copy-start(bf16[4,128]{1,0:T(4,128)(2,1)S(1)} %get-tuple-element.268) | copy-start | bytes 3076
  24.6 71.9 %copy-start.163 = (bf16[4,128]{1,0:T(4,128)(2,1)}, bf16[4,128]{1,0:T(4,128)(2,1)S(1)}, u32[]{:S(2)}) copy-start(bf16[4,128]{1,0:T(4,128)(2,1)S(1)} %get-tuple-element.269) | copy-start | bytes 3076
  24.8 68.3 %copy-start.67 = (bf16[4,16,256]{2,1,0:T(8,128)(2,1)}, bf16[4,16,256]{2,1,0:T(8,128)(2,1)S(1)}, u32[]{:S(2)}) copy-start(bf16[4,16,256]{2,1,0:T(8,128)(2,1)S(1)} %add_convert_fusion.7) | copy-start | bytes 98308
  93.0 437.5 %copy-start.99 = (f32[768]{0:T(1024)}, f32[768]{0:T(1024)S(1)}, u32[]{:S(2)}) copy-start(f32[768]{0:T(1024)S(1)} %get-tuple-element.178) | copy-start | bytes 9220
  95.1 435.4 %copy-start.12 = (f32[4,256,768]{2,1,0:T(8,128)}, f32[4,256,768]{2,1,0:T(8,128)S(1)}, u32[]{:S(2)}) copy-start(f32[4,256,768]{2,1,0:T(8,128)S(1)} %get-tuple-element.271) | copy-start | bytes 9437188
  98.4 396.9 %copy-start.64 = (f32[4,768]{1,0:T(4,128)}, f32[4,768]{1,0:T(4,128)S(1)}, u32[]{:S(2)}) copy-start(f32[4,768]{1,0:T(4,128)S(1)} %fusion.82) | copy-start | bytes 36868
  346.0 149.3 %copy-start.96 = (f32[4608]{0:T(1024)S(1)}, f32[4608]{0:T(1024)}, u32[]{:S(2)}) copy-start(f32[4608]{0:T(1024)} %add.579) | copy-start | bytes 55300
  350.1 149.4 %copy-start.113 = (f32[4,768]{1,0:T(4,128)}, f32[4,768]{1,0:T(4,128)S(1)}, u32[]{:S(2)}) copy-start(f32[4,768]{1,0:T(4,128)S(1)} %get-tuple-element.256) | copy-start | bytes 36868
  350.1 149.4 %copy-start.154 = (f32[4,768]{1,0:T(4,128)}, f32[4,768]{1,0:T(4,128)S(1)}, u32[]{:S(2)}) copy-start(f32[4,768]{1,0:T(4,128)S(1)} %get-tuple-element.255) | copy-start | bytes 36868
  350.1 180.5 %copy-start.121 = (f32[4,768]{1,0:T(4,128)}, f32[4,768]{1,0:T(4,128)S(1)}, u32[]{:S(2)}) copy-start(f32[4,768]{1,0:T(4,128)S(1)} %get-tuple-element.257) | copy-start | bytes 36868
  350.1 186.5 %copy-start.56 = (f32[4,768]{1,0:T(4,128)}, f32[4,768]{1,0:T(4,128)S(1)}, u32[]{:S(2)}) copy-start(f32[4,768]{1,0:T(4,128)S(1)} %get-tuple-element.254) | copy-start | bytes 36868
  350.1 186.5 %copy-start.62 = (f32[4,768]{1,0:T(4,128)}, f32[4,768]{1,0:T(4,128)S(1)}, u32[]{:S(2)}) copy-start(f32[4,768]{1,0:T(4,128)S(1)} %get-tuple-element.253) | copy-start | bytes 36868
  350.1 198.5 %copy-start.115 = (f32[4,768]{1,0:T(4,128)}, f32[4,768]{1,0:T(4,128)S(1)}, u32[]{:S(2)}) copy-start(f32[4,768]{1,0:T(4,128)S(1)} %get-tuple-element.252) | copy-start | bytes 36868
  499.4 62.2 %copy-start.87 = (f32[4,768]{1,0:T(4,128)}, f32[4,768]{1,0:T(4,128)S(1)}, u32[]{:S(2)}) copy-start(f32[4,768]{1,0:T(4,128)S(1)} %get-tuple-element.250) | copy-start | bytes 36868
  499.5 62.2 %copy-start.152 = (f32[4,768]{1,0:T(4,128)}, f32[4,768]{1,0:T(4,128)S(1)}, u32[]{:S(2)}) copy-start(f32[4,768]{1,0:T(4,128)S(1)} %get-tuple-element.249) | copy-start | bytes 36868
  499.5 96.0 %copy-start.60 = (f32[4,768]{1,0:T(4,128)}, f32[4,768]{1,0:T(4,128)S(1)}, u32[]{:S(2)}) copy-start(f32[4,768]{1,0:T(4,128)S(1)} %get-tuple-element.247) | copy-start | bytes 36868
  499.5 158.9 %copy-start.54 = (f32[4,768]{1,0:T(4,128)}, f32[4,768]{1,0:T(4,128)S(1)}, u32[]{:S(2)}) copy-start(f32[4,768]{1,0:T(4,128)S(1)} %get-tuple-element.248) | copy-start | bytes 36868
  499.5 158.9 %copy-start.117 = (f32[4,768]{1,0:T(4,128)}, f32[4,768]{1,0:T(4,128)S(1)}, u32[]{:S(2)}) copy-start(f32[4,768]{1,0:T(4,128)S(1)} %get-tuple-element.246) | copy-start | bytes 36868
  499.5 162.5 %copy-start.85 = (f32[4,768]{1,0:T(4,128)}, f32[4,768]{1,0:T(4,128)S(1)}, u32[]{:S(2)}) copy-start(f32[4,768]{1,0:T(4,128)S(1)} %get-tuple-element.251) | copy-start | bytes 36868
  536.0 12.6 copy-start.8
  561.2 168.1 %copy-start.10 = (f32[4,256,768]{2,1,0:T(8,128)}, f32[4,256,768]{2,1,0:T(8,128)S(1)}, u32[]{:S(2)}) copy-start(f32[4,256,768]{2,1,0:T(8,128)S(1)} %get-tuple-element.232) | copy-start | bytes 9437188
  594.9 63.5 %copy-start.2 = (f32[4,256,768]{2,1,0:T(8,128)}, f32[4,256,768]{2,1,0:T(8,128)S(1)}, u32[]{:S(2)}) copy-start(f32[4,256,768]{2,1,0:T(8,128)S(1)} %get-tuple-element.230) | copy-start | bytes 9437188
  594.9 63.5 %copy-start.73 = (f32[4,256]{1,0:T(4,128)}, f32[4,256]{1,0:T(4,128)S(1)}, u32[]{:S(2)}) copy-start(f32[4,256]{1,0:T(4,128)S(1)} %broadcast_multiply_fusion.1) | copy-start | bytes 12292
  595.4 63.0 %copy-start.79 = (f32[4,256]{1,0:T(4,128)}, f32[4,256]{1,0:T(4,128)S(1)}, u32[]{:S(2)}) copy-start(f32[4,256]{1,0:T(4,128)S(1)} %fusion.127) | copy-start | bytes 12292
  628.6 29.8 %copy-start.22 = (f32[4,256,768]{2,1,0:T(8,128)}, f32[4,256,768]{2,1,0:T(8,128)S(1)}, u32[]{:S(2)}) copy-start(f32[4,256,768]{2,1,0:T(8,128)S(1)} %get-tuple-element.226) | copy-start | bytes 9437188
  628.6 29.8 %copy-start.150 = (f32[4,256]{1,0:T(4,128)}, f32[4,256]{1,0:T(4,128)S(1)}, u32[]{:S(2)}) copy-start(f32[4,256]{1,0:T(4,128)S(1)} %negate_multiply_fusion.4) | copy-start | bytes 12292
  670.3 18.4 slice-start
  670.3 18.4 slice-start.1
  714.9 366.0 %reduce-scatter.23.cloned.1.call-start = ((), (), s32[]{:S(2)}) async-start(), calls=%async_computation.16 | async-start | bytes 7077888
  732.3 27.3 %copy-start.31 = (f32[4,256,768]{2,1,0:T(8,128)}, f32[4,256,768]{2,1,0:T(8,128)S(1)}, u32[]{:S(2)}) copy-start(f32[4,256,768]{2,1,0:T(8,128)S(1)} %get-tuple-element.222) | copy-start | bytes 9437188
  732.4 15.5 copy-start.9
  732.4 15.5 copy-start.57
  732.4 15.5 copy-start.70
  872.4 208.4 %reduce-scatter.21.cloned.1.call-start = ((), (), s32[]{:S(2)}) async-start(), calls=%async_computation.15 | async-start | bytes 11059200
  923.4 225.5 %reduce-scatter.19.cloned.1.call-start = ((), (), s32[]{:S(2)}) async-start(), calls=%async_computation.14 | async-start | bytes 11059200
  973.6 496.7 %reduce-scatter.15.cloned.1.call-start = ((), (), s32[]{:S(2)}) async-start(), calls=%async_computation.8 | async-start | bytes 37158912 | tf_op jit(solution)/shard_map/reduce_scatter | solution.py:353
  979.3 16.1 slice-start.7
  1026.2 765.5 %reduce-scatter.17.cloned.1.call-start = ((), (), s32[]{:S(2)}) async-start(), calls=%async_computation.9 | async-start | bytes 37158912 | tf_op jit(solution)/shard_map/reduce_scatter | solution.py:353
  1032.4 16.0 slice-start.5
  1078.6 956.6 %all-reduce.5.cloned.1.call-start = ((), (), s32[]{:S(2)}) async-start(), calls=%async_computation.18 | async-start | bytes 24592384 | tf_op jit(solution)/shard_map/psum | solution.py:356
  2047.9 24.2 %copy-start.39 = (f32[769,192]{1,0:T(8,128)S(1)}, f32[769,192]{1,0:T(8,128)}, u32[]{:S(2)}) copy-start(f32[769,192]{1,0:T(8,128)} %get-tuple-element.200) | copy-start | bytes 1771780
  (149 other events, 780.6 us)
Sparse Core Ops, SparseCore 0:
  10.3 37.6 all-gather.12
  50.2 37.2 all-gather.10
  89.7 52.1 all-gather.20
  144.0 52.1 all-gather.16
  198.2 147.7 all-gather.14
  348.1 147.1 all-gather.18
  715.0 60.6 reduce-scatter.24
  872.6 68.4 reduce-scatter.22
  943.4 101.5 reduce-scatter.20
  1047.3 101.5 reduce-scatter.18
  1151.3 318.9 reduce-scatter.14
  1472.7 318.9 reduce-scatter.16
  1796.9 238.2 all-reduce.4
where the time goes:
time: 2130 us; the launch traced here: 2120 us
  waiting for transfers between devices  1340 us (63%)
  matrix products  338 us (16%)
  local copies, waits for them, and re-layouts  211 us (10%)
  other arithmetic  156 us (7%)
  blocking collectives  56.1 us (3%)
  between operations  22.4 us (1%)
    reduce_scatter x2, waiting for transfers between devices, per_device(): lax.psum_scatter(inner_grad, 'shard', scatter_dimension=0, tiled=True)  643 us
    dot_general x55, matrix products, contract(): return jnp.einsum(pattern, left, right, preferred_element_type=jnp.float32)  335 us
    all_gather x2, waiting for transfers between devices, per_device(): lax.all_gather(inner_weights[layer_idx].astype(jnp.bfloat16), 'shard', ax...  275 us
    psum x1, waiting for transfers between devices, per_device(): inner_part, outer_part = lax.psum((inner_part, outer_part), 'rep')  196 us
    all_gather x2, waiting for transfers between devices, per_device(): lax.all_gather(outer_weights[layer_idx].astype(jnp.bfloat16), 'shard', ax...  93.6 us
    unnamed x393, local copies, waits for them, and re-layouts  71.4 us
    unnamed x17, waiting for transfers between devices  69.3 us
    concatenate x2, local copies, waits for them, and re-layouts, layer_backward(): jnp.concatenate([second_grad, query_bias[None], value_bias[None], proj_bi...  50.6 us
  transfers between devices with their start and end apart: 13, of which 10 were waited for; matrix products, arithmetic and copies ran while one was open for 20% of the time, Pallas kernels for 0%

commit v1 on v0

v1 whole, which is shorter than its diff:
```python
from jax.sharding import PartitionSpec as P
import functools, math
import jax, jax.numpy as jnp
from jax import lax
from jax.experimental import pallas as pl
from jax.experimental.pallas import tpu as pltpu
D=768; HEADS=12; HDIM=64; FF=3072; TOK=256
norm_eps=1e-6
bf=jnp.bfloat16; f32=jnp.float32
VLIM=60*1024*1024
def mm(a,b): return lax.dot_general(a,b,(((1,),(0,)),((),())),preferred_element_type=f32)
def mm_nt(a,b): return lax.dot_general(a,b,(((1,),(1,)),((),())),preferred_element_type=f32)
def mm_tn(a,b): return lax.dot_general(a,b,(((0,),(0,)),((),())),preferred_element_type=f32)
def ln_parts(x):
    c=x-jnp.mean(x,axis=-1,keepdims=True)
    r=lax.rsqrt(jnp.mean(c*c,axis=-1,keepdims=True)+norm_eps)
    return c*r, r
def ln_back(dy, xhat, r, sc):
    dxh=dy*(1.0+sc)
    m1=jnp.mean(dxh,axis=-1,keepdims=True); m2=jnp.mean(dxh*xhat,axis=-1,keepdims=True)
    return r*(dxh-m1-xhat*m2)
def half_masks():
    lane=lax.broadcasted_iota(jnp.int32,(1,128),1)
    lo=(lane<HDIM)
    return lo
C0=math.sqrt(2.0/math.pi); C1=0.044715

def fwd_kernel(x_ref, mod_ref, bias_ref, wa_ref, w1_ref, w2_ref,
               normed_ref, qkv_ref, lse_ref, mixed_ref, attn_ref, mid_ref, ntwo_ref, upper_ref, activ_ref, down_ref, out_ref):
    x=x_ref[...]
    mod=lambda j: mod_ref[0, j:j+1, :]
    bias=lambda j: bias_ref[j:j+1, :]
    xh,_=ln_parts(x)
    normed=(xh*(1.0+mod(1))+mod(0)).astype(bf)
    normed_ref[...]=normed
    qkv_ref[:, :D]=(mm(normed, wa_ref[0])+bias(0)).astype(bf)
    qkv_ref[:, D:2*D]=mm(normed, wa_ref[1]).astype(bf)
    qkv_ref[:, 2*D:]=(mm(normed, wa_ref[2])+bias(1)).astype(bf)
    lo=half_masks()
    for hp in range(HEADS//2):
        c=hp*128
        q=qkv_ref[:, c:c+128]; k=qkv_ref[:, D+c:D+c+128]; v=qkv_ref[:, 2*D+c:2*D+c+128]
        outs=[]
        for h in range(2):
            keep=lo if h==0 else jnp.logical_not(lo)
            qm=jnp.where(keep, q, jnp.zeros_like(q))
            s=mm_nt(qm,k)*(HDIM**-0.5)
            m=jnp.max(s,axis=-1,keepdims=True)
            e=jnp.exp(s-m)
            l=jnp.sum(e,axis=-1,keepdims=True)
            p=(e*(1.0/l)).astype(bf)
            lse_ref[:, 2*hp+h:2*hp+h+1]=m+jnp.log(l)
            outs.append(mm(p,v))
        mixed_ref[:, c:c+128]=jnp.where(lo, outs[0], outs[1]).astype(bf)
    attn=mm(mixed_ref[...], wa_ref[3])+bias(2)
    attn_ref[...]=attn
    mid=x+mod(2)*attn
    mid_ref[...]=mid
    xh2,_=ln_parts(mid)
    ntwo=(xh2*(1.0+mod(4))+mod(3)).astype(bf)
    ntwo_ref[...]=ntwo
    down=jnp.broadcast_to(bias(13),(TOK,D))
    for j in range(4):
        up=mm(ntwo, w1_ref[j])+bias(3+j)
        upper_ref[:, j*D:(j+1)*D]=up
        t=jnp.tanh(C0*(up+C1*(up*up*up)))
        act=(0.5*up*(1.0+t)).astype(bf)
        activ_ref[:, j*D:(j+1)*D]=act
        down=down+mm_nt(act, w2_ref[j])
    down_ref[...]=down
    out_ref[...]=mid_ref[...]+mod(5)*down

def full(shape):
    n=len(shape)
    return pl.BlockSpec(shape, lambda i: (0,)*n, pipeline_mode=pl.Buffered(1))
def rows(width): return pl.BlockSpec((TOK,width), lambda i:(i,0))
def layer_fwd(x, mod, bias, wa, w1, w2):
    T=x.shape[0]; n=T//TOK
    sd=jax.ShapeDtypeStruct
    widths=[(D,bf),(3*D,bf),(128,f32),(D,bf),(D,f32),(D,f32),(D,bf),(FF,f32),(FF,bf),(D,f32),(D,f32)]
    return pl.pallas_call(fwd_kernel, grid=(n,),
        in_specs=[rows(D), pl.BlockSpec((1,8,D),lambda i:(i,0,0)), full((16,D)), full((4,D,D)), full((4,D,D)), full((4,D,D))],
        out_specs=[rows(w) for w,_ in widths],
        out_shape=[sd((T,w),t) for w,t in widths],
        compiler_params=pltpu.CompilerParams(vmem_limit_bytes=VLIM),
        cost_estimate=pl.CostEstimate(flops=2*T*(9216*D+2*TOK*D), bytes_accessed=60_000_000, transcendentals=T*FF*2),
    )(x,mod,bias,wa,w1,w2)

def bwd_mlp_kernel(g_ref, mod_ref, wa3_ref, w1_ref, w2_ref, down_ref, upper_ref, mid_ref, attn_ref,
                   dlow_ref, ulow_ref, gmid_ref, alow_ref, gmix_ref, dmod_ref, db_ref):
    i=pl.program_id(0)
    mod=lambda j: mod_ref[0, j:j+1, :]
    g=g_ref[...]
    gd=g*mod(5)
    dl=gd.astype(bf)
    dlow_ref[...]=dl
    @pl.when(i==0)
    def _(): db_ref[...]=jnp.zeros_like(db_ref)
    s0=lambda v: jnp.sum(v,axis=0,keepdims=True)
    dmod_ref[0,5:6,:]=s0(g*down_ref[...])
    db_ref[13:14,:]+=s0(gd)
    gn=jnp.zeros((TOK,D),f32)
    for j in range(4):
        ga=mm(dl, w2_ref[j])
        up=upper_ref[:, j*D:(j+1)*D]
        u2=up*up
        t=jnp.tanh(C0*(up+C1*(u2*up)))
        gu=ga*(0.5*(1.0+t)+(0.5*C0)*up*(1.0-t*t)*(1.0+(3.0*C1)*u2))
        db_ref[3+j:4+j,:]+=s0(gu)
        ul=gu.astype(bf)
        ulow_ref[:, j*D:(j+1)*D]=ul
        gn=gn+mm_nt(ul, w1_ref[j])
    xh,r=ln_parts(mid_ref[...])
    dmod_ref[0,3:4,:]=s0(gn)
    dmod_ref[0,4:5,:]=s0(gn*xh)
    gm=g_ref[...]+ln_back(gn,xh,r,mod(4))
    gmid_ref[...]=gm
    ga=gm*mod(2)
    dmod_ref[0,2:3,:]=s0(gm*attn_ref[...])
    db_ref[2:3,:]+=s0(ga)
    al=ga.astype(bf)
    alow_ref[...]=al
    gmix_ref[...]=mm_nt(al, wa3_ref[0]).astype(bf)
def layer_bwd_mlp(g, mod, wa, w1, w2, down, upper, mid, attn):
    T=g.shape[0]; n=T//TOK
    sd=jax.ShapeDtypeStruct
    m3=pl.BlockSpec((1,8,D),lambda i:(i,0,0))
    return pl.pallas_call(bwd_mlp_kernel, grid=(n,),
        in_specs=[rows(D), m3, pl.BlockSpec((1,D,D),lambda i:(3,0,0),pipeline_mode=pl.Buffered(1)), full((4,D,D)), full((4,D,D)), rows(D), rows(FF), rows(D), rows(D)],
        out_specs=[rows(D),rows(FF),rows(D),rows(D),rows(D),m3,pl.BlockSpec((16,D),lambda i:(0,0))],
        out_shape=[sd((T,D),bf),sd((T,FF),bf),sd((T,D),f32),sd((T,D),bf),sd((T,D),bf),sd((n,8,D),f32),sd((16,D),f32)],
        compiler_params=pltpu.CompilerParams(vmem_limit_bytes=VLIM),
        cost_estimate=pl.CostEstimate(flops=2*T*D*(2*FF+D), bytes_accessed=50_000_000, transcendentals=T*FF),
    )(g,mod,wa,w1,w2,down,upper,mid,attn)

def bwd_attn_kernel(gmix_ref, gmid_ref, mod_ref, wa_ref, qkv_ref, lse_ref, x_ref,
                    low_ref, gin_ref, dmod_ref, db_ref):
    i=pl.program_id(0)
    mod=lambda j: mod_ref[0, j:j+1, :]
    @pl.when(i==0)
    def _(): db_ref[...]=jnp.zeros_like(db_ref)
    s0=lambda v: jnp.sum(v,axis=0,keepdims=True)
    lo=half_masks()
    zero=jnp.zeros((TOK,128),bf)
    for hp in range(HEADS//2):
        c=hp*128
        q=qkv_ref[:, c:c+128]; k=qkv_ref[:, D+c:D+c+128]; v=qkv_ref[:, 2*D+c:2*D+c+128]
        gm=gmix_ref[:, c:c+128]
        res=[]
        for h in range(2):
            keep=lo if h==0 else jnp.logical_not(lo)
            qm=jnp.where(keep,q,zero); gmm=jnp.where(keep,gm,zero)
            s=mm_nt(qm,k)*(HDIM**-0.5)
            p=jnp.exp(s-lse_ref[:, 2*hp+h:2*hp+h+1])
            dp=mm_nt(gmm,v)
            ds=p*(dp-jnp.sum(p*dp,axis=-1,keepdims=True))
            dsl=ds.astype(bf)
            res.append((mm(dsl,k), mm_tn(dsl,q), mm_tn(p.astype(bf),gm)))
        for j in range(3):
            o=jnp.where(lo,res[0][j],res[1][j])
            if j<2: o=o*(HDIM**-0.5)
            ol=o.astype(bf)
            low_ref[:, j*D+c:j*D+c+128]=ol
            if j!=1:
                row=0 if j==0 else 1
                db_ref[row:row+1, c:c+128]+=s0(ol.astype(f32))
    gn=mm_nt(low_ref[:, :D], wa_ref[0])+mm_nt(low_ref[:, D:2*D], wa_ref[1])+mm_nt(low_ref[:, 2*D:], wa_ref[2])
    xh,r=ln_parts(x_ref[...])
    dmod_ref[...]=jnp.zeros_like(dmod_ref)
    dmod_ref[0,0:1,:]=s0(gn)
    dmod_ref[0,1:2,:]=s0(gn*xh)
    gin_ref[...]=gmid_ref[...]+ln_back(gn,xh,r,mod(1))
def layer_bwd_attn(gmix, gmid, mod, wa, qkv, lse, x):
    T=gmix.shape[0]; n=T//TOK
    sd=jax.ShapeDtypeStruct
    m3=pl.BlockSpec((1,8,D),lambda i:(i,0,0))
    return pl.pallas_call(bwd_attn_kernel, grid=(n,),
        in_specs=[rows(D),rows(D),m3,full((3,D,D)),rows(3*D),rows(128),rows(D)],
        out_specs=[rows(3*D),rows(D),m3,pl.BlockSpec((8,D),lambda i:(0,0))],
        out_shape=[sd((T,3*D),bf),sd((T,D),f32),sd((n,8,D),f32),sd((8,D),f32)],
        compiler_params=pltpu.CompilerParams(vmem_limit_bytes=VLIM),
        cost_estimate=pl.CostEstimate(flops=2*T*D*(3*D+5*TOK), bytes_accessed=25_000_000, transcendentals=T*TOK*HEADS),
    )(gmix,gmid,mod,wa,qkv,lse,x)

def dw_kernel(x_ref, dy_ref, o_ref, xt_ref):
    @pl.when(pl.program_id(0)==0)
    def _(): xt_ref[...]=x_ref[...].T
    o_ref[...]=mm(xt_ref[...], dy_ref[...])
def dw(x, dy):
    T=x.shape[0]; C=dy.shape[1]; W=384
    return pl.pallas_call(dw_kernel, grid=(C//W,),
        in_specs=[pl.BlockSpec((T,D),lambda i:(0,0)), pl.BlockSpec((T,W),lambda i:(0,i))],
        out_specs=pl.BlockSpec((D,W),lambda i:(0,i)),
        out_shape=jax.ShapeDtypeStruct((D,C),f32),
        scratch_shapes=[pltpu.VMEM((D,T),bf)],
        compiler_params=pltpu.CompilerParams(vmem_limit_bytes=VLIM),
    )(x,dy)
def gather_kernel(R, nz, U, w_ref, out_ref, zs, zr, xs, xr, cs, cr, ls):
    rep=lax.axis_index("rep"); shard=lax.axis_index("shard")
    z=shard//2; c=lax.rem(shard,2)
    dev=lambda r,zz,cc: (r, 2*zz+cc)
    MESH=pl.DeviceIdType.MESH
    bar=pltpu.get_barrier_semaphore()
    peers=[dev(rep, lax.rem(z+k,nz), c) for k in range(1,nz)]+[dev(jnp.bitwise_xor(rep,j), z, c) for j in range(1,R)]+[dev(rep,z,1-c)]
    for p in peers: pl.semaphore_signal(bar, inc=1, device_id=p, device_id_type=MESH)
    pl.semaphore_wait(bar, len(peers))
    def zcopy(u,k):
        return pltpu.make_async_remote_copy(src_ref=w_ref.at[u,rep], dst_ref=out_ref.at[u,rep,z,c], send_sem=zs.at[u,k-1], recv_sem=zr.at[u,k-1],
            device_id=dev(rep,lax.rem(z+k,nz),c), device_id_type=MESH)
    def xcopy(u,j,k):
        o=lax.rem(z-k+nz,nz)
        return pltpu.make_async_remote_copy(src_ref=out_ref.at[u,rep,o,c], dst_ref=out_ref.at[u,rep,o,c], send_sem=xs.at[u,j-1,k-1], recv_sem=xr.at[u,j-1,k-1],
            device_id=dev(jnp.bitwise_xor(rep,j),z,c), device_id_type=MESH)
    def ccopy(u,j):
        r=jnp.bitwise_xor(rep,j)
        return pltpu.make_async_remote_copy(src_ref=out_ref.at[u,r,:,c], dst_ref=out_ref.at[u,r,:,c], send_sem=cs.at[u,j], recv_sem=cr.at[u,j],
            device_id=dev(rep,z,1-c), device_id_type=MESH)
    locs=[pltpu.make_async_copy(w_ref.at[u], out_ref.at[u,:,z,c], ls.at[u]) for u in range(U)]
    for u in range(U):
        for k in range(1,nz): zcopy(u,k).start()
    for u in range(U): locs[u].start()
    for u in range(U):
        for k in range(1,nz):
            zcopy(u,k).wait_recv()
            for j in range(1,R): xcopy(u,j,k).start()
        locs[u].wait()
        ccopy(u,0).start()
    for u in range(U):
        for j in range(1,R):
            for k in range(1,nz): xcopy(u,j,k).wait_recv()
            ccopy(u,j).start()
    for u in range(U):
        for j in range(R): ccopy(u,j).wait()
        for k in range(1,nz): zcopy(u,k).wait_send()
        for j in range(1,R):
            for k in range(1,nz): xcopy(u,j,k).wait_send()

def gather_layer(w, R, S, cid):
    U,_,rows_,W=w.shape
    nz=S//2
    dma=pltpu.SemaphoreType.DMA
    any_=pl.BlockSpec(memory_space=pl.ANY)
    out=pl.pallas_call(functools.partial(gather_kernel,R,nz,U),
        in_specs=[any_], out_specs=any_, out_shape=jax.ShapeDtypeStruct((U,R,nz,2,rows_,W),bf),
        scratch_shapes=[dma((U,nz-1)),dma((U,nz-1)),dma((U,R-1,nz-1)),dma((U,R-1,nz-1)),dma((U,R)),dma((U,R)),dma((U,))],
        compiler_params=pltpu.CompilerParams(collective_id=cid, has_side_effects=True, vmem_limit_bytes=4*1024*1024),
    )(w)
    out=out.reshape(U,R,D,W)
    if R==4: return [out[u] for u in range(U)]
    m=R//4
    return [out[u].reshape(4,m,D,W).transpose(0,2,1,3).reshape(4,D,D) for u in range(U)]
P_SIZE=16; GRID=16; LAYERS=2; LAT_DEV=4; FREQ=256; NCLASS=1000
clip_coef=2.5; beta_one=0.9; beta_two=0.999; adam_eps=1e-8; learn_rate=0.01; weight_decay=0.01; step_count=10.0
BIAS=14
def position_table(grid_side, feature_width):
    quarter=feature_width//4
    omega=jnp.exp(-math.log(10000.0)*jnp.arange(quarter,dtype=f32)/quarter)
    ids=jnp.arange(grid_side*grid_side,dtype=jnp.int32)
    a=(ids%grid_side).astype(f32)[:,None]*omega[None,:]
    d=(ids//grid_side).astype(f32)[:,None]*omega[None,:]
    return jnp.concatenate([jnp.sin(a),jnp.cos(a),jnp.sin(d),jnp.cos(d)],axis=1)
def time_features(steps, count):
    half=count//2
    freq=jnp.exp(-math.log(10000.0)*jnp.arange(half,dtype=f32)/half)
    ang=steps.astype(f32)[:,None]*freq[None,:]
    return jnp.concatenate([jnp.cos(ang),jnp.sin(ang)],axis=1)
def modulate(x, sh, sc):
    c=x-jnp.mean(x,axis=-1,keepdims=True)
    v=jnp.mean(c*c,axis=-1,keepdims=True)
    return c*lax.rsqrt(v+norm_eps)*(1.0+sc[:,None,:])+sh[:,None,:]
def adam_update(w,g,m,v,factor):
    s=g*factor
    m2=beta_one*m+(1.0-beta_one)*s
    v2=beta_two*v+(1.0-beta_two)*s*s
    mh=m2/(1.0-beta_one**step_count)
    vh=v2/(1.0-beta_two**step_count)
    w2=w-learn_rate*(mh/(jnp.sqrt(vh)+adam_eps)+weight_decay*w)
    return (w2,m2,v2,w2.astype(bf))
def dot32(pattern,a,b): return jnp.einsum(pattern,a,b,preferred_element_type=f32)
def silu_back(v,g): return jax.vjp(jax.nn.silu,v)[1](g)[0]
ALL=("rep","shard")

def per_device(latents,target_noise,labels,time_steps,inner_weights,outer_weights,embed_table,final_mod,head_weights,
               inner_moment,inner_square,outer_moment,outer_square,embed_moment,embed_square,final_moment,final_square,head_moment,head_square):
    R=lax.axis_size("rep"); S=lax.axis_size("shard")
    rep=lax.axis_index("rep"); shard=lax.axis_index("shard")
    own=D//S; W=4*D//R; N=LAT_DEV*R*S; G=LAT_DEV*S
    count=N*TOK*P_SIZE
    inner_low=inner_weights.astype(bf); outer_low=outer_weights.astype(bf)
    gathered=[]
    for l in range(LAYERS):
        slab=jnp.stack([inner_low[l,:,:4*D],inner_low[l,:,4*D:8*D],outer_low[l,:FF].T])
        slab=slab.reshape(3,own,R,W).transpose(0,2,1,3)
        gathered.append(gather_layer(slab,R,S,l))
    embed_low=embed_table.astype(bf); final_low=final_mod.astype(bf); head_low=head_weights.astype(bf)
    small=jnp.concatenate([outer_low[:,FF:].reshape(LAYERS*BIAS,own),embed_low[:P_SIZE+1]],axis=0)
    small=lax.all_gather(small,"shard",axis=1,tiled=True)
    biases=small[:LAYERS*BIAS].reshape(LAYERS,BIAS,D).astype(f32)
    patch_w=small[LAYERS*BIAS:LAYERS*BIAS+P_SIZE]; patch_b=small[LAYERS*BIAS+P_SIZE].astype(f32)
    ids=lax.all_gather(jnp.stack([time_steps,labels],axis=1),ALL,axis=0,tiled=True)
    steps_all=ids[:,0]; labels_all=ids[:,1]
    r1=P_SIZE+1; r2=P_SIZE+2+FREQ; r3=P_SIZE+3+FREQ+D
    features=time_features(steps_all,FREQ).astype(bf)
    hidden=dot32("nf,fd->nd",features,embed_low[r1:r1+FREQ])+embed_low[r1+FREQ].astype(f32)
    act_own=jax.nn.silu(hidden).astype(bf)
    time_act=lax.all_gather(act_own,"shard",axis=1,tiled=True)
    hot=labels_all[:,None]==jnp.arange(NCLASS,dtype=jnp.int32)[None,:]
    condition=dot32("nd,de->ne",time_act,embed_low[r2:r2+D])+embed_low[r2+D].astype(f32)+dot32("nc,ce->ne",hot.astype(bf),embed_low[r3:])
    cond_own=jax.nn.silu(condition).astype(bf)
    cond_all=lax.all_gather(cond_own,"shard",axis=1,tiled=True)
    cond_group=lax.dynamic_slice_in_dim(cond_own,rep*G,G,0)
    ada_own=inner_low[:,:,4*D+FF:]
    part=dot32("gd,lde->gle",cond_group,ada_own)
    modul=lax.psum_scatter(part,"shard",scatter_dimension=0,tiled=True)
    modul=modul.reshape(LAT_DEV,LAYERS,6,D)+biases[:,7:13].reshape(1,LAYERS,6,D)
    modul=jnp.pad(modul.transpose(1,0,2,3),((0,0),(0,0),(0,2),(0,0)))
    fin_cols=2*D//S
    fin_part=dot32("gd,de->ge",lax.dynamic_slice_in_dim(cond_all,rep*G,G,0),final_low[:D])+final_low[D].astype(f32)
    fin_mod=lax.all_to_all(fin_part.reshape(S,LAT_DEV,fin_cols),"shard",0,0,tiled=True)
    fin_mod=fin_mod.reshape(S,LAT_DEV,fin_cols).transpose(1,0,2).reshape(LAT_DEV,2*D)
    ramp=0.0001+(0.02-0.0001)*jnp.arange(1000,dtype=f32)/999.0
    upto=jnp.arange(1000,dtype=jnp.int32)[None,:]<=time_steps[:,None]
    abar=jnp.exp(jnp.sum(jnp.where(upto,jnp.log(1.0-ramp)[None,:],0.0),axis=1))
    patches=(jnp.sqrt(abar)[:,None,None]*latents+jnp.sqrt(1.0-abar)[:,None,None]*target_noise).astype(bf)
    stream=dot32("gpt,pd->gtd",patches,patch_w)+patch_b+position_table(GRID,D)[None]
    stream=stream.reshape(LAT_DEV*TOK,D)
    saved=[]
    for l in range(LAYERS):
        wa,w1,w2=gathered[l]
        bias=jnp.pad(biases[l],((0,2),(0,0)))
        o=layer_fwd(stream,modul[l],bias,wa,w1,w2)
        saved.append((stream,)+tuple(o))
        stream=o[-1]
    stream3=stream.reshape(LAT_DEV,TOK,D)
    fin_shift,fin_scale=jnp.split(fin_mod,2,axis=1)
    fin_normed=modulate(stream3,fin_shift,fin_scale).astype(bf)
    output=dot32("gtd,dp->gtp",fin_normed,head_low[:D])+head_low[D].astype(f32)
    differ=output-jnp.swapaxes(target_noise,1,2)
    loss_part=jnp.sum(differ*differ)/count
    grad_output=2.0*(differ*(1.0/count))
    head_bias=jnp.sum(grad_output,axis=(0,1))
    output_low=grad_output.astype(bf)
    head_grad=jnp.concatenate([dot32("gtd,gtp->dp",fin_normed,output_low),head_bias[None]],axis=0)
    grad_fin_normed=dot32("gtp,dp->gtd",output_low,head_low[:D])
    grad_stream,g_shift,g_scale=jax.vjp(modulate,stream3,fin_shift,fin_scale)[1](grad_fin_normed)
    grad_stream=grad_stream.reshape(LAT_DEV*TOK,D)
    grad_fin=jnp.concatenate([g_shift,g_scale],axis=1)
    fin_rows=lax.all_gather(grad_fin.astype(bf),ALL,axis=0,tiled=True)
    fin_mine=lax.dynamic_slice_in_dim(fin_rows,shard*fin_cols,fin_cols,1)
    final_main=dot32("nd,ne->de",cond_all,fin_mine)
    grad_cond=lax.psum_scatter(dot32("ne,de->nd",fin_mine,final_low[:D]),"shard",scatter_dimension=1,tiled=True)
    unit_parts=[None]*LAYERS; ada_parts=[None]*LAYERS; bias_grads=[None]*LAYERS
    for l in range(LAYERS-1,-1,-1):
        wa,w1,w2=gathered[l]
        x,normed,qkv,lse,mixed,attn,mid,ntwo,upper,activ,down,_=saved[l]
        dlow,ulow,gmid,alow,gmix,dm1,db1=layer_bwd_mlp(grad_stream,modul[l],wa,w1,w2,down,upper,mid,attn)
        low,grad_stream,dm2,db2=layer_bwd_attn(gmix,gmid,modul[l],wa,qkv,lse,x)
        units=[jnp.concatenate([dot32("td,te->de",normed,low),dot32("td,te->de",mixed,alow)],axis=1),dw(ntwo,ulow),dw(dlow,activ)]
        units=[lax.psum_scatter(u.astype(bf),"shard",scatter_dimension=0,tiled=True) for u in units]
        unit_parts[l]=[lax.psum(u.astype(f32),"rep") for u in units]
        dmod=jnp.concatenate([dm2[:,:2],dm1[:,2:6]],axis=1)
        rows_all=lax.all_gather(dmod.astype(bf).reshape(LAT_DEV,6*D),ALL,axis=0,tiled=True)
        ada_parts[l]=dot32("nd,ne->de",cond_own,rows_all)
        grad_cond=grad_cond+dot32("ne,de->nd",rows_all,ada_own[l])
        bias_grads[l]=jnp.concatenate([db2[0:2],db1[2:7],jnp.sum(dmod,axis=0),db1[13:14]],axis=0)
    gs=grad_stream.reshape(LAT_DEV,TOK,D)
    patch_grad=dot32("gpt,gtd->pd",patches,gs.astype(bf))
    patch_bias=jnp.sum(grad_stream,axis=0)
    fin_bias=jnp.sum(grad_fin,axis=0).reshape(2,D)
    tail=jnp.zeros((1,D),f32).at[0,0].set(loss_part)
    head_flat=head_grad.reshape(-1)
    head_rows=-(-head_flat.shape[0]//D)
    head_flat=jnp.pad(head_flat,(0,head_rows*D-head_flat.shape[0])).reshape(head_rows,D)
    sums=lax.psum(jnp.concatenate(bias_grads+[patch_grad,patch_bias[None],fin_bias,head_flat,tail],axis=0),ALL)
    o1=LAYERS*BIAS; o2=o1+P_SIZE+1; o3=o2+2; o4=o3+head_rows
    mean_loss=sums[o4,0]
    head_total=sums[o3:o4].reshape(-1)[:(D+1)*P_SIZE].reshape(D+1,P_SIZE)
    fin_bias_own=lax.dynamic_slice_in_dim(sums[o2:o3].reshape(2*D),shard*fin_cols,fin_cols,0)
    mine=lax.dynamic_slice_in_dim(sums[:o2],shard*own,own,1)
    grad_condition=silu_back(condition,grad_cond)
    b2=jnp.sum(grad_condition,axis=0)
    clow=grad_condition.astype(bf)
    second=dot32("nd,ne->de",time_act,clow)
    class_grad=jnp.einsum("nc,nd->cd",hot.astype(f32),grad_condition,precision=lax.Precision.HIGHEST)
    grad_time_act=lax.psum_scatter(dot32("ne,de->nd",clow,embed_low[r2:r2+D]),"shard",scatter_dimension=1,tiled=True)
    grad_time=silu_back(hidden,grad_time_act)
    first=dot32("nf,nd->fd",features,grad_time.astype(bf))
    embed_grad=jnp.concatenate([mine[o1:o2],first,jnp.sum(grad_time,axis=0)[None],second,b2[None],class_grad],axis=0)
    final_grad=jnp.concatenate([final_main,fin_bias_own[None]],axis=0)
    inner_grad=jnp.stack([jnp.concatenate([unit_parts[l][0],unit_parts[l][1],ada_parts[l]],axis=1) for l in range(LAYERS)])
    outer_grad=jnp.stack([jnp.concatenate([unit_parts[l][2].T,mine[l*BIAS:(l+1)*BIAS]],axis=0) for l in range(LAYERS)])
    sq=lambda a: jnp.sum(a*a)
    square=lax.psum(sq(inner_grad)+sq(outer_grad)+sq(embed_grad)+sq(final_grad),"shard")
    grad_norm=jnp.sqrt(square+sq(head_total))
    factor=jnp.minimum(1.0,clip_coef*math.sqrt(D/count)/grad_norm)
    out=[mean_loss,grad_norm]
    for w,g,m,v in ((inner_weights,inner_grad,inner_moment,inner_square),(outer_weights,outer_grad,outer_moment,outer_square),
                    (embed_table,embed_grad,embed_moment,embed_square),(final_mod,final_grad,final_moment,final_square),
                    (head_weights,head_total,head_moment,head_square)):
        out.extend(adam_update(w,g,m,v,factor))
    return tuple(out)

def solution(mesh):
    lat=P(ALL,None,None); one=P(ALL); inn=P(None,"shard",None); oute=P(None,None,"shard"); col=P(None,"shard")
    in_specs=(lat,lat,one,one,inn,oute,col,col,P(),inn,inn,oute,oute,col,col,col,col,P(),P())
    out_specs=(P(),P())+(inn,)*4+(oute,)*4+(col,)*8+(P(),)*4
    return jax.shard_map(per_device,mesh=mesh,in_specs=in_specs,out_specs=out_specs,check_vma=False)
```

time: 2130 us -> 1420 us (0.67)
  waiting for transfers between devices: 1340 us -> 421 us
  Pallas kernels: 0 us -> 388 us
  matrix products: 338 us -> 47.4 us
  blocking collectives: 56.1 us -> 345 us
  local copies, waits for them, and re-layouts: 211 us -> 77.6 us
  other arithmetic: 156 us -> 103 us
    all_gather x6 -> x2, waiting for transfers between devices: 430 us -> 28.3 us  [per_device(): lax.all_gather(dmod.astype(bf).reshape(LAT_DEV, 6 * D), ALL, axis=0, tile...]
    pallas_call x0 -> x12, Pallas kernels: none -> 388 us  [the longest x2 148 us: gather_layer(): pl.pallas_call(functools.partial(gather_kernel, R, nz, U), in_specs=[any_...]
    dot_general x56 -> x24, matrix products: 338 us -> 47.4 us  [the longest x23 46.2 us: dot32(): return jnp.einsum(pattern, a, b, preferred_element_type=f32)]
    reduce_scatter x2 -> x8, waiting for transfers between devices: 643 us -> 373 us  [the longest x6 328 us: per_device(): lax.psum_scatter(u.astype(bf), 'shard', scatter_dimension=0, tiled=True)]
    psum x1 -> x2, waiting for transfers between devices: 196 us -> 19.8 us  [the longest x1 19.8 us: per_device(): lax.psum(jnp.concatenate(bias_grads + [patch_grad, patch_bias[None], fin_...]
    psum x2, blocking collectives: 56.1 us -> 212 us  [the longest x1 196 us: per_device(): unit_parts[l] = [lax.psum(u.astype(f32), 'rep') for u in units]]
    all_gather x0 -> x5, blocking collectives: none -> 133 us  [the longest x1 46.3 us: per_device(): fin_rows = lax.all_gather(grad_fin.astype(bf), ALL, axis=0, tiled=True)]
    unnamed x17 -> x14, waiting for transfers between devices: 69.3 us -> 0.23 us
  transfers between devices with their start and end apart: 13 -> 14, of which waited for: 10 -> 10; matrix products, arithmetic and copies ran while one was open for 20% -> 11% of each run, Pallas kernels for 0% -> 14%
where the time goes in v1:
time: 1420 us; the launch traced here: 1410 us
  waiting for transfers between devices  421 us (30%)
  Pallas kernels  388 us (27%)
  blocking collectives  345 us (24%)
  other arithmetic  103 us (7%)
  local copies, waits for them, and re-layouts  77.6 us (5%)
  matrix products  47.4 us (3%)
  between operations  22.5 us (2%)
    reduce_scatter x6, waiting for transfers between devices, per_device(): lax.psum_scatter(u.astype(bf), 'shard', scatter_dimension=0, tiled=True)  328 us
    psum x1, blocking collectives, per_device(): unit_parts[l] = [lax.psum(u.astype(f32), 'rep') for u in units]  196 us
    pallas_call x2, Pallas kernels, gather_layer(): pl.pallas_call(functools.partial(gather_kernel, R, nz, U), in_specs=[any_...  148 us
    pallas_call x2, Pallas kernels, layer_fwd(): pl.pallas_call(fwd_kernel, grid=(n,), in_specs=[rows(D), pl.BlockSpec((1,...  71.2 us
    pallas_call x2, Pallas kernels, layer_bwd_attn(): pl.pallas_call(bwd_attn_kernel, grid=(n,), in_specs=[rows(D), rows(D), m3...  63.8 us
    pallas_call x4, Pallas kernels, dw(): pl.pallas_call(dw_kernel, grid=(C // W,), in_specs=[pl.BlockSpec((T, D),...  53 us
    pallas_call x2, Pallas kernels, layer_bwd_mlp(): pl.pallas_call(bwd_mlp_kernel, grid=(n,), in_specs=[rows(D), m3, pl.Block...  51.8 us
    all_gather x1, blocking collectives, per_device(): fin_rows = lax.all_gather(grad_fin.astype(bf), ALL, axis=0, tiled=True)  46.3 us
  transfers between devices with their start and end apart: 14, of which 10 were waited for; matrix products, arithmetic and copies ran while one was open for 11% of the time, Pallas kernels for 14%

profile of v1, /device:TPU:0, one launch (start us, length us, event | category | flops | bytes accessed | tf_op | source)
XLA Modules:
  0.0 1409.7 jit_solution(9243943228210598158)
XLA Ops:
  7.9 43.3 %all-gather.1 = s32[32,4,2]{1,2,0:T(2,128)S(1)} all-gather(s32[1,4,2]{1,2,0:T(2,128)S(1)} %add_bitcast_fusion.1), channel_id=1, replica_groups=mesh['rep'=4,'shard'=8] {'rep','shard'}, dimensions={0}, use_global_device_ids=true | all-gather | bytes 1056 | tf_op jit(solution)/shard_map/all_gather | solution.py:300
  55.2 14.1 all_gather.23
  70.5 14.1 %all_gather.24 = bf16[128,768]{0,1:T(8,128)(2,1)S(1)} all-gather(bf16[128,96]{0,1:T(8,128)(2,1)S(1)} %get-tuple-element.258), channel_id=1, replica_groups=mesh['rep'=4,'shard'=8] {'shard'}, dimensions={1}, use_global_device_ids=true | all-gather | bytes 221184 | tf_op jit(solution)/shard_map/all_gather | solution.py:310
  85.6 4.0 all-to-all-start
  89.6 3.8 convert_element_type.180
  103.1 14.8 %all-gather = bf16[8,96,45]{1,2,0:T(8,128)(2,1)S(1)} all-gather(bf16[1,96,45]{1,2,0:T(8,128)(2,1)S(1)} %maximum_bitcast_fusion.6), channel_id=1, replica_groups=mesh['rep'=4,'shard'=8] {'shard'}, dimensions={0}, use_global_device_ids=true | all-gather | bytes 77760 | tf_op jit(solution)/shard_map/all_gather | solution.py:297
  122.0 72.7 %shard_map.354 = bf16[3,4,4,2,96,768]{5,4,3,2,1,0:T(8,128)(2,1)S(1)} custom-call(bf16[3,4,96,768]{3,2,1,0:T(8,128)(2,1)S(1)} %maximum_bitcast_fusion.2.w_ref), custom_call_target="tpu_custom_call" | custom-call | tf_op jit(solution)/shard_map/pallas_call | solution.py:243
  194.7 5.6 fusion.75
  200.6 75.6 %shard_map.356 = bf16[3,4,4,2,96,768]{5,4,3,2,1,0:T(8,128)(2,1)S(1)} custom-call(bf16[3,4,96,768]{3,2,1,0:T(8,128)(2,1)S(1)} %maximum_bitcast_fusion.3.w_ref), custom_call_target="tpu_custom_call" | custom-call | tf_op jit(solution)/shard_map/pallas_call | solution.py:243
  276.2 5.7 fusion.74
  292.4 35.8 %shard_map.355 = (bf16[1024,768]{1,0:T(8,128)(2,1)}, bf16[1024,2304]{1,0:T(8,128)(2,1)}, f32[1024,128]{1,0:T(8,128)}, bf16[1024,768]{1,0:T(8,128)(2,1)}, f32[102...) custom-call(f32[1024,768]{1,0:T(8,128)} %bitcast.168, ...), custom_call_target="tpu_custom_call" | custom-call | flops 15300820992 | bytes 60000000 | tf_op jit(solution)/shard_map/pallas_call | solution.py:81
  328.2 35.4 %shard_map.357 = (bf16[1024,768]{1,0:T(8,128)(2,1)}, bf16[1024,2304]{1,0:T(8,128)(2,1)}, f32[1024,128]{1,0:T(8,128)}, bf16[1024,768]{1,0:T(8,128)(2,1)}, f32[102...) custom-call(f32[1024,768]{1,0:T(8,128)} %get-tuple-element.78.x_ref,, ...), custom_call_target="tpu_custom_call" | custom-call | flops 15300820992 | bytes 60000000 | tf_op jit(solution)/shard_map/pallas_call | solution.py:81
  375.1 25.9 %shard_map.358 = (bf16[1024,768]{1,0:T(8,128)(2,1)}, bf16[1024,3072]{1,0:T(8,128)(2,1)}, f32[1024,768]{1,0:T(8,128)}, bf16[1024,768]{1,0:T(8,128)(2,1)}, bf16[10...) custom-call(f32[1024,768]{1,0:T(8,128)} %bitcast.167, f32[4,8,768]{2,1,0:T(8,128)} %get-tuple-element.240.mod_ref, ...), custom_call_target="tpu_custom_call" | custom-call | flops 10871635968 | bytes 50000000 | tf_op jit(solution)/shard_map/pallas_call | solution.py:128
  401.0 31.8 %shard_map.359 = (bf16[1024,2304]{1,0:T(8,128)(2,1)}, f32[1024,768]{1,0:T(8,128)}, f32[4,8,768]{2,1,0:T(8,128)}, f32[8,768]{1,0:T(8,128)}) custom-call(bf16[1024,768]{1,0:T(8,128)(2,1)} %get-tuple-element.84.gmix_ref, f32[1024,768]{1,0:T(8,128)} %get-tuple-element.85.gmid_ref, f32[4,8,768]{2,1,0:T(8,128)} %get-tuple-element.240.mod_ref, ...), custom_call_target="tpu_custom_call" | custom-call | flops 5637144576 | bytes 25000000 | tf_op jit(solution)/shard_map/pallas_call | solution.py:177
  432.8 25.9 %shard_map.360 = (bf16[1024,768]{1,0:T(8,128)(2,1)}, bf16[1024,3072]{1,0:T(8,128)(2,1)}, f32[1024,768]{1,0:T(8,128)}, bf16[1024,768]{1,0:T(8,128)(2,1)}, bf16[10...) custom-call(f32[1024,768]{1,0:T(8,128)} %get-tuple-element.88.g_ref, ...), custom_call_target="tpu_custom_call" | custom-call | flops 10871635968 | bytes 50000000 | tf_op jit(solution)/shard_map/pallas_call | solution.py:128
  458.7 32.0 %shard_map.361 = (bf16[1024,2304]{1,0:T(8,128)(2,1)}, f32[1024,768]{1,0:T(8,128)}, f32[4,8,768]{2,1,0:T(8,128)}, f32[8,768]{1,0:T(8,128)}) custom-call(bf16[1024,768]{1,0:T(8,128)(2,1)} %get-tuple-element.93.gmix_ref, f32[1024,768]{1,0:T(8,128)} %get-tuple-element.94.gmid_ref, f32[4,8,768]{2,1,0:T(8,128)} %get-tuple-element.241.mod_ref, ...), custom_call_target="tpu_custom_call" | custom-call | flops 5637144576 | bytes 25000000 | tf_op jit(solution)/shard_map/pallas_call | solution.py:177
  498.2 46.3 %all-gather.4 = bf16[32,4,1536]{2,1,0:T(4,128)(2,1)} all-gather(bf16[1,4,1536]{2,1,0:T(4,128)(2,1)S(1)} %fusion.43), channel_id=1, replica_groups=mesh['rep'=4,'shard'=8] {'rep','shard'}, dimensions={0}, use_global_device_ids=true | all-gather | bytes 405504 | tf_op jit(solution)/shard_map/all_gather | solution.py:348
  571.3 4.4 concatenate.62
  577.3 28.3 %all-gather.10.cloned.1.call-done = bf16[32,4,4608]{2,1,0:T(4,128)(2,1)} async-done(((bf16[1,4,4608]{2,1,0:T(4,128)(2,1)}), bf16[32,4,4608]{2,1,0:T(4,128)(2,1)}) %all-gather.10.cloned.1.call-update) | async-done | bytes 1179664 | tf_op jit(solution)/shard_map/all_gather | solution.py:362
  607.0 30.4 %reduce-scatter.22.cloned.1.call-done = f32[128,96]{0,1:T(8,128)} async-done(((f32[128,768]{0,1:T(8,128)}), f32[128,96]{0,1:T(8,128)}) %reduce-scatter.22.cloned.1.call-update) | async-done | bytes 49168 | tf_op jit(solution)/shard_map/reduce_scatter | solution.py:351
  641.9 13.3 shard_map.364
  655.2 6.6 convert_element_type.201
  661.9 13.2 shard_map.365
  675.0 6.5 convert_element_type.203
  681.6 3.5 convolution_convert_fusion.3
  685.1 6.5 convolution_convert_fusion.1
  691.6 2.7 pad_maximum_fusion.1
  694.4 3.5 convolution_convert_fusion.2
  697.9 6.5 convolution_convert_fusion
  704.3 2.8 pad_maximum_fusion.2
  707.3 13.1 shard_map.362
  720.4 6.6 convert_element_type.192
  727.1 13.4 shard_map.363
  740.5 6.6 convert_element_type.197
  749.2 19.8 %all-reduce.12.cloned.1.call-done = f32[65,768]{0,1:T(8,128)} async-done(((f32[65,768]{0,1:T(8,128)}), f32[65,768]{0,1:T(8,128)}) %all-reduce.12.cloned.1.call-update) | async-done | bytes 199696 | tf_op jit(solution)/shard_map/psum | solution.py:374
  787.2 14.2 %reduce-scatter.24.cloned.1.call-done = f32[128,96]{0,1:T(8,128)} async-done(((f32[128,768]{0,1:T(8,128)}), f32[128,96]{0,1:T(8,128)}) %reduce-scatter.24.cloned.1.call-update) | async-done | bytes 49168 | tf_op jit(solution)/shard_map/reduce_scatter | solution.py:385
  803.8 53.2 %reduce-scatter.18.cloned.1.call-done = bf16[96,3072]{1,0:T(8,128)(2,1)} async-done(((bf16[768,3072]{1,0:T(8,128)(2,1)}), bf16[96,3072]{1,0:T(8,128)(2,1)}) %reduce-scatter.18.cloned.1.call-update) | async-done | bytes 589840 | tf_op jit(solution)/shard_map/reduce_scatter | solution.py:359
  859.2 53.6 %reduce-scatter.20.cloned.1.call-done = bf16[96,3072]{1,0:T(8,128)(2,1)} async-done(((bf16[768,3072]{1,0:T(8,128)(2,1)}), bf16[96,3072]{1,0:T(8,128)(2,1)}) %reduce-scatter.20.cloned.1.call-update) | async-done | bytes 589840 | tf_op jit(solution)/shard_map/reduce_scatter | solution.py:359
  915.0 53.6 %reduce-scatter.10.cloned.1.call-done = bf16[96,3072]{1,0:T(8,128)(2,1)} async-done(((bf16[768,3072]{1,0:T(8,128)(2,1)}), bf16[96,3072]{1,0:T(8,128)(2,1)}) %reduce-scatter.10.cloned.1.call-update) | async-done | bytes 589840 | tf_op jit(solution)/shard_map/reduce_scatter | solution.py:359
  968.5 56.2 %reduce-scatter.14.cloned.1.call-done = bf16[96,3072]{1,0:T(8,128)(2,1)} async-done(((bf16[768,3072]{1,0:T(8,128)(2,1)}), bf16[96,3072]{1,0:T(8,128)(2,1)}) %reduce-scatter.14.cloned.1.call-update) | async-done | bytes 589840 | tf_op jit(solution)/shard_map/reduce_scatter | solution.py:359
  1024.7 55.8 %reduce-scatter.12.cloned.1.call-done = bf16[96,3072]{1,0:T(8,128)(2,1)} async-done(((bf16[768,3072]{1,0:T(8,128)(2,1)}), bf16[96,3072]{1,0:T(8,128)(2,1)}) %reduce-scatter.12.cloned.1.call-update) | async-done | bytes 589840 | tf_op jit(solution)/shard_map/reduce_scatter | solution.py:359
  1080.5 56.2 %reduce-scatter.16.cloned.1.call-done = bf16[96,3072]{1,0:T(8,128)(2,1)} async-done(((bf16[768,3072]{1,0:T(8,128)(2,1)}), bf16[96,3072]{1,0:T(8,128)(2,1)}) %reduce-scatter.16.cloned.1.call-update) | async-done | bytes 589840 | tf_op jit(solution)/shard_map/reduce_scatter | solution.py:359
  1136.7 196.4 %all-reduce.17 = (f32[96,3072]{1,0:T(8,128)}, f32[96,3072]{1,0:T(8,128)}, f32[96,3072]{1,0:T(8,128)}, f32[96,3072]{1,0:T(8,128)}) all-reduce(bf16[96,3072]{1,0:T(8,128)(2,1)} %reduce-scatter.16.cloned.1.call-done, bf16[96,3072]{1,0:T(8,128)(2,1)} %reduce-scatter.14.cloned.1.call-done, ...), channel_id=1, replica_groups=mesh['rep'=4,'shard'=8] {'rep'}, use_global_device_ids=true, to_apply=%region_23.24 | all-reduce | flops 1179648 | bytes 7077888 | tf_op jit(solution)/shard_map/psum | solution.py:360
  1339.1 2.7 multiply_reduce_fusion
  1348.6 15.9 %psum.63 = f32[]{:T(128)} all-reduce(f32[]{:T(128)S(6)} %add.328), channel_id=1, replica_groups=mesh['rep'=4,'shard'=8] {'shard'}, use_global_device_ids=true, to_apply=%region_36.37 | all-reduce | flops 1 | bytes 8 | tf_op jit(solution)/shard_map/psum | solution.py:393
  1367.7 3.6 fusion.64
  1374.7 5.3 fusion.68
  1381.2 20.6 %fusion.70 = (bf16[2,96,10752]{2,1,0:T(8,128)(2,1)}, f32[2,96,10752]{2,1,0:T(8,128)}, f32[2,96,10752]{2,1,0:T(8,128)}, f32[2,96,10752]{2,1,0:T(8,128)}) fusion(f32[2,96,10752]{2,1,0:T(8,128)} %param.25, f32[]{:T(128)S(6)} %min.3, f32[1,96,10752]{2,1,0:T(8,128)S(1)} %copy-done.2, f32[1,96,10752]{2,1,0:T(8,128)S(1)} %copy-done.4, f32[2,96,10752]{2,1,0:T(8,128)} %param.30, ...), kind=kLoop, calls=%fused_computation.186 | loop fusion | flops 37158912 | bytes 61931524 | tf_op jit(solution)/shard_map/convert_element_type | solution.py:278
  (325 shorter events, 125.9 us)
Async XLA Ops:
  51.3 19.2 %copy-start.62 = (s32[128]{0:T(128)}, s32[128]{0:T(128)S(1)}, u32[]{:S(2)}) copy-start(s32[128]{0:T(128)S(1)} %get-tuple-element.248) | copy-start | bytes 1540
  54.0 43.0 %copy-start.23 = (bf16[2043,96]{1,0:T(8,128)(2,1)}, bf16[2043,96]{1,0:T(8,128)(2,1)S(1)}, u32[]{:S(2)}) copy-start(bf16[2043,96]{1,0:T(8,128)(2,1)S(1)} %copy.192) | copy-start | bytes 1176772
  54.3 15.2 %copy-start.47 = (bf16[128,128]{1,0:T(8,128)(2,1)}, bf16[128,128]{1,0:T(8,128)(2,1)S(1)}, u32[]{:S(2)}) copy-start(bf16[128,128]{1,0:T(8,128)(2,1)S(1)} %get-tuple-element.250) | copy-start | bytes 98308
  54.3 30.3 %copy-start.49 = (bf16[128,128]{1,0:T(8,128)(2,1)}, bf16[128,128]{1,0:T(8,128)(2,1)S(1)}, u32[]{:S(2)}) copy-start(bf16[128,128]{1,0:T(8,128)(2,1)S(1)} %get-tuple-element.251) | copy-start | bytes 98308
  70.5 22.9 %copy-start.35 = (bf16[128,96]{0,1:T(8,128)(2,1)}, bf16[128,96]{0,1:T(8,128)(2,1)S(1)}, u32[]{:S(2)}) copy-start(bf16[128,96]{0,1:T(8,128)(2,1)S(1)} %get-tuple-element.258) | copy-start | bytes 73732
  85.6 204.1 %all-to-all-start = ((f32[8,4,192]{2,1,0:T(4,128)}), f32[8,4,192]{2,1,0:T(4,128)}, u32[]{:S(2)}, u32[]{:S(2)}) async-start(f32[8,4,192]{2,1,0:T(4,128)} %reshape.273), calls=%async_computation | async-start | bytes 65536 | tf_op jit(solution)/shard_map/all_to_all | solution.py:319
  89.6 201.0 %all-reduce.14.cloned.1.call-start = ((), (), s32[]{:S(2)}) async-start(), calls=%async_computation.20 | async-start | bytes 2359296
  96.9 478.9 %all-gather.8.cloned.1.call-start = ((), (), s32[]{:S(2)}) async-start(), calls=%async_computation.18 | async-start | bytes 1216512 | tf_op jit(solution)/shard_map/all_gather | solution.py:362
  276.2 7.6 copy-start.53
  276.2 7.6 copy-start.54
  276.2 7.6 copy-start.65
  276.2 7.6 copy-start.66
  290.6 76.4 %copy-start.55 = (f32[4,768]{1,0:T(4,128)}, f32[4,768]{1,0:T(4,128)S(1)}, u32[]{:S(2)}) copy-start(f32[4,768]{1,0:T(4,128)S(1)} %get-tuple-element.243) | copy-start | bytes 36868
  458.7 32.9 %copy-start.60 = (f32[4,8,768]{2,1,0:T(8,128)S(1)}, f32[4,8,768]{2,1,0:T(8,128)}, u32[]{:S(2)}) copy-start(f32[4,8,768]{2,1,0:T(8,128)} %get-tuple-element.100) | copy-start | bytes 294916
  493.5 112.0 %all-gather.10.cloned.1.call-start = ((), (), s32[]{:S(2)}) async-start(), calls=%async_computation.19 | async-start | bytes 1216512 | tf_op jit(solution)/shard_map/all_gather | solution.py:362
  496.7 140.6 %reduce-scatter.22.cloned.1.call-start = ((), (), s32[]{:S(2)}) async-start(), calls=%async_computation.16 | async-start | bytes 442368 | tf_op jit(solution)/shard_map/reduce_scatter | solution.py:351
  548.4 220.6 %all-reduce.12.cloned.1.call-start = ((), (), s32[]{:S(2)}) async-start(), calls=%async_computation.9 | async-start | bytes 786432 | tf_op jit(solution)/shard_map/psum | solution.py:374
  550.6 11.6 copy-start.51
  552.6 16.7 %copy-start.13 = (f32[1024,768]{1,0:T(8,128)S(1)}, f32[1024,768]{1,0:T(8,128)}, u32[]{:S(2)}) copy-start(f32[1024,768]{1,0:T(8,128)} %get-tuple-element.105) | copy-start | bytes 9437188
  555.6 10.9 copy-start.59
  555.6 12.8 copy-start.58
  575.7 63.3 %copy-start.68 = (f32[128,96]{0,1:T(8,128)S(1)}, f32[128,96]{0,1:T(8,128)}, u32[]{:S(2)}) copy-start(f32[128,96]{0,1:T(8,128)} %get-tuple-element.259) | copy-start | bytes 147460
  575.8 225.6 %reduce-scatter.24.cloned.1.call-start = ((), (), s32[]{:S(2)}) async-start(), calls=%async_computation.17 | async-start | bytes 442368 | tf_op jit(solution)/shard_map/reduce_scatter | solution.py:385
  577.2 63.6 %copy-start.24 = (bf16[2043,96]{1,0:T(8,128)(2,1)S(1)}, bf16[2043,96]{1,0:T(8,128)(2,1)}, u32[]{:S(2)}) copy-start(bf16[2043,96]{1,0:T(8,128)(2,1)} %copy-done.23) | copy-start | bytes 1176772
  640.8 140.1 %copy-start.32 = (f32[128,96]{0,1:T(8,128)}, f32[128,96]{0,1:T(8,128)S(1)}, u32[]{:S(2)}) copy-start(f32[128,96]{0,1:T(8,128)S(1)} %get-tuple-element.263) | copy-start | bytes 147460
  641.8 215.2 %reduce-scatter.18.cloned.1.call-start = ((), (), s32[]{:S(2)}) async-start(), calls=%async_computation.14 | async-start | bytes 5308416 | tf_op jit(solution)/shard_map/reduce_scatter | solution.py:359
  661.8 250.9 %reduce-scatter.20.cloned.1.call-start = ((), (), s32[]{:S(2)}) async-start(), calls=%async_computation.15 | async-start | bytes 5308416 | tf_op jit(solution)/shard_map/reduce_scatter | solution.py:359
  681.6 287.0 %reduce-scatter.10.cloned.1.call-start = ((), (), s32[]{:S(2)}) async-start(), calls=%async_computation.10 | async-start | bytes 5308416 | tf_op jit(solution)/shard_map/reduce_scatter | solution.py:359
  694.3 330.4 %reduce-scatter.14.cloned.1.call-start = ((), (), s32[]{:S(2)}) async-start(), calls=%async_computation.12 | async-start | bytes 5308416 | tf_op jit(solution)/shard_map/reduce_scatter | solution.py:359
  707.2 373.3 %reduce-scatter.12.cloned.1.call-start = ((), (), s32[]{:S(2)}) async-start(), calls=%async_computation.11 | async-start | bytes 5308416 | tf_op jit(solution)/shard_map/reduce_scatter | solution.py:359
  727.0 409.6 %reduce-scatter.16.cloned.1.call-start = ((), (), s32[]{:S(2)}) async-start(), calls=%async_computation.13 | async-start | bytes 5308416 | tf_op jit(solution)/shard_map/reduce_scatter | solution.py:359
  747.1 33.8 %copy-start.63 = (s32[128]{0:T(128)S(1)}, s32[128]{0:T(128)}, u32[]{:S(2)}) copy-start(s32[128]{0:T(128)} %copy-done.62) | copy-start | bytes 1540
  747.1 594.8 %all-reduce.16.cloned.1.call-start = ((), (), s32[]{:S(2)}) async-start(), calls=%async_computation.21 | async-start | bytes 4718592 | tf_op jit(solution)/shard_map/psum | solution.py:360
  749.2 34.0 %copy-start.11 = (f32[768,192]{0,1:T(8,128)}, f32[768,192]{0,1:T(8,128)S(1)}, u32[]{:S(2)}) copy-start(f32[768,192]{0,1:T(8,128)S(1)} %fusion.28) | copy-start | bytes 1769476
  772.5 8.4 copy-start.25
  774.4 11.2 copy-start.36
  775.5 11.7 copy-start.30
  782.1 19.3 %copy-start.57 = (f32[128,96]{0,1:T(8,128)S(1)}, f32[128,96]{0,1:T(8,128)}, u32[]{:S(2)}) copy-start(f32[128,96]{0,1:T(8,128)} %get-tuple-element.257) | copy-start | bytes 147460
  783.2 19.2 %copy-start.48 = (bf16[128,128]{1,0:T(8,128)(2,1)S(1)}, bf16[128,128]{1,0:T(8,128)(2,1)}, u32[]{:S(2)}) copy-start(bf16[128,128]{1,0:T(8,128)(2,1)} %copy-done.47) | copy-start | bytes 98308
  783.3 19.2 %copy-start.50 = (bf16[128,128]{1,0:T(8,128)(2,1)S(1)}, bf16[128,128]{1,0:T(8,128)(2,1)}, u32[]{:S(2)}) copy-start(bf16[128,128]{1,0:T(8,128)(2,1)} %copy-done.49) | copy-start | bytes 98308
  785.6 17.0 %copy-start.18 = (f32[1000,96]{0,1:T(8,128)S(1)}, f32[1000,96]{0,1:T(8,128)}, u32[]{:S(2)}) copy-start(f32[1000,96]{0,1:T(8,128)} %fusion.7) | copy-start | bytes 1152004
  785.6 17.0 %copy-start.43 = (f32[17,96]{0,1:T(8,128)S(1)}, f32[17,96]{0,1:T(8,128)}, u32[]{:S(2)}) copy-start(f32[17,96]{0,1:T(8,128)} %dynamic-slice.10) | copy-start | bytes 19588
  785.6 17.0 %copy-start.44 = (f32[1,96]{0,1:T(8,128)S(1)}, f32[1,96]{0,1:T(8,128)}, u32[]{:S(2)}) copy-start(f32[1,96]{0,1:T(8,128)} %copy.222) | copy-start | bytes 1156
  859.2 473.9 %copy-start.10 = (f32[96,4608]{1,0:T(8,128)S(1)}, f32[96,4608]{1,0:T(8,128)}, u32[]{:S(2)}) copy-start(f32[96,4608]{1,0:T(8,128)} %fusion.80) | copy-start | bytes 5308420
  1341.8 24.1 %copy-start.31 = (f32[769,16]{0,1:T(8,128)S(1)}, f32[769,16]{0,1:T(8,128)}, u32[]{:S(2)}) copy-start(f32[769,16]{0,1:T(8,128)} %copy-done.30) | copy-start | bytes 147652
  1341.9 24.1 %copy-start.40 = (f32[769,16]{0,1:T(8,128)S(1)}, f32[769,16]{0,1:T(8,128)}, u32[]{:S(2)}) copy-start(f32[769,16]{0,1:T(8,128)} %param.29) | copy-start | bytes 147652
  1343.3 24.4 %copy-start.26 = (f32[1,192]{0,1:T(8,128)S(1)}, f32[1,192]{0,1:T(8,128)}, u32[]{:S(2)}) copy-start(f32[1,192]{0,1:T(8,128)} %copy-done.25) | copy-start | bytes 2308
  1374.7 6.4 copy-start.4
  (38 other events, 110.0 us)
Sparse Core Ops, SparseCore 0:
  97.0 77.4 all-reduce.13
  493.7 55.7 all-gather.7
  552.4 53.0 all-gather.9
  607.7 29.6 reduce-scatter.21
  643.4 125.6 all-reduce.11
  771.7 29.6 reduce-scatter.23
  803.8 53.1 reduce-scatter.17
  859.4 53.3 reduce-scatter.19
  915.2 53.3 reduce-scatter.9
  971.3 53.3 reduce-scatter.13
  1027.1 53.3 reduce-scatter.11
  1083.3 53.3 reduce-scatter.15
  1140.7 110.8 all-reduce.15

commit v2 on v1

--- a/solution.py
+++ b/solution.py
@@ -133,13 +133,14 @@
         cost_estimate=pl.CostEstimate(flops=2*T*D*(2*FF+D), bytes_accessed=50_000_000, transcendentals=T*FF),
     )(g,mod,wa,w1,w2,down,upper,mid,attn)
 
-def bwd_attn_kernel(gmix_ref, gmid_ref, mod_ref, wa_ref, qkv_ref, lse_ref, x_ref,
+def bwd_attn_kernel(gmix_ref, alow_ref, gmid_ref, mod_ref, wa_ref, qkv_ref, lse_ref, x_ref,
                     low_ref, gin_ref, dmod_ref, db_ref):
     i=pl.program_id(0)
     mod=lambda j: mod_ref[0, j:j+1, :]
     @pl.when(i==0)
     def _(): db_ref[...]=jnp.zeros_like(db_ref)
     s0=lambda v: jnp.sum(v,axis=0,keepdims=True)
+    low_ref[:, 3*D:]=alow_ref[...]
     lo=half_masks()
     zero=jnp.zeros((TOK,128),bf)
     for hp in range(HEADS//2):
@@ -164,37 +165,24 @@
             if j!=1:
                 row=0 if j==0 else 1
                 db_ref[row:row+1, c:c+128]+=s0(ol.astype(f32))
-    gn=mm_nt(low_ref[:, :D], wa_ref[0])+mm_nt(low_ref[:, D:2*D], wa_ref[1])+mm_nt(low_ref[:, 2*D:], wa_ref[2])
+    gn=mm_nt(low_ref[:, :D], wa_ref[0])+mm_nt(low_ref[:, D:2*D], wa_ref[1])+mm_nt(low_ref[:, 2*D:3*D], wa_ref[2])
     xh,r=ln_parts(x_ref[...])
     dmod_ref[...]=jnp.zeros_like(dmod_ref)
     dmod_ref[0,0:1,:]=s0(gn)
     dmod_ref[0,1:2,:]=s0(gn*xh)
     gin_ref[...]=gmid_ref[...]+ln_back(gn,xh,r,mod(1))
-def layer_bwd_attn(gmix, gmid, mod, wa, qkv, lse, x):
+def layer_bwd_attn(gmix, alow, gmid, mod, wa, qkv, lse, x):
     T=gmix.shape[0]; n=T//TOK
     sd=jax.ShapeDtypeStruct
     m3=pl.BlockSpec((1,8,D),lambda i:(i,0,0))
     return pl.pallas_call(bwd_attn_kernel, grid=(n,),
-        in_specs=[rows(D),rows(D),m3,full((3,D,D)),rows(3*D),rows(128),rows(D)],
-        out_specs=[rows(3*D),rows(D),m3,pl.BlockSpec((8,D),lambda i:(0,0))],
-        out_shape=[sd((T,3*D),bf),sd((T,D),f32),sd((n,8,D),f32),sd((8,D),f32)],
+        in_specs=[rows(D),rows(D),rows(D),m3,full((3,D,D)),rows(3*D),rows(128),rows(D)],
+        out_specs=[rows(4*D),rows(D),m3,pl.BlockSpec((8,D),lambda i:(0,0))],
+        out_shape=[sd((T,4*D),bf),sd((T,D),f32),sd((n,8,D),f32),sd((8,D),f32)],
         compiler_params=pltpu.CompilerParams(vmem_limit_bytes=VLIM),
         cost_estimate=pl.CostEstimate(flops=2*T*D*(3*D+5*TOK), bytes_accessed=25_000_000, transcendentals=T*TOK*HEADS),
-    )(gmix,gmid,mod,wa,qkv,lse,x)
-
-def dw_kernel(x_ref, dy_ref, o_ref, xt_ref):
-    @pl.when(pl.program_id(0)==0)
-    def _(): xt_ref[...]=x_ref[...].T
-    o_ref[...]=mm(xt_ref[...], dy_ref[...])
-def dw(x, dy):
-    T=x.shape[0]; C=dy.shape[1]; W=384
-    return pl.pallas_call(dw_kernel, grid=(C//W,),
-        in_specs=[pl.BlockSpec((T,D),lambda i:(0,0)), pl.BlockSpec((T,W),lambda i:(0,i))],
-        out_specs=pl.BlockSpec((D,W),lambda i:(0,i)),
-        out_shape=jax.ShapeDtypeStruct((D,C),f32),
-        scratch_shapes=[pltpu.VMEM((D,T),bf)],
-        compiler_params=pltpu.CompilerParams(vmem_limit_bytes=VLIM),
-    )(x,dy)
+    )(gmix,alow,gmid,mod,wa,qkv,lse,x)
+
 def gather_kernel(R, nz, U, w_ref, out_ref, zs, zr, xs, xr, cs, cr, ls):
     rep=lax.axis_index("rep"); shard=lax.axis_index("shard")
     z=shard//2; c=lax.rem(shard,2)
@@ -249,8 +237,222 @@
     if R==4: return [out[u] for u in range(U)]
     m=R//4
     return [out[u].reshape(4,m,D,W).transpose(0,2,1,3).reshape(4,D,D) for u in range(U)]
+CW=384; NCH=8
+def bit_orders(R):
+    bits=[1<<i for i in range(R.bit_length()-1)]
+    return [bits[g%len(bits):]+bits[:g%len(bits)] if bits else [] for g in range(NCH//R)]
+def grad_plan(R):
+    orders=bit_orders(R); G=NCH//R; n=len(orders[0])
+    def stage(g,m): return next(i for i,b in enumerate(orders[g]) if m&b)
+    pos=[]
+    for i in range(n+1):
+        ms=[[m for m in range(R) if (m==0 and i==n) or (m and stage(g,m)==i)] for g in range(G)]
+        if i<n: ms=[sorted(v,key=lambda m,g=g:(-bin(m).count("1"),m)) for g,v in enumerate(ms)]
+        for a in range(len(ms[0])):
+            for g in range(G): pos.append((g,ms[g][a],i))
+    send={}; keep={}; recv={}
+    for g,m,i in pos:
+        if m: send[g,m]=len(send)
+        if i>0 or m==0: keep[g,m]=len(keep)
+    for i in range(n):
+        for g in range(G):
+            for m in range(R):
+                if not any(m&b for b in orders[g][:i+1]): recv[g,i,m]=len(recv)
+    return orders,n,pos,send,keep,recv
+
+def grad_kernel(R,nz,own,T, xa,xb,xc,xd, da,db,dc, out_ref, xin,xt,dy,sbuf,obuf,rbuf,sb,rb,kf,zs,zr,az,
+                xsem,dsem,csend,crecv,ssem,rsem,zss,zrs,ass,ars,als):
+    orders,n,pos,send,keep,recv=grad_plan(R)
+    G=NCH//R
+    MESH=pl.DeviceIdType.MESH
+    rep=lax.axis_index("rep"); shard=lax.axis_index("shard")
+    z=shard//2; c=lax.rem(shard,2)
+    xor=lambda m: jnp.bitwise_xor(rep,m)
+    mate=(rep,2*z+1-c)
+    zdev=lambda k: (rep, 2*lax.rem(z+k,nz)+c)
+    rdev=lambda m: (xor(m), shard)
+    bar=pltpu.get_barrier_semaphore()
+    peers=[mate]+[zdev(k) for k in range(1,nz)]+[rdev(m) for m in range(1,R)]
+    for p in peers: pl.semaphore_signal(bar,inc=1,device_id=p,device_id_type=MESH)
+    xs=(xa,xb,xc,xd)
+    xcopy=lambda i: pltpu.make_async_copy(xs[i],xin.at[i%2],xsem.at[i%2])
+    chunk=lambda k: pos[k][0]*R+xor(pos[k][1])
+    def dstart(u,k):
+        for i,ref in enumerate((da,db,dc)):
+            @pl.when(u==i)
+            def _(): pltpu.make_async_copy(ref.at[:,pl.ds(pl.multiple_of(chunk(k)*CW,128),CW)],dy.at[k%4],dsem.at[k%4]).start()
+    def dwait(k): pltpu.make_async_copy(da.at[:,pl.ds(0,CW)],dy.at[k%4],dsem.at[k%4]).wait()
+    ccopy=lambda k: pltpu.make_async_remote_copy(src_ref=sbuf.at[k%2],dst_ref=rbuf.at[k%4],send_sem=csend.at[k%2],recv_sem=crecv.at[k%4],device_id=mate,device_id_type=MESH)
+    def scopy(u,g,m):
+        i=next(i for i,b in enumerate(orders[g]) if m&b); b=orders[g][i]
+        a=send[g,m]; d=recv[g,i,m^b]
+        return pltpu.make_async_remote_copy(src_ref=sb.at[u,a],dst_ref=rb.at[u,d],send_sem=ssem.at[u,a],recv_sem=rsem.at[u,d],device_id=rdev(b),device_id_type=MESH)
+    def rwait(u,g,i,m):
+        d=recv[g,i,m]
+        pltpu.make_async_remote_copy(src_ref=sb.at[u,0],dst_ref=rb.at[u,d],send_sem=ssem.at[u,0],recv_sem=rsem.at[u,d],device_id=rdev(1),device_id_type=MESH).wait_recv()
+    zcopy=lambda u,g,k: pltpu.make_async_remote_copy(src_ref=zs.at[u,g,lax.rem(z+k,nz)],dst_ref=zr.at[u,g,k-1],send_sem=zss.at[u,g,k-1],recv_sem=zrs.at[u,g,k-1],device_id=zdev(k),device_id_type=MESH)
+    def acopy(u,g,m): return pltpu.make_async_remote_copy(src_ref=az.at[u,g],dst_ref=out_ref.at[u,g*R+rep],send_sem=ass.at[u,g,m-1],recv_sem=ars.at[u,g,m-1],device_id=rdev(m),device_id_type=MESH)
+    alocal=lambda u,g: pltpu.make_async_copy(az.at[u,g],out_ref.at[u,g*R+rep],als.at[u,g])
+    def arecv(u,g,m):
+        return pltpu.make_async_remote_copy(src_ref=az.at[u,g],dst_ref=out_ref.at[u,g*R+xor(m)],send_sem=ass.at[u,g,m-1],recv_sem=ars.at[u,g,m-1],device_id=rdev(m),device_id_type=MESH)
+    xcopy(0).start(); xcopy(1).start(); dstart(0,0); dstart(0,1)
+    for i in range(4):
+        xcopy(i).wait()
+        xt[i]=xin[i%2].T
+        if i+2<4: xcopy(i+2).start()
+    pl.semaphore_wait(bar,len(peers))
+    def consume(u,k):
+        g,m,i=pos[k]
+        ccopy(k).wait_recv()
+        total=obuf[k%2]+rbuf[k%4]
+        if i==0 and m:
+            sb[u,send[g,m]]=total.astype(bf)
+            scopy(u,g,m).start()
+        else: kf[u,keep[g,m]]=total.reshape(nz,own,CW)
+    def products(u):
+        for k in range(NCH):
+            if k+2<NCH: dstart(u,k+2)
+            else:
+                @pl.when(u<2)
+                def _(): dstart(u+1,k+2-NCH)
+            dwait(k)
+            xi=u+(u//2)*(chunk(k)//6)
+            p=mm(xt[xi],dy[k%4]).reshape(nz,2,own,CW)
+            even=p[:,0].reshape(nz*own,CW); odd=p[:,1].reshape(nz*own,CW)
+            if k>=2: ccopy(k).wait_send()
+            else:
+                @pl.when(u>0)
+                def _(): ccopy(k).wait_send()
+            sbuf[k%2]=jnp.where(c==0,odd,even)
+            obuf[k%2]=jnp.where(c==0,even,odd)
+            ccopy(k).start()
+            if k>0: consume(u,k-1)
+            else:
+                @pl.when(u>0)
+                def _(): consume(u-1,NCH-1)
+    def middle(u,i):
+        for g,m,j in pos:
+            if m and j==i:
+                v=kf[u,keep[g,m]].reshape(nz*own,CW)
+                for i2 in range(i):
+                    rwait(u,g,i2,m); v=v+rb[u,recv[g,i2,m]].astype(f32)
+                sb[u,send[g,m]]=v.astype(bf)
+                scopy(u,g,m).start()
+    def along(u):
+        for g in range(G):
+            v=kf[u,keep[g,0]]
+            for i2 in range(n):
+                rwait(u,g,i2,0); v=v+rb[u,recv[g,i2,0]].astype(f32).reshape(nz,own,CW)
+            kf[u,keep[g,0]]=v
+            zs[u,g]=v.astype(bf)
+            for k in range(1,nz): zcopy(u,g,k).start()
+    def spread(u):
+        for g in range(G):
+            v=kf[u,keep[g,0],z]
+            for k in range(1,nz):
+                zcopy(u,g,k).wait_recv(); v=v+zr[u,g,k-1].astype(f32)
+            az[u,g]=v
+            alocal(u,g).start()
+            for m in range(1,R): acopy(u,g,m).start()
+    depth=max(n-1,0)
+    def step(t,_):
+        @pl.when(t<3)
+        def _(): products(t)
+        @pl.when(t==3)
+        def _(): consume(2,NCH-1)
+        for i in range(1,n):
+            @pl.when(jnp.logical_and(t>=i,t<3+i))
+            def _(): middle(t-i,i)
+        @pl.when(jnp.logical_and(t>=1+depth,t<4+depth))
+        def _(): along(t-1-depth)
+        @pl.when(jnp.logical_and(t>=2+depth,t<5+depth))
+        def _(): spread(t-2-depth)
+        return 0
+    lax.fori_loop(0,5+depth,step,0)
+    def finish(u,_):
+        for g in range(G):
+            alocal(u,g).wait()
+            for m in range(1,R): arecv(u,g,m).wait_recv(); acopy(u,g,m).wait_send()
+            for k in range(1,nz): zcopy(u,g,k).wait_send()
+            for m in range(1,R): scopy(u,g,m).wait_send()
+        return 0
+    lax.fori_loop(0,3,finish,0)
+    ccopy(NCH-2).wait_send(); ccopy(NCH-1).wait_send()
+
+def layer_grads(R,S,cid,xs,dys):
+    T=xs[0].shape[0]; nz=S//2; own=D//S; G=NCH//R
+    orders,n,pos,send,keep,recv=grad_plan(R)
+    dma=pltpu.SemaphoreType.DMA; V=pltpu.VMEM
+    any_=pl.BlockSpec(memory_space=pl.ANY)
+    ns,nk,nr=max(len(send),1),len(keep),max(len(recv),1)
+    return pl.pallas_call(functools.partial(grad_kernel,R,nz,own,T),
+        in_specs=[any_]*7, out_specs=any_, out_shape=jax.ShapeDtypeStruct((3,NCH,own,CW),f32),
+        scratch_shapes=[V((2,T,D),bf),V((4,D,T),bf),V((4,T,CW),bf),V((2,D//2,CW),f32),V((2,D//2,CW),f32),V((4,D//2,CW),f32),
+            V((3,ns,D//2,CW),bf),V((3,nr,D//2,CW),bf),V((3,nk,nz,own,CW),f32),V((3,G,nz,own,CW),bf),V((3,G,nz-1,own,CW),bf),V((3,G,own,CW),f32),
+            dma((2,)),dma((4,)),dma((2,)),dma((4,)),dma((3,ns)),dma((3,nr)),dma((3,G,nz-1)),dma((3,G,nz-1)),dma((3,G,R-1)),dma((3,G,R-1)),dma((3,G))],
+        compiler_params=pltpu.CompilerParams(collective_id=cid,has_side_effects=True,vmem_limit_bytes=VLIM),
+        cost_estimate=pl.CostEstimate(flops=2*T*D*9216,bytes_accessed=40_000_000,transcendentals=0),
+    )(*xs,*dys)
+LAYERS=2
+beta_one=0.9; beta_two=0.999; adam_eps=1e-8; learn_rate=0.01; weight_decay=0.01; step_count=10.0
+def adam_update(w,g,m,v,factor):
+    s=g*factor
+    m2=beta_one*m+(1.0-beta_one)*s
+    v2=beta_two*v+(1.0-beta_two)*s*s
+    mh=m2/(1.0-beta_one**step_count)
+    vh=v2/(1.0-beta_two**step_count)
+    w2=w-learn_rate*(mh/(jnp.sqrt(vh)+adam_eps)+weight_decay*w)
+    return (w2,m2,v2,w2.astype(bf))
+def inner_adam_kernel(f_ref,g0_ref,g1_ref,ada_ref,w_ref,m_ref,v_ref,*outs):
+    factor=f_ref[0]; l=pl.program_id(0); j=pl.program_id(1)
+    def put(sl,g):
+        for o,val in zip(outs,adam_update(w_ref[0,:,sl],g,m_ref[0,:,sl],v_ref[0,:,sl],factor)): o[0,:,sl]=val
+    for a in range(2):
+        sl=slice(a*CW,(a+1)*CW)
+        for layer,ref in enumerate((g0_ref,g1_ref)):
+            @pl.when(jnp.logical_and(j<8,l==layer))
+            def _(): put(sl,ref[0,a])
+        @pl.when(j>=8)
+        def _(): put(sl,ada_ref[0,:,sl])
+def inner_adam(factor,g0,g1,ada,w,m,v):
+    own=w.shape[1]; C=w.shape[2]; W=2*CW
+    blk=pl.BlockSpec((1,own,W),lambda l,j:(l,0,j))
+    def gmap(layer):
+        def index(l,j):
+            jj=jnp.minimum(j,7); on=jnp.where(l==layer,jj,7*(l>layer))
+            return (2-on//4, on%4, 0, 0)
+        return pl.BlockSpec((1,2,own,CW),index)
+    sd=jax.ShapeDtypeStruct
+    return pl.pallas_call(inner_adam_kernel,grid=(LAYERS,C//W),
+        in_specs=[pl.BlockSpec(memory_space=pltpu.SMEM),gmap(0),gmap(1),pl.BlockSpec((1,own,W),lambda l,j:(l,0,jnp.maximum(j-8,0))),blk,blk,blk],
+        out_specs=[blk]*4,out_shape=[sd(w.shape,f32)]*3+[sd(w.shape,bf)],
+        compiler_params=pltpu.CompilerParams(vmem_limit_bytes=VLIM))(factor,g0,g1,ada,w,m,v)
+def outer_adam_kernel(f_ref,g0_ref,g1_ref,b_ref,w_ref,m_ref,v_ref,*outs):
+    factor=f_ref[0]; l=pl.program_id(0); j=pl.program_id(1)
+    def put(sl,g):
+        for o,val in zip(outs,adam_update(w_ref[0,sl],g,m_ref[0,sl],v_ref[0,sl],factor)): o[0,sl]=val
+    for a in range(2):
+        sl=slice(a*CW,(a+1)*CW)
+        for layer,ref in enumerate((g0_ref,g1_ref)):
+            @pl.when(jnp.logical_and(j<4,l==layer))
+            def _(): put(sl,ref[0,a].T)
+    @pl.when(j==4)
+    def _(): put(slice(0,16),b_ref[0])
+def outer_adam(factor,g0,g1,b,w,m,v):
+    own=w.shape[2]; W=2*CW
+    blk=pl.BlockSpec((1,W,own),lambda l,j:(l,j,0))
+    def gmap(layer):
+        def index(l,j):
+            jj=jnp.minimum(j,3); on=jnp.where(l==layer,jj,3*(l>layer))
+            return (0, on, 0, 0)
+        return pl.BlockSpec((1,2,own,CW),index)
+    sd=jax.ShapeDtypeStruct
+    return pl.pallas_call(outer_adam_kernel,grid=(LAYERS,5),
+        in_specs=[pl.BlockSpec(memory_space=pltpu.SMEM),gmap(0),gmap(1),pl.BlockSpec((1,16,own),lambda l,j:(l,0,0)),blk,blk,blk],
+        out_specs=[blk]*4,out_shape=[sd(w.shape,f32)]*3+[sd(w.shape,bf)],
+        compiler_params=pltpu.CompilerParams(vmem_limit_bytes=VLIM))(factor,g0,g1,b,w,m,v)
 P_SIZE=16; GRID=16; LAYERS=2; LAT_DEV=4; FREQ=256; NCLASS=1000
-clip_coef=2.5; beta_one=0.9; beta_two=0.999; adam_eps=1e-8; learn_rate=0.01; weight_decay=0.01; step_count=10.0
+clip_coef=2.5
 BIAS=14
 def position_table(grid_side, feature_width):
     quarter=feature_width//4
@@ -268,14 +470,6 @@
     c=x-jnp.mean(x,axis=-1,keepdims=True)
     v=jnp.mean(c*c,axis=-1,keepdims=True)
     return c*lax.rsqrt(v+norm_eps)*(1.0+sc[:,None,:])+sh[:,None,:]
-def adam_update(w,g,m,v,factor):
-    s=g*factor
-    m2=beta_one*m+(1.0-beta_one)*s
-    v2=beta_two*v+(1.0-beta_two)*s*s
-    mh=m2/(1.0-beta_one**step_count)
-    vh=v2/(1.0-beta_two**step_count)
-    w2=w-learn_rate*(mh/(jnp.sqrt(vh)+adam_eps)+weight_decay*w)
-    return (w2,m2,v2,w2.astype(bf))
 def dot32(pattern,a,b): return jnp.einsum(pattern,a,b,preferred_element_type=f32)
 def silu_back(v,g): return jax.vjp(jax.nn.silu,v)[1](g)[0]
 ALL=("rep","shard")
@@ -349,20 +543,20 @@
     fin_mine=lax.dynamic_slice_in_dim(fin_rows,shard*fin_cols,fin_cols,1)
     final_main=dot32("nd,ne->de",cond_all,fin_mine)
     grad_cond=lax.psum_scatter(dot32("ne,de->nd",fin_mine,final_low[:D]),"shard",scatter_dimension=1,tiled=True)
-    unit_parts=[None]*LAYERS; ada_parts=[None]*LAYERS; bias_grads=[None]*LAYERS
+    ada_parts=[None]*LAYERS; bias_grads=[None]*LAYERS; operands=[None]*LAYERS
     for l in range(LAYERS-1,-1,-1):
         wa,w1,w2=gathered[l]
         x,normed,qkv,lse,mixed,attn,mid,ntwo,upper,activ,down,_=saved[l]
         dlow,ulow,gmid,alow,gmix,dm1,db1=layer_bwd_mlp(grad_stream,modul[l],wa,w1,w2,down,upper,mid,attn)
-        low,grad_stream,dm2,db2=layer_bwd_attn(gmix,gmid,modul[l],wa,qkv,lse,x)
-        units=[jnp.concatenate([dot32("td,te->de",normed,low),dot32("td,te->de",mixed,alow)],axis=1),dw(ntwo,ulow),dw(dlow,activ)]
-        units=[lax.psum_scatter(u.astype(bf),"shard",scatter_dimension=0,tiled=True) for u in units]
-        unit_parts[l]=[lax.psum(u.astype(f32),"rep") for u in units]
+        low,grad_stream,dm2,db2=layer_bwd_attn(gmix,alow,gmid,modul[l],wa,qkv,lse,x)
+        operands[l]=((dlow,ntwo,normed,mixed),(activ,ulow,low))
         dmod=jnp.concatenate([dm2[:,:2],dm1[:,2:6]],axis=1)
         rows_all=lax.all_gather(dmod.astype(bf).reshape(LAT_DEV,6*D),ALL,axis=0,tiled=True)
         ada_parts[l]=dot32("nd,ne->de",cond_own,rows_all)
         grad_cond=grad_cond+dot32("ne,de->nd",rows_all,ada_own[l])
         bias_grads[l]=jnp.concatenate([db2[0:2],db1[2:7],jnp.sum(dmod,axis=0),db1[13:14]],axis=0)
+    ops1,grad_stream=lax.optimization_barrier((operands[1],grad_stream))
+    grads1=layer_grads(R,S,LAYERS+1,*ops1)
     gs=grad_stream.reshape(LAT_DEV,TOK,D)
     patch_grad=dot32("gpt,gtd->pd",patches,gs.astype(bf))
     patch_bias=jnp.sum(grad_stream,axis=0)
@@ -377,25 +571,31 @@
     head_total=sums[o3:o4].reshape(-1)[:(D+1)*P_SIZE].reshape(D+1,P_SIZE)
     fin_bias_own=lax.dynamic_slice_in_dim(sums[o2:o3].reshape(2*D),shard*fin_cols,fin_cols,0)
     mine=lax.dynamic_slice_in_dim(sums[:o2],shard*own,own,1)
+    grad_cond,grads1=lax.optimization_barrier((grad_cond,grads1))
     grad_condition=silu_back(condition,grad_cond)
     b2=jnp.sum(grad_condition,axis=0)
     clow=grad_condition.astype(bf)
     second=dot32("nd,ne->de",time_act,clow)
     class_grad=jnp.einsum("nc,nd->cd",hot.astype(f32),grad_condition,precision=lax.Precision.HIGHEST)
-    grad_time_act=lax.psum_scatter(dot32("ne,de->nd",clow,embed_low[r2:r2+D]),"shard",scatter_dimension=1,tiled=True)
+    time_part=dot32("ne,de->nd",clow,embed_low[r2:r2+D])
+    time_part,ops0=lax.optimization_barrier((time_part,operands[0]))
+    grad_time_act=lax.psum_scatter(time_part,"shard",scatter_dimension=1,tiled=True)
+    grads0=layer_grads(R,S,LAYERS,*ops0)
+    grads0,grad_time_act=lax.optimization_barrier((grads0,grad_time_act))
     grad_time=silu_back(hidden,grad_time_act)
     first=dot32("nf,nd->fd",features,grad_time.astype(bf))
     embed_grad=jnp.concatenate([mine[o1:o2],first,jnp.sum(grad_time,axis=0)[None],second,b2[None],class_grad],axis=0)
     final_grad=jnp.concatenate([final_main,fin_bias_own[None]],axis=0)
-    inner_grad=jnp.stack([jnp.concatenate([unit_parts[l][0],unit_parts[l][1],ada_parts[l]],axis=1) for l in range(LAYERS)])
-    outer_grad=jnp.stack([jnp.concatenate([unit_parts[l][2].T,mine[l*BIAS:(l+1)*BIAS]],axis=0) for l in range(LAYERS)])
+    ada_grad=jnp.stack(ada_parts)
+    bias_grad=jnp.pad(mine[:o1].reshape(LAYERS,BIAS,own),((0,0),(0,2),(0,0)))
     sq=lambda a: jnp.sum(a*a)
-    square=lax.psum(sq(inner_grad)+sq(outer_grad)+sq(embed_grad)+sq(final_grad),"shard")
+    square=lax.psum(sq(grads0)+sq(grads1)+sq(ada_grad)+sq(bias_grad)+sq(embed_grad)+sq(final_grad),"shard")
     grad_norm=jnp.sqrt(square+sq(head_total))
     factor=jnp.minimum(1.0,clip_coef*math.sqrt(D/count)/grad_norm)
     out=[mean_loss,grad_norm]
-    for w,g,m,v in ((inner_weights,inner_grad,inner_moment,inner_square),(outer_weights,outer_grad,outer_moment,outer_square),
-                    (embed_table,embed_grad,embed_moment,embed_square),(final_mod,final_grad,final_moment,final_square),
+    out.extend(inner_adam(factor.reshape(1),grads0,grads1,ada_grad,inner_weights,inner_moment,inner_square))
+    out.extend(outer_adam(factor.reshape(1),grads0,grads1,bias_grad,outer_weights,outer_moment,outer_square))
+    for w,g,m,v in ((embed_table,embed_grad,embed_moment,embed_square),(final_mod,final_grad,final_moment,final_square),
                     (head_weights,head_total,head_moment,head_square)):
         out.extend(adam_update(w,g,m,v,factor))
     return tuple(out)

time: 1420 us -> 1030 us (0.73)
  waiting for transfers between devices: 421 us -> 105 us
  Pallas kernels: 388 us -> 594 us
  blocking collectives: 345 us -> 145 us
  other arithmetic: 103 us -> 45.4 us
  matrix products: 47.4 us -> 27.4 us
    reduce_scatter x7 -> x1, waiting for transfers between devices: 343 us -> 0.01 us  [per_device(): lax.psum_scatter(time_part, 'shard', scatter_dimension=1, tiled=True)]
    pallas_call x6, Pallas kernels: 117 us -> 325 us  [the longest x2 215 us: layer_grads(): pl.pallas_call(functools.partial(grad_kernel, R, nz, own, T), in_specs=[a...]
    psum x2 -> x1, blocking collectives: 212 us -> 14.4 us  [per_device(): lax.psum(sq(grads0) + sq(grads1) + sq(ada_grad) + sq(bias_grad) + sq(embe...]
    all_gather x2, waiting for transfers between devices: 28.3 us -> 77.2 us  [per_device(): lax.all_gather(dmod.astype(bf).reshape(LAT_DEV, 6 * D), ALL, axis=0, tile...]
    convert_element_type x5 -> x3, other arithmetic: 33.2 us -> 5.47 us  [adam_update(): return (w2, m2, v2, w2.astype(bf))]
    convert_element_type x4 -> x0, other arithmetic: 26.3 us -> none  [per_device(): u.astype(bf)]
    dot_general x23 -> x19, matrix products: 46.2 us -> 25.4 us  [dot32(): return jnp.einsum(pattern, a, b, preferred_element_type=f32)]
    psum x1, waiting for transfers between devices: 19.8 us -> 0.02 us  [per_device(): lax.psum(jnp.concatenate(bias_grads + [patch_grad, patch_bias[None], fin_...]
  transfers between devices with their start and end apart: 14 -> 7, of which waited for: 10 -> 3; matrix products, arithmetic and copies ran while one was open for 11% -> 6% of each run, Pallas kernels for 14% -> 35%
where the time goes in v2:
time: 1030 us; the launch traced here: 1020 us
  Pallas kernels  594 us (58%)
  blocking collectives  145 us (14%)
  waiting for transfers between devices  105 us (10%)
  local copies, waits for them, and re-layouts  79.2 us (8%)
  other arithmetic  45.4 us (4%)
  matrix products  27.4 us (3%)
  between operations  23.9 us (2%)
    pallas_call x2, Pallas kernels, layer_grads(): pl.pallas_call(functools.partial(grad_kernel, R, nz, own, T), in_specs=[a...  215 us
    pallas_call x2, Pallas kernels, gather_layer(): pl.pallas_call(functools.partial(gather_kernel, R, nz, U), in_specs=[any_...  147 us
    all_gather x2, waiting for transfers between devices, per_device(): lax.all_gather(dmod.astype(bf).reshape(LAT_DEV, 6 * D), ALL, axis=0, tile...  77.2 us
    pallas_call x2, Pallas kernels, layer_fwd(): pl.pallas_call(fwd_kernel, grid=(n,), in_specs=[rows(D), pl.BlockSpec((1,...  71.2 us
    pallas_call x2, Pallas kernels, layer_bwd_attn(): pl.pallas_call(bwd_attn_kernel, grid=(n,), in_specs=[rows(D), rows(D), ro...  64.7 us
    pallas_call x2, Pallas kernels, layer_bwd_mlp(): pl.pallas_call(bwd_mlp_kernel, grid=(n,), in_specs=[rows(D), m3, pl.Block...  51.9 us
    all_gather x1, blocking collectives, per_device(): fin_rows = lax.all_gather(grad_fin.astype(bf), ALL, axis=0, tiled=True)  43.4 us
    all_gather x1, blocking collectives, per_device(): lax.all_gather(jnp.stack([time_steps, labels], axis=1), ALL, axis=0, tile...  43.3 us
  transfers between devices with their start and end apart: 7, of which 3 were waited for; matrix products, arithmetic and copies ran while one was open for 6% of the time, Pallas kernels for 35%

profile of v2, /device:TPU:0, one launch (start us, length us, event | category | flops | bytes accessed | tf_op | source)
XLA Modules:
  0.0 1023.5 jit_solution(17319330896290743677)
XLA Ops:
  9.5 43.3 %all-gather.1 = s32[32,4,2]{1,2,0:T(2,128)S(1)} all-gather(s32[1,4,2]{1,2,0:T(2,128)S(1)} %add_bitcast_fusion.1), channel_id=1, replica_groups=mesh['rep'=4,'shard'=8] {'rep','shard'}, dimensions={0}, use_global_device_ids=true | all-gather | bytes 1056 | tf_op jit(solution)/shard_map/all_gather | solution.py:494
  54.1 14.1 %all_gather.23 = bf16[128,768]{0,1:T(8,128)(2,1)S(1)} all-gather(bf16[128,96]{0,1:T(8,128)(2,1)S(1)} %get-tuple-element.346), channel_id=1, replica_groups=mesh['rep'=4,'shard'=8] {'shard'}, dimensions={1}, use_global_device_ids=true | all-gather | bytes 221184 | tf_op jit(solution)/shard_map/all_gather | solution.py:500
  68.1 5.8 convert_element_type.144
  75.2 3.0 fusion
  78.2 14.6 %all_gather.24 = bf16[128,768]{0,1:T(8,128)(2,1)S(1)} all-gather(bf16[128,96]{0,1:T(8,128)(2,1)S(1)} %get-tuple-element.348), channel_id=1, replica_groups=mesh['rep'=4,'shard'=8] {'shard'}, dimensions={1}, use_global_device_ids=true | all-gather | bytes 221184 | tf_op jit(solution)/shard_map/all_gather | solution.py:504
  94.5 3.3 all-to-all-start
  99.6 2.9 fusion.72
  103.8 14.8 %all-gather = bf16[8,96,45]{1,2,0:T(8,128)(2,1)S(1)} all-gather(bf16[1,96,45]{1,2,0:T(8,128)(2,1)S(1)} %maximum_bitcast_fusion.2), channel_id=1, replica_groups=mesh['rep'=4,'shard'=8] {'shard'}, dimensions={0}, use_global_device_ids=true | all-gather | bytes 77760 | tf_op jit(solution)/shard_map/all_gather | solution.py:491
  120.4 74.0 %shard_map.354 = bf16[3,4,4,2,96,768]{5,4,3,2,1,0:T(8,128)(2,1)S(1)} custom-call(bf16[3,4,96,768]{3,2,1,0:T(8,128)(2,1)S(1)} %maximum_bitcast_fusion.w_ref), custom_call_target="tpu_custom_call" | custom-call | tf_op jit(solution)/shard_map/pallas_call | solution.py:231
  194.4 5.6 fusion.71
  200.8 72.7 %shard_map.356 = bf16[3,4,4,2,96,768]{5,4,3,2,1,0:T(8,128)(2,1)S(1)} custom-call(bf16[3,4,96,768]{3,2,1,0:T(8,128)(2,1)S(1)} %maximum_bitcast_fusion.1.w_ref), custom_call_target="tpu_custom_call" | custom-call | tf_op jit(solution)/shard_map/pallas_call | solution.py:231
  273.6 5.5 fusion.70
  279.1 1.9 multiply_sine_fusion.1
  281.4 2.2 add_add_fusion.1
  289.6 35.8 %shard_map.355 = (bf16[1024,768]{1,0:T(8,128)(2,1)}, bf16[1024,2304]{1,0:T(8,128)(2,1)}, f32[1024,128]{1,0:T(8,128)}, bf16[1024,768]{1,0:T(8,128)(2,1)}, f32[102...) custom-call(f32[1024,768]{1,0:T(8,128)} %bitcast.147, ...), custom_call_target="tpu_custom_call" | custom-call | flops 15300820992 | bytes 60000000 | tf_op jit(solution)/shard_map/pallas_call | solution.py:81
  325.4 35.4 %shard_map.357 = (bf16[1024,768]{1,0:T(8,128)(2,1)}, bf16[1024,2304]{1,0:T(8,128)(2,1)}, f32[1024,128]{1,0:T(8,128)}, bf16[1024,768]{1,0:T(8,128)(2,1)}, f32[102...) custom-call(f32[1024,768]{1,0:T(8,128)} %get-tuple-element.106.x_ref, ...), custom_call_target="tpu_custom_call" | custom-call | flops 15300820992 | bytes 60000000 | tf_op jit(solution)/shard_map/pallas_call | solution.py:81
  360.8 2.3 reduce_sum.195
  364.2 2.2 multiply_reduce_fusion.8
  369.6 2.2 multiply_reduce_fusion.3
  371.8 2.2 broadcast_add_fusion
  373.9 25.9 %shard_map.358 = (bf16[1024,768]{1,0:T(8,128)(2,1)}, bf16[1024,3072]{1,0:T(8,128)(2,1)}, f32[1024,768]{1,0:T(8,128)}, bf16[1024,768]{1,0:T(8,128)(2,1)}, bf16[10...) custom-call(f32[1024,768]{1,0:T(8,128)} %bitcast.146, f32[4,8,768]{2,1,0:T(8,128)} %get-tuple-element.328.mod_ref, ...), custom_call_target="tpu_custom_call" | custom-call | flops 10871635968 | bytes 50000000 | tf_op jit(solution)/shard_map/pallas_call | solution.py:128
  399.9 32.2 %shard_map.359 = (bf16[1024,3072]{1,0:T(8,128)(2,1)}, f32[1024,768]{1,0:T(8,128)}, f32[4,8,768]{2,1,0:T(8,128)}, f32[8,768]{1,0:T(8,128)}) custom-call(bf16[1024,768]{1,0:T(8,128)(2,1)} %get-tuple-element.112.gmix_ref, bf16[1024,768]{1,0:T(8,128)(2,1)} %get-tuple-element.113.alow_ref, f32[1024,768]{1,0:T(8,128)} %get-tuple-element.114.gmid_ref, ...), custom_call_target="tpu_custom_call" | custom-call | flops 5637144576 | bytes 25000000 | tf_op jit(solution)/shard_map/pallas_call | solution.py:178
  432.1 26.0 %shard_map.360 = (bf16[1024,768]{1,0:T(8,128)(2,1)}, bf16[1024,3072]{1,0:T(8,128)(2,1)}, f32[1024,768]{1,0:T(8,128)}, bf16[1024,768]{1,0:T(8,128)(2,1)}, bf16[10...) custom-call(f32[1024,768]{1,0:T(8,128)} %get-tuple-element.117.g_ref, ...), custom_call_target="tpu_custom_call" | custom-call | flops 10871635968 | bytes 50000000 | tf_op jit(solution)/shard_map/pallas_call | solution.py:128
  461.3 32.5 %shard_map.361 = (bf16[1024,3072]{1,0:T(8,128)(2,1)}, f32[1024,768]{1,0:T(8,128)}, f32[4,8,768]{2,1,0:T(8,128)}, f32[8,768]{1,0:T(8,128)}) custom-call(bf16[1024,768]{1,0:T(8,128)(2,1)} %get-tuple-element.122.gmix_ref, bf16[1024,768]{1,0:T(8,128)(2,1)} %get-tuple-element.123.alow_ref, f32[1024,768]{1,0:T(8,128)} %get-tuple-element.124.gmid_ref, ...), custom_call_target="tpu_custom_call" | custom-call | flops 5637144576 | bytes 25000000 | tf_op jit(solution)/shard_map/pallas_call | solution.py:178
  493.8 3.2 fusion.73
  512.5 4.7 concatenate.42
  518.9 2.4 copy.255.w_ref
  521.2 3.7 copy.256.m_ref
  524.9 2.3 copy.257.v_ref
  527.2 43.4 %all-gather.2 = bf16[32,4,1536]{2,1,0:T(4,128)(2,1)S(1)} all-gather(bf16[1,4,1536]{2,1,0:T(4,128)(2,1)S(1)} %fusion.41), channel_id=1, replica_groups=mesh['rep'=4,'shard'=8] {'rep','shard'}, dimensions={0}, use_global_device_ids=true | all-gather | bytes 405504 | tf_op jit(solution)/shard_map/all_gather | solution.py:542
  571.9 108.1 %shard_map.362.g1_ref = f32[3,8,96,384]{3,2,1,0:T(8,128)} custom-call(bf16[1024,768]{1,0:T(8,128)(2,1)} %get-tuple-element.144.xa, bf16[1024,768]{1,0:T(8,128)(2,1)} %get-tuple-element.145.xb, bf16[1024,768]{1,0:T(8,128)(2,1)} %get-tuple-element.146.xc, bf16[1024,768]{1,0:T(8,128)(2,1)} %get-tuple-element.147.xd, bf16[1024,3072]{1,0:T(8,128)(2,1)} %get-tuple-element.148.da, ...), custom_call_target="tpu_custom_call" | custom-call | flops 14495514624 | bytes 40000000 | tf_op jit(solution)/shard_map/pallas_call | solution.py:388
  688.9 21.6 %all-gather.10.cloned.1.call-done = bf16[32,4,4608]{2,1,0:T(4,128)(2,1)} async-done(((bf16[1,4,4608]{2,1,0:T(4,128)(2,1)}), bf16[32,4,4608]{2,1,0:T(4,128)(2,1)}) %all-gather.10.cloned.1.call-update) | async-done | bytes 1179664 | tf_op jit(solution)/shard_map/all_gather | solution.py:554
  711.9 55.6 %all-gather.8.cloned.1.call-done = bf16[32,4,4608]{2,1,0:T(4,128)(2,1)} async-done(((bf16[1,4,4608]{2,1,0:T(4,128)(2,1)}), bf16[32,4,4608]{2,1,0:T(4,128)(2,1)}) %all-gather.8.cloned.1.call-update) | async-done | bytes 1179664 | tf_op jit(solution)/shard_map/all_gather | solution.py:554
  772.1 27.8 %reduce-scatter.4.cloned.1.call-done = f32[128,96]{0,1:T(8,128)} async-done(((f32[128,768]{0,1:T(8,128)}), f32[128,96]{0,1:T(8,128)}) %reduce-scatter.4.cloned.1.call-update) | async-done | bytes 49168 | tf_op jit(solution)/shard_map/reduce_scatter | solution.py:545
  804.6 107.0 %shard_map.363.g0_ref = f32[3,8,96,384]{3,2,1,0:T(8,128)} custom-call(bf16[1024,768]{1,0:T(8,128)(2,1)} %get-tuple-element.159.xa, bf16[1024,768]{1,0:T(8,128)(2,1)} %get-tuple-element.160.xb, bf16[1024,768]{1,0:T(8,128)(2,1)} %get-tuple-element.161.xc, bf16[1024,768]{1,0:T(8,128)(2,1)} %get-tuple-element.162.xd, bf16[1024,3072]{1,0:T(8,128)(2,1)} %get-tuple-element.163.da, ...), custom_call_target="tpu_custom_call" | custom-call | flops 14495514624 | bytes 40000000 | tf_op jit(solution)/shard_map/pallas_call | solution.py:388
  911.7 5.3 pad_maximum_fusion
  917.8 2.0 fusion.5
  919.7 1.8 fusion.42
  927.4 3.5 multiply_reduce_fusion.2
  936.1 14.4 %psum.15 = f32[]{:T(128)} all-reduce(f32[]{:T(128)S(6)} %add.284), channel_id=1, replica_groups=mesh['rep'=4,'shard'=8] {'shard'}, use_global_device_ids=true, to_apply=%region_26.27 | all-reduce | flops 1 | bytes 8 | tf_op jit(solution)/shard_map/psum | solution.py:592
  951.9 12.4 %shard_map.365 = (f32[2,3086,96]{2,1,0:T(8,128)}, f32[2,3086,96]{2,1,0:T(8,128)}, f32[2,3086,96]{2,1,0:T(8,128)}, bf16[2,3086,96]{2,1,0:T(8,128)(2,1)}) custom-call(f32[1]{0:T(128)} %bitcast.47.f_ref, f32[3,8,96,384]{3,2,1,0:T(8,128)} %shard_map.363.g0_ref, f32[3,8,96,384]{3,2,1,0:T(8,128)} %shard_map.362.g1_ref, f32[2,16,96]{2,1,0:T(8,128)} %get-tuple-element.332.b_ref, ...), custom_call_target="tpu_custom_call" | custom-call | tf_op jit(solution)/shard_map/pallas_call | solution.py:450
  964.3 3.4 copy.258
  967.8 3.4 copy.259
  971.2 3.6 copy.260
  974.8 2.6 copy.261
  979.2 1.8 fusion.62
  980.9 2.0 fusion.64
  982.9 32.4 %shard_map.364 = (f32[2,96,10752]{2,1,0:T(8,128)}, f32[2,96,10752]{2,1,0:T(8,128)}, f32[2,96,10752]{2,1,0:T(8,128)}, bf16[2,96,10752]{2,1,0:T(8,128)(2,1)}) custom-call(f32[1]{0:T(128)} %bitcast.47.f_ref, f32[3,8,96,384]{3,2,1,0:T(8,128)} %shard_map.363.g0_ref, f32[3,8,96,384]{3,2,1,0:T(8,128)} %shard_map.362.g1_ref, ...), custom_call_target="tpu_custom_call" | custom-call | tf_op jit(solution)/shard_map/pallas_call | solution.py:426
  (264 shorter events, 70.9 us)
Async XLA Ops:
  7.2 280.6 %all-reduce.11.cloned.1.call-start = ((), (), s32[]{:S(2)}) async-start(), calls=%async_computation.8 | async-start | bytes 2359296
  8.7 65.5 %copy-start.16 = (bf16[2043,96]{1,0:T(8,128)(2,1)}, bf16[2043,96]{1,0:T(8,128)(2,1)S(1)}, u32[]{:S(2)}) copy-start(bf16[2043,96]{1,0:T(8,128)(2,1)S(1)} %copy.220) | copy-start | bytes 1176772
  52.9 21.4 %copy-start.45 = (s32[128]{0:T(128)}, s32[128]{0:T(128)S(1)}, u32[]{:S(2)}) copy-start(s32[128]{0:T(128)S(1)} %get-tuple-element.338) | copy-start | bytes 1540
  68.1 5.8 copy-start.22
  74.0 18.9 %copy-start.7 = (f32[769,192]{0,1:T(8,128)S(1)}, f32[769,192]{0,1:T(8,128)}, u32[]{:S(2)}) copy-start(f32[769,192]{0,1:T(8,128)} %param.28) | copy-start | bytes 1771780
  92.8 9.7 copy-start.2
  94.5 193.2 %all-to-all-start = ((f32[8,4,192]{2,1,0:T(4,128)}), f32[8,4,192]{2,1,0:T(4,128)S(1)}, u32[]{:S(2)}, u32[]{:S(2)}) async-start(f32[8,4,192]{2,1,0:T(4,128)} %reshape.280), calls=%async_computation | async-start | bytes 65536 | tf_op jit(solution)/shard_map/all_to_all | solution.py:513
  97.8 582.5 %all-reduce.9.cloned.1.call-start = ((), (), s32[]{:S(2)}) async-start(), calls=%async_computation.3 | async-start | bytes 786432 | tf_op jit(solution)/shard_map/psum | solution.py:568
  102.6 17.5 %copy-start.11 = (bf16[1,96,3072]{2,1,0:T(8,128)(2,1)S(1)}, bf16[1,96,3072]{2,1,0:T(8,128)(2,1)}, u32[]{:S(2)}) copy-start(bf16[1,96,3072]{2,1,0:T(8,128)(2,1)} %get-tuple-element.318) | copy-start | bytes 1769476
  102.7 17.5 %copy-start.12 = (bf16[1,96,3072]{2,1,0:T(8,128)(2,1)S(1)}, bf16[1,96,3072]{2,1,0:T(8,128)(2,1)}, u32[]{:S(2)}) copy-start(bf16[1,96,3072]{2,1,0:T(8,128)(2,1)} %get-tuple-element.319) | copy-start | bytes 1769476
  194.4 5.6 copy-start.13
  194.4 6.1 copy-start.10
  273.5 5.6 copy-start.43
  273.5 5.6 copy-start.44
  273.5 5.6 copy-start.47
  273.5 7.8 copy-start.35
  273.6 7.8 copy-start.36
  281.0 4.0 copy-start.51
  281.4 8.2 copy-start.27
  287.8 76.4 %copy-start.37 = (f32[4,768]{1,0:T(4,128)}, f32[4,768]{1,0:T(4,128)S(1)}, u32[]{:S(2)}) copy-start(f32[4,768]{1,0:T(4,128)S(1)} %get-tuple-element.331) | copy-start | bytes 36868
  432.1 27.5 %copy-start.42 = (f32[16,768]{1,0:T(8,128)S(1)}, f32[16,768]{1,0:T(8,128)}, u32[]{:S(2)}) copy-start(f32[16,768]{1,0:T(8,128)} %get-tuple-element.132) | copy-start | bytes 147460
  432.1 27.5 %copy-start.50 = (f32[16]{0:T(128)S(1)}, f32[16]{0:T(128)}, u32[]{:S(2)}) copy-start(f32[16]{0:T(128)} %get-tuple-element.293) | copy-start | bytes 196
  432.1 27.6 %copy-start.30 = (f32[768,16]{0,1:T(8,128)S(1)}, f32[768,16]{0,1:T(8,128)}, u32[]{:S(2)}) copy-start(f32[768,16]{0,1:T(8,128)} %convolution_bitcast_fusion.3) | copy-start | bytes 147460
  432.1 28.2 %copy-start.34 = (f32[4,768]{1,0:T(4,128)S(1)}, f32[4,768]{1,0:T(4,128)}, u32[]{:S(2)}) copy-start(f32[4,768]{1,0:T(4,128)} %get-tuple-element.288) | copy-start | bytes 36868
  493.8 4.2 copy-start.28
  493.8 6.6 copy-start.40
  493.8 8.5 copy-start.41
  512.5 6.3 copy-start.3
  517.3 193.2 %all-gather.10.cloned.1.call-start = ((), (), s32[]{:S(2)}) async-start(), calls=%async_computation.7 | async-start | bytes 1216512 | tf_op jit(solution)/shard_map/all_gather | solution.py:554
  518.0 249.5 %all-gather.8.cloned.1.call-start = ((), (), s32[]{:S(2)}) async-start(), calls=%async_computation.6 | async-start | bytes 1216512 | tf_op jit(solution)/shard_map/all_gather | solution.py:554
  518.8 281.1 %reduce-scatter.4.cloned.1.call-start = ((), (), s32[]{:S(2)}) async-start(), calls=%async_computation.4 | async-start | bytes 442368 | tf_op jit(solution)/shard_map/reduce_scatter | solution.py:545
  521.2 3.7 copy-start.9
  571.8 108.1 %copy-start.15 = (bf16[128,768]{0,1:T(8,128)(2,1)S(1)}, bf16[128,768]{0,1:T(8,128)(2,1)}, u32[]{:S(2)}) copy-start(bf16[128,768]{0,1:T(8,128)(2,1)} %copy-done.14) | copy-start | bytes 589828
  571.8 351.3 %reduce-scatter.6.cloned.1.call-start = ((), (), s32[]{:S(2)}) async-start(), calls=%async_computation.5 | async-start | bytes 442368 | tf_op jit(solution)/shard_map/reduce_scatter | solution.py:582
  680.3 8.5 copy-start.4
  682.1 29.7 %copy-start.18 = (f32[1,192]{0,1:T(8,128)}, f32[1,192]{0,1:T(8,128)S(1)}, u32[]{:S(2)}) copy-start(f32[1,192]{0,1:T(8,128)S(1)} %copy.252) | copy-start | bytes 2308
  770.5 32.8 %copy-start.39 = (f32[128,96]{0,1:T(8,128)S(1)}, f32[128,96]{0,1:T(8,128)}, u32[]{:S(2)}) copy-start(f32[128,96]{0,1:T(8,128)} %get-tuple-element.349) | copy-start | bytes 147460
  770.5 32.9 %copy-start.17 = (bf16[2043,96]{1,0:T(8,128)(2,1)S(1)}, bf16[2043,96]{1,0:T(8,128)(2,1)}, u32[]{:S(2)}) copy-start(bf16[2043,96]{1,0:T(8,128)(2,1)} %copy-done.16) | copy-start | bytes 1176772
  911.7 6.1 copy-start.46
  911.7 9.9 copy-start.1
  971.2 7.9 copy-start.5
  971.2 7.9 copy-start.8
  971.2 7.9 copy-start.19
  971.2 7.9 copy-start.24
  971.2 7.9 copy-start.25
  977.4 3.5 copy-start.6
  977.4 3.5 copy-start.20
  977.4 3.5 copy-start.21
  (12 other events, 22.0 us)
Sparse Core Ops, SparseCore 0:
  78.3 66.6 all-reduce.10
  517.4 133.2 all-reduce.8
  654.8 55.6 all-gather.9
  714.3 53.1 all-gather.7
  770.3 29.6 reduce-scatter.3
  804.7 28.7 reduce-scatter.5

commit v3 on v2

--- a/solution.py
+++ b/solution.py
@@ -26,7 +26,8 @@
 C0=math.sqrt(2.0/math.pi); C1=0.044715
 
 def fwd_kernel(x_ref, mod_ref, bias_ref, wa_ref, w1_ref, w2_ref,
-               normed_ref, qkv_ref, lse_ref, mixed_ref, attn_ref, mid_ref, ntwo_ref, upper_ref, activ_ref, down_ref, out_ref):
+               normed_ref, qkv_ref, lse_ref, mixed_ref, attn_ref, mid_ref, ntwo_ref, upper_ref, activ_ref, down_ref, out_ref, hook=lambda p: None):
+    hook(0)
     x=x_ref[...]
     mod=lambda j: mod_ref[0, j:j+1, :]
     bias=lambda j: bias_ref[j:j+1, :]
@@ -38,6 +39,7 @@
     qkv_ref[:, 2*D:]=(mm(normed, wa_ref[2])+bias(1)).astype(bf)
     lo=half_masks()
     for hp in range(HEADS//2):
+        hook(1+hp)
         c=hp*128
         q=qkv_ref[:, c:c+128]; k=qkv_ref[:, D+c:D+c+128]; v=qkv_ref[:, 2*D+c:2*D+c+128]
         outs=[]
@@ -52,6 +54,7 @@
             lse_ref[:, 2*hp+h:2*hp+h+1]=m+jnp.log(l)
             outs.append(mm(p,v))
         mixed_ref[:, c:c+128]=jnp.where(lo, outs[0], outs[1]).astype(bf)
+    hook(7)
     attn=mm(mixed_ref[...], wa_ref[3])+bias(2)
     attn_ref[...]=attn
     mid=x+mod(2)*attn
@@ -61,6 +64,7 @@
     ntwo_ref[...]=ntwo
     down=jnp.broadcast_to(bias(13),(TOK,D))
     for j in range(4):
+        hook(8+j)
         up=mm(ntwo, w1_ref[j])+bias(3+j)
         upper_ref[:, j*D:(j+1)*D]=up
         t=jnp.tanh(C0*(up+C1*(up*up*up)))
@@ -183,60 +187,229 @@
         cost_estimate=pl.CostEstimate(flops=2*T*D*(3*D+5*TOK), bytes_accessed=25_000_000, transcendentals=T*TOK*HEADS),
     )(gmix,alow,gmid,mod,wa,qkv,lse,x)
 
-def gather_kernel(R, nz, U, w_ref, out_ref, zs, zr, xs, xr, cs, cr, ls):
-    rep=lax.axis_index("rep"); shard=lax.axis_index("shard")
-    z=shard//2; c=lax.rem(shard,2)
-    dev=lambda r,zz,cc: (r, 2*zz+cc)
-    MESH=pl.DeviceIdType.MESH
-    bar=pltpu.get_barrier_semaphore()
-    peers=[dev(rep, lax.rem(z+k,nz), c) for k in range(1,nz)]+[dev(jnp.bitwise_xor(rep,j), z, c) for j in range(1,R)]+[dev(rep,z,1-c)]
-    for p in peers: pl.semaphore_signal(bar, inc=1, device_id=p, device_id_type=MESH)
-    pl.semaphore_wait(bar, len(peers))
-    def zcopy(u,k):
-        return pltpu.make_async_remote_copy(src_ref=w_ref.at[u,rep], dst_ref=out_ref.at[u,rep,z,c], send_sem=zs.at[u,k-1], recv_sem=zr.at[u,k-1],
-            device_id=dev(rep,lax.rem(z+k,nz),c), device_id_type=MESH)
-    def xcopy(u,j,k):
-        o=lax.rem(z-k+nz,nz)
-        return pltpu.make_async_remote_copy(src_ref=out_ref.at[u,rep,o,c], dst_ref=out_ref.at[u,rep,o,c], send_sem=xs.at[u,j-1,k-1], recv_sem=xr.at[u,j-1,k-1],
-            device_id=dev(jnp.bitwise_xor(rep,j),z,c), device_id_type=MESH)
-    def ccopy(u,j):
-        r=jnp.bitwise_xor(rep,j)
-        return pltpu.make_async_remote_copy(src_ref=out_ref.at[u,r,:,c], dst_ref=out_ref.at[u,r,:,c], send_sem=cs.at[u,j], recv_sem=cr.at[u,j],
-            device_id=dev(rep,z,1-c), device_id_type=MESH)
-    locs=[pltpu.make_async_copy(w_ref.at[u], out_ref.at[u,:,z,c], ls.at[u]) for u in range(U)]
-    for u in range(U):
-        for k in range(1,nz): zcopy(u,k).start()
-    for u in range(U): locs[u].start()
-    for u in range(U):
-        for k in range(1,nz):
-            zcopy(u,k).wait_recv()
-            for j in range(1,R): xcopy(u,j,k).start()
-        locs[u].wait()
-        ccopy(u,0).start()
-    for u in range(U):
-        for j in range(1,R):
-            for k in range(1,nz): xcopy(u,j,k).wait_recv()
-            ccopy(u,j).start()
-    for u in range(U):
-        for j in range(R): ccopy(u,j).wait()
-        for k in range(1,nz): zcopy(u,k).wait_send()
-        for j in range(1,R):
-            for k in range(1,nz): xcopy(u,j,k).wait_send()
-
-def gather_layer(w, R, S, cid):
-    U,_,rows_,W=w.shape
-    nz=S//2
+MESH=pl.DeviceIdType.MESH
+class Gather:
+    def __init__(self,R,nz,U,w_ref,out_ref,zs,zr,xs,xr,cs,cr,ls):
+        self.R,self.nz,self.U=R,nz,U
+        self.w,self.out=w_ref,out_ref
+        self.zs,self.zr,self.xs,self.xr,self.cs,self.cr,self.ls=zs,zr,xs,xr,cs,cr,ls
+        self.rep=lax.axis_index("rep"); self.shard=lax.axis_index("shard")
+        self.z=self.shard//2; self.c=lax.rem(self.shard,2)
+        self.relay=R==4
+    def at(self,m,z,other=False): return (jnp.bitwise_xor(self.rep,m), 2*z+(1-self.c if other else self.c))
+    def peers(self):
+        return [self.at(0,lax.rem(self.z+k,self.nz)) for k in range(1,self.nz)]+[self.at(m,self.z) for m in range(1,self.R)]+[self.at(0,self.z,True)]
+    def copy(self,src,dst,s,r,dev): return pltpu.make_async_remote_copy(src_ref=src,dst_ref=dst,send_sem=s,recv_sem=r,device_id=dev,device_id_type=MESH)
+    def along(self,u,o,up):
+        b=self.out.at[u,self.rep,o,self.c]
+        return self.copy(b,b,self.zs.at[u,o,1 if up else 0],self.zr.at[u,o],self.at(0,self.z+(1 if up else -1)))
+    def own(self,u,up):
+        return self.copy(self.w.at[u,self.rep],self.out.at[u,self.rep,self.z,self.c],self.zs.at[u,self.z,1 if up else 0],self.zr.at[u,self.z],self.at(0,self.z+(1 if up else -1)))
+    def across(self,u,o,m,q,to):
+        b=self.out.at[u,jnp.bitwise_xor(self.rep,q),o,self.c]
+        return self.copy(b,b,self.xs.at[u,m-1,o],self.xr.at[u,m-1,o],self.at(to,self.z))
+    def swap(self,u,m):
+        b=self.out.at[u,jnp.bitwise_xor(self.rep,m),:,self.c]
+        return self.copy(b,b,self.cs.at[u,m],self.cr.at[u,m],self.at(0,self.z,True))
+    def local(self,u): return pltpu.make_async_copy(self.w.at[u],self.out.at[u,:,self.z,self.c],self.ls.at[u])
+    def start(self):
+        for u in range(self.U):
+            @pl.when(self.z<self.nz-1)
+            def _(): self.own(u,True).start()
+            @pl.when(self.z>0)
+            def _(): self.own(u,False).start()
+        for u in range(self.U): self.local(u).start()
+    def sides(self,h):
+        z,nz=self.z,self.nz
+        return ((z>=h,z-h,True,z<nz-1),(z+h<nz,z+h,False,z>0))
+    def arrive(self,h,u):
+        for there,o,up,more in self.sides(h):
+            @pl.when(there)
+            def _():
+                self.along(u,o,up).wait_recv()
+                @pl.when(more)
+                def _(): self.along(u,o,up).start()
+                for m in range(1,self.R):
+                    if not (self.relay and m==3): self.across(u,o,m,0,m).start()
+    def pass_on(self,h,u):
+        if not self.relay: return
+        for there,o,up,more in self.sides(h):
+            for par,(q,to) in enumerate(((1,2),(2,1))):
+                @pl.when(jnp.logical_and(there,lax.rem(u+o+self.nz,2)==par))
+                def _():
+                    self.across(u,o,q,0,q).wait_recv()
+                    self.across(u,o,3,q,to).start()
+    def swap_own(self,u):
+        self.local(u).wait(); self.swap(u,0).start()
+    def swap_block(self,u,m):
+        for o in range(self.nz):
+            seen=self.relay and m<3
+            cond=o!=self.z
+            if seen: cond=jnp.logical_and(cond,(u+o+self.nz)%2!=m-1)
+            if seen and (u+o+self.nz)%2==m-1: continue
+            @pl.when(o!=self.z)
+            def _(): self.across(u,o,m,0,m).wait_recv()
+        self.swap(u,m).start()
+    def ticks(self):
+        U,nz=self.U,self.nz
+        order=[(h,u) for h in range(1,nz) for u in range(U)]
+        out=[]
+        for i in range(len(order)+U):
+            if i<len(order): out.append(functools.partial(self.arrive,*order[i]))
+            if i>=U: out.append(functools.partial(self.pass_on,*order[i-U]))
+            if i>=len(order): out.append(functools.partial(self.swap_own,i-len(order)))
+        for u in range(U):
+            for m in range(1,self.R): out.append(functools.partial(self.swap_block,u,m))
+        return out
+    def finish(self):
+        for u in range(self.U):
+            for m in range(self.R): self.swap(u,m).wait()
+            @pl.when(self.z<self.nz-1)
+            def _(): self.own(u,True).wait_send()
+            @pl.when(self.z>0)
+            def _(): self.own(u,False).wait_send()
+            for h in range(1,self.nz):
+                for there,o,up,more in self.sides(h):
+                    @pl.when(there)
+                    def _():
+                        @pl.when(more)
+                        def _(): self.along(u,o,up).wait_send()
+                        for m in range(1,self.R): self.across(u,o,m,0,m).wait_send()
+def gather_sems(R,nz,U):
     dma=pltpu.SemaphoreType.DMA
-    any_=pl.BlockSpec(memory_space=pl.ANY)
-    out=pl.pallas_call(functools.partial(gather_kernel,R,nz,U),
-        in_specs=[any_], out_specs=any_, out_shape=jax.ShapeDtypeStruct((U,R,nz,2,rows_,W),bf),
-        scratch_shapes=[dma((U,nz-1)),dma((U,nz-1)),dma((U,R-1,nz-1)),dma((U,R-1,nz-1)),dma((U,R)),dma((U,R)),dma((U,))],
-        compiler_params=pltpu.CompilerParams(collective_id=cid, has_side_effects=True, vmem_limit_bytes=4*1024*1024),
-    )(w)
+    return [dma((U,nz,2)),dma((U,nz)),dma((U,R-1,nz)),dma((U,R-1,nz)),dma((U,R)),dma((U,R)),dma((U,))]
+def unit_blocks(out,R):
+    U=out.shape[0]; W=out.shape[-1]
     out=out.reshape(U,R,D,W)
     if R==4: return [out[u] for u in range(U)]
     m=R//4
     return [out[u].reshape(4,m,D,W).transpose(0,2,1,3).reshape(4,D,D) for u in range(U)]
+def meet(peers):
+    bar=pltpu.get_barrier_semaphore()
+    for p in peers: pl.semaphore_signal(bar,inc=1,device_id=p,device_id_type=MESH)
+    pl.semaphore_wait(bar,len(peers))
+
+def first_kernel(R,nz,U,own, w_ref,fo_ref,sm_ref,t1_ref,t2_ref,cls_ref,tb_ref,ada_ref,fin_ref,finb_ref,
+                 out_ref,f_ref,sg_ref,hid_ref,act_ref,con_ref,call_ref,mod_ref,fm_ref,
+                 cgs,pm,mr,ps,zrv,fps, fs1,fr1,fs2,fr2,ss,sr,as_,ar,cs_,cr_,ms,mrs,pz,pzr,vs,vr, *gsems):
+    S=2*nz; NP=S*R*8
+    ga=Gather(R,nz,U,w_ref,out_ref,*gsems)
+    rep=lax.axis_index("rep"); shard=lax.axis_index("shard"); z=shard//2; c=lax.rem(shard,2)
+    rpeer=lambda m: (jnp.bitwise_xor(rep,m),shard)
+    speer=lambda k: (rep,lax.rem(shard+k,S))
+    mate=(rep,2*z+1-c)
+    peers=[rpeer(m) for m in range(1,R)]+[speer(k) for k in range(1,S)]
+    def send(src,dst,s,r,dev): return pltpu.make_async_remote_copy(src_ref=src,dst_ref=dst,send_sem=s,recv_sem=r,device_id=dev,device_id_type=MESH)
+    meet(peers)
+    f1=lambda m: send(fo_ref,f_ref.at[shard,rep],fs1.at[m-1],fr1.at[m-1],rpeer(m))
+    for m in range(1,R): f1(m).start()
+    smc=lambda k: send(sm_ref,sg_ref.at[shard],ss.at[k-1],sr.at[k-1],speer(k))
+    ga.start(); ticks=ga.ticks()
+    f_ref[shard,rep]=fo_ref[...]
+    sg_ref[shard]=sm_ref[...]
+    for m in range(1,R): f1(m).wait_recv()
+    f2=lambda k: send(f_ref.at[shard],f_ref.at[shard],fs2.at[k-1],fr2.at[k-1],speer(k))
+    for k in range(1,S): f2(k).start()
+    for k in range(1,S): smc(k).start()
+    for t in ticks[:U]: t()
+    for k in range(1,S): f2(k).wait_recv()
+    feats=f_ref[...].reshape(NP,384)
+    hidden=mm_nt(feats[:,:256].astype(bf),t1_ref[...])+tb_ref[0:1,:]
+    hid_ref[...]=hidden
+    act_ref[shard]=(hidden/(1.0+jnp.exp(-hidden))).astype(bf)
+    ac=lambda k: send(act_ref.at[shard],act_ref.at[shard],as_.at[k-1],ar.at[k-1],speer(k))
+    for k in range(1,S): ac(k).start()
+    hot=(feats[:,256:257].astype(jnp.int32)==lax.broadcasted_iota(jnp.int32,(1,cls_ref.shape[1]),1))
+    con=mm_nt(jnp.where(hot,1.0,0.0).astype(bf),cls_ref[...])
+    for t in ticks[U:2*U]: t()
+    for k in range(1,S): ac(k).wait_recv()
+    sec=mm_nt(act_ref[0],t2_ref[0])
+    for s in range(1,S): sec=sec+mm_nt(act_ref[s],t2_ref[s])
+    con=(sec+tb_ref[1:2,:])+con
+    con_ref[...]=con
+    cond=con/(1.0+jnp.exp(-con))
+    call_ref[shard]=cond.astype(bf)
+    cc=lambda k: send(call_ref.at[shard],call_ref.at[shard],cs_.at[k-1],cr_.at[k-1],speer(k))
+    for k in range(1,S): cc(k).start()
+    cgs[...]=cond.reshape(S,R,8,own)
+    cg=cgs[:,rep].reshape(S*8,own).astype(bf)
+    first=lax.rem(lax.broadcasted_iota(jnp.int32,(S*8,1),0),8)<4
+    for b in range(6):
+        sl=slice(b*D,(b+1)*D)
+        v=jnp.where(first,mm(cg,ada_ref[0,:,sl]),mm(cg,ada_ref[1,:,sl]))
+        pm[:,:,:,sl]=v.reshape(nz,2,8,D)
+    mc=send(pm.at[:,1-c],mr,ms,mrs,mate)
+    mc.start()
+    for t in ticks[2*U:4*U]: t()
+    mc.wait_recv()
+    ps[...]=pm[:,c]+mr[...]
+    zc=lambda k: send(ps.at[lax.rem(z+k,nz)],zrv.at[k-1],pz.at[k-1],pzr.at[k-1],(rep,2*lax.rem(z+k,nz)+c))
+    for k in range(1,nz): zc(k).start()
+    for k in range(1,S): cc(k).wait_recv()
+    fp=mm(call_ref[0],fin_ref[0])
+    for s in range(1,S): fp=fp+mm(call_ref[s],fin_ref[s])
+    fps[...]=(fp+finb_ref[0:1,:]).reshape(S,R,8,fin_ref.shape[2])
+    vc=lambda k: send(fps.at[lax.rem(shard+k,S),rep],fm_ref.at[shard],vs.at[k-1],vr.at[k-1],speer(k))
+    for k in range(1,S): vc(k).start()
+    fm_ref[shard]=fps[shard,rep]
+    for t in ticks[4*U:]: t()
+    total=ps[z]
+    for k in range(1,nz): zc(k).wait_recv(); total=total+zrv[k-1]
+    mod_ref[...]=total
+    for k in range(1,S): vc(k).wait_recv(); smc(k).wait_recv()
+    for m in range(1,R): f1(m).wait_send()
+    for k in range(1,S):
+        for cp in (f2,smc,ac,cc,vc): cp(k).wait_send()
+    mc.wait_send()
+    for k in range(1,nz): zc(k).wait_send()
+    ga.finish()
+
+def first_call(w,fo,sm,t1,t2,cls,tb,ada,fin,finb,R,S,cid):
+    U,_,own,W=w.shape; nz=S//2; NP=S*R*8; FC=fin.shape[2]
+    dma=pltpu.SemaphoreType.DMA; V=pltpu.VMEM; sd=jax.ShapeDtypeStruct
+    any_=pl.BlockSpec(memory_space=pl.ANY); vm=pl.BlockSpec(memory_space=pltpu.VMEM)
+    return pl.pallas_call(functools.partial(first_kernel,R,nz,U,own),
+        in_specs=[vm]*10, out_specs=[any_]+[vm]*8,
+        out_shape=[sd((U,R,nz,2,own,W),bf),sd((S,R,8,384),f32),sd((S,)+sm.shape,bf),sd((NP,own),f32),sd((S,NP,own),bf),sd((NP,own),f32),sd((S,NP,own),bf),sd((8,6*D),f32),sd((S,8,FC),f32)],
+        scratch_shapes=[V((S,R,8,own),f32),V((nz,2,8,6*D),f32),V((nz,8,6*D),f32),V((nz,8,6*D),f32),V((max(nz-1,1),8,6*D),f32),V((S,R,8,FC),f32),
+            dma((R-1,)),dma((R-1,))]+[dma((S-1,))]*8+[dma(()),dma(()),dma((nz-1,)),dma((nz-1,)),dma((S-1,)),dma((S-1,))]+gather_sems(R,nz,U),
+        compiler_params=pltpu.CompilerParams(collective_id=cid,has_side_effects=True,vmem_limit_bytes=VLIM),
+    )(w,fo,sm,t1,t2,cls,tb,ada,fin,finb)
+
+def fwd_gather_kernel(R,nz,U,x_ref,mod_ref,bias_ref,wa_ref,w1_ref,w2_ref,w_ref,*rest):
+    outs=rest[:11]; out_ref=rest[11]; gsems=rest[12:]
+    i=pl.program_id(0); last=pl.num_programs(0)-1
+    ga=Gather(R,nz,U,w_ref,out_ref,*gsems)
+    @pl.when(i==0)
+    def _():
+        meet(ga.peers()); ga.start()
+    ticks=ga.ticks(); used=set()
+    def hook(p):
+        for step in range(4):
+            n=12*step+p-6
+            if n>=0 and n%2==0 and n//2<len(ticks):
+                used.add(n//2)
+                pl.when(i==step)(ticks[n//2])
+    fwd_kernel(x_ref,mod_ref,bias_ref,wa_ref,w1_ref,w2_ref,*outs,hook=hook)
+    @pl.when(i==last)
+    def _():
+        for n,t in enumerate(ticks):
+            if n not in used: t()
+        ga.finish()
+FWD_WIDTHS=[(D,bf),(3*D,bf),(128,f32),(D,bf),(D,f32),(D,f32),(D,bf),(FF,f32),(FF,bf),(D,f32),(D,f32)]
+def layer_fwd_gather(x,mod,bias,wa,w1,w2,w,R,S,cid):
+    T=x.shape[0]; n=T//TOK; U,_,own,W=w.shape; nz=S//2
+    sd=jax.ShapeDtypeStruct
+    any_=pl.BlockSpec(memory_space=pl.ANY)
+    o=pl.pallas_call(functools.partial(fwd_gather_kernel,R,nz,U),grid=(n,),
+        in_specs=[rows(D),pl.BlockSpec((1,8,D),lambda i:(i,0,0)),full((16,D)),full((4,D,D)),full((4,D,D)),full((4,D,D)),pl.BlockSpec(memory_space=pltpu.VMEM)],
+        out_specs=[rows(v) for v,_ in FWD_WIDTHS]+[any_],
+        out_shape=[sd((T,v),t) for v,t in FWD_WIDTHS]+[sd((U,R,nz,2,own,W),bf)],
+        scratch_shapes=gather_sems(R,nz,U),
+        compiler_params=pltpu.CompilerParams(collective_id=cid,has_side_effects=True,vmem_limit_bytes=VLIM),
+        cost_estimate=pl.CostEstimate(flops=2*T*(9216*D+2*TOK*D),bytes_accessed=60_000_000,transcendentals=T*FF*2),
+    )(x,mod,bias,wa,w1,w2,w)
+    return o[:11],o[11]
 CW=384; NCH=8
 def bit_orders(R):
     bits=[1<<i for i in range(R.bit_length()-1)]
@@ -430,17 +603,17 @@
 def outer_adam_kernel(f_ref,g0_ref,g1_ref,b_ref,w_ref,m_ref,v_ref,*outs):
     factor=f_ref[0]; l=pl.program_id(0); j=pl.program_id(1)
     def put(sl,g):
-        for o,val in zip(outs,adam_update(w_ref[0,sl],g,m_ref[0,sl],v_ref[0,sl],factor)): o[0,sl]=val
+        for o,val in zip(outs,adam_update(w_ref[0,:,sl],g,m_ref[0,:,sl],v_ref[0,:,sl],factor)): o[0,:,sl]=val
     for a in range(2):
         sl=slice(a*CW,(a+1)*CW)
         for layer,ref in enumerate((g0_ref,g1_ref)):
             @pl.when(jnp.logical_and(j<4,l==layer))
-            def _(): put(sl,ref[0,a].T)
+            def _(): put(sl,ref[0,a])
     @pl.when(j==4)
-    def _(): put(slice(0,16),b_ref[0])
+    def _(): put(slice(0,128),b_ref[0])
 def outer_adam(factor,g0,g1,b,w,m,v):
-    own=w.shape[2]; W=2*CW
-    blk=pl.BlockSpec((1,W,own),lambda l,j:(l,j,0))
+    own=w.shape[1]; W=2*CW
+    blk=pl.BlockSpec((1,own,W),lambda l,j:(l,0,j))
     def gmap(layer):
         def index(l,j):
             jj=jnp.minimum(j,3); on=jnp.where(l==layer,jj,3*(l>layer))
@@ -448,7 +621,7 @@
         return pl.BlockSpec((1,2,own,CW),index)
     sd=jax.ShapeDtypeStruct
     return pl.pallas_call(outer_adam_kernel,grid=(LAYERS,5),
-        in_specs=[pl.BlockSpec(memory_space=pltpu.SMEM),gmap(0),gmap(1),pl.BlockSpec((1,16,own),lambda l,j:(l,0,0)),blk,blk,blk],
+        in_specs=[pl.BlockSpec(memory_space=pltpu.SMEM),gmap(0),gmap(1),pl.BlockSpec((1,own,128),lambda l,j:(l,0,0)),blk,blk,blk],
         out_specs=[blk]*4,out_shape=[sd(w.shape,f32)]*3+[sd(w.shape,bf)],
         compiler_params=pltpu.CompilerParams(vmem_limit_bytes=VLIM))(factor,g0,g1,b,w,m,v)
 P_SIZE=16; GRID=16; LAYERS=2; LAT_DEV=4; FREQ=256; NCLASS=1000
@@ -480,38 +653,42 @@
     rep=lax.axis_index("rep"); shard=lax.axis_index("shard")
     own=D//S; W=4*D//R; N=LAT_DEV*R*S; G=LAT_DEV*S
     count=N*TOK*P_SIZE
-    inner_low=inner_weights.astype(bf); outer_low=outer_weights.astype(bf)
-    gathered=[]
-    for l in range(LAYERS):
-        slab=jnp.stack([inner_low[l,:,:4*D],inner_low[l,:,4*D:8*D],outer_low[l,:FF].T])
-        slab=slab.reshape(3,own,R,W).transpose(0,2,1,3)
-        gathered.append(gather_layer(slab,R,S,l))
-    embed_low=embed_table.astype(bf); final_low=final_mod.astype(bf); head_low=head_weights.astype(bf)
-    small=jnp.concatenate([outer_low[:,FF:].reshape(LAYERS*BIAS,own),embed_low[:P_SIZE+1]],axis=0)
-    small=lax.all_gather(small,"shard",axis=1,tiled=True)
+    inner_low=inner_weights.astype(bf)
+    outer_turn=lambda a: a.transpose(0,2,1)
+    outer_low=outer_turn(outer_weights).astype(bf)
+    def slab(l):
+        s=jnp.stack([inner_low[l,:,:4*D],inner_low[l,:,4*D:8*D],outer_low[l,:,:FF]])
+        return s.reshape(3,own,R,W).transpose(0,2,1,3)
+    embed_low=embed_table.T.astype(bf); final_low=final_mod.astype(bf); head_low=head_weights.astype(bf)
+    r1=P_SIZE+1; r2=P_SIZE+2+FREQ; r3=P_SIZE+3+FREQ+D
+    fin_cols=2*D//S
+    small=jnp.concatenate([outer_low[0,:,FF:],outer_low[1,:,FF:],embed_low[:,:P_SIZE+1]],axis=1).T
+    small=jnp.pad(small,((0,48-small.shape[0]),(0,0)))
+    mine_rows=jnp.concatenate([time_features(time_steps,FREQ).astype(bf).astype(f32),labels.astype(f32)[:,None],jnp.zeros((LAT_DEV,127),f32)],axis=1)
+    mine_rows=jnp.concatenate([mine_rows,mine_rows],axis=0)
+    second_w=embed_low[:,r2:r2+D]
+    table=jnp.pad(embed_low[:,r3:],((0,0),(0,1024-NCLASS)))
+    biases2=jnp.pad(jnp.stack([embed_low[:,r1+FREQ],embed_low[:,r2+D]]).astype(f32),((0,6),(0,0)))
+    ada_own=inner_low[:,:,4*D+FF:]
+    fin_bias=jnp.pad(final_low[D:].astype(f32),((0,7),(0,0)))
+    first=first_call(slab(0),mine_rows,small,embed_low[:,r1:r1+FREQ],second_w.reshape(own,S,own).transpose(1,0,2),table,biases2,ada_own,final_low[:D].reshape(S,own,fin_cols),fin_bias,R,S,0)
+    gather0,rows_all,small,hidden,time_act,condition,cond_all,modul,fin_mod=first
+    def latent_order(a):
+        a=a.reshape(a.shape[:-2]+(S,R,8,a.shape[-1]))[...,:LAT_DEV,:]
+        return jnp.swapaxes(a,-4,-3).reshape(a.shape[:-4]+(N,a.shape[-1]))
+    rows_all=latent_order(rows_all.reshape(S*R*8,384))
+    features=rows_all[:,:FREQ].astype(bf)
+    hot=rows_all[:,FREQ:FREQ+1]==jnp.arange(NCLASS,dtype=jnp.int32).astype(f32)[None,:]
+    hidden=latent_order(hidden); condition=latent_order(condition)
+    wide=lambda a: latent_order(a).transpose(1,0,2).reshape(N,D)
+    time_act=wide(time_act); cond_all=wide(cond_all)
+    cond_own=lax.dynamic_slice_in_dim(cond_all,shard*own,own,1)
+    small=small.transpose(1,0,2).reshape(48,D)
     biases=small[:LAYERS*BIAS].reshape(LAYERS,BIAS,D).astype(f32)
     patch_w=small[LAYERS*BIAS:LAYERS*BIAS+P_SIZE]; patch_b=small[LAYERS*BIAS+P_SIZE].astype(f32)
-    ids=lax.all_gather(jnp.stack([time_steps,labels],axis=1),ALL,axis=0,tiled=True)
-    steps_all=ids[:,0]; labels_all=ids[:,1]
-    r1=P_SIZE+1; r2=P_SIZE+2+FREQ; r3=P_SIZE+3+FREQ+D
-    features=time_features(steps_all,FREQ).astype(bf)
-    hidden=dot32("nf,fd->nd",features,embed_low[r1:r1+FREQ])+embed_low[r1+FREQ].astype(f32)
-    act_own=jax.nn.silu(hidden).astype(bf)
-    time_act=lax.all_gather(act_own,"shard",axis=1,tiled=True)
-    hot=labels_all[:,None]==jnp.arange(NCLASS,dtype=jnp.int32)[None,:]
-    condition=dot32("nd,de->ne",time_act,embed_low[r2:r2+D])+embed_low[r2+D].astype(f32)+dot32("nc,ce->ne",hot.astype(bf),embed_low[r3:])
-    cond_own=jax.nn.silu(condition).astype(bf)
-    cond_all=lax.all_gather(cond_own,"shard",axis=1,tiled=True)
-    cond_group=lax.dynamic_slice_in_dim(cond_own,rep*G,G,0)
-    ada_own=inner_low[:,:,4*D+FF:]
-    part=dot32("gd,lde->gle",cond_group,ada_own)
-    modul=lax.psum_scatter(part,"shard",scatter_dimension=0,tiled=True)
-    modul=modul.reshape(LAT_DEV,LAYERS,6,D)+biases[:,7:13].reshape(1,LAYERS,6,D)
-    modul=jnp.pad(modul.transpose(1,0,2,3),((0,0),(0,0),(0,2),(0,0)))
-    fin_cols=2*D//S
-    fin_part=dot32("gd,de->ge",lax.dynamic_slice_in_dim(cond_all,rep*G,G,0),final_low[:D])+final_low[D].astype(f32)
-    fin_mod=lax.all_to_all(fin_part.reshape(S,LAT_DEV,fin_cols),"shard",0,0,tiled=True)
-    fin_mod=fin_mod.reshape(S,LAT_DEV,fin_cols).transpose(1,0,2).reshape(LAT_DEV,2*D)
+    modul=modul.reshape(LAYERS,LAT_DEV,6,D)+biases[:,None,7:13]
+    modul=jnp.pad(modul,((0,0),(0,0),(0,2),(0,0)))
+    fin_mod=fin_mod[:,:LAT_DEV].transpose(1,0,2).reshape(LAT_DEV,2*D)
     ramp=0.0001+(0.02-0.0001)*jnp.arange(1000,dtype=f32)/999.0
     upto=jnp.arange(1000,dtype=jnp.int32)[None,:]<=time_steps[:,None]
     abar=jnp.exp(jnp.sum(jnp.where(upto,jnp.log(1.0-ramp)[None,:],0.0),axis=1))
@@ -519,10 +696,14 @@
     stream=dot32("gpt,pd->gtd",patches,patch_w)+patch_b+position_table(GRID,D)[None]
     stream=stream.reshape(LAT_DEV*TOK,D)
     saved=[]
+    gathered=[unit_blocks(gather0,R)]
     for l in range(LAYERS):
         wa,w1,w2=gathered[l]
         bias=jnp.pad(biases[l],((0,2),(0,0)))
-        o=layer_fwd(stream,modul[l],bias,wa,w1,w2)
+        if l==0:
+            o,gather1=layer_fwd_gather(stream,modul[l],bias,wa,w1,w2,slab(1),R,S,1)
+            gathered.append(unit_blocks(gather1,R))
+        else: o=layer_fwd(stream,modul[l],bias,wa,w1,w2)
         saved.append((stream,)+tuple(o))
         stream=o[-1]
     stream3=stream.reshape(LAT_DEV,TOK,D)
@@ -539,11 +720,7 @@
     grad_stream,g_shift,g_scale=jax.vjp(modulate,stream3,fin_shift,fin_scale)[1](grad_fin_normed)
     grad_stream=grad_stream.reshape(LAT_DEV*TOK,D)
     grad_fin=jnp.concatenate([g_shift,g_scale],axis=1)
-    fin_rows=lax.all_gather(grad_fin.astype(bf),ALL,axis=0,tiled=True)
-    fin_mine=lax.dynamic_slice_in_dim(fin_rows,shard*fin_cols,fin_cols,1)
-    final_main=dot32("nd,ne->de",cond_all,fin_mine)
-    grad_cond=lax.psum_scatter(dot32("ne,de->nd",fin_mine,final_low[:D]),"shard",scatter_dimension=1,tiled=True)
-    ada_parts=[None]*LAYERS; bias_grads=[None]*LAYERS; operands=[None]*LAYERS
+    ada_parts=[None]*LAYERS; bias_grads=[None]*LAYERS; operands=[None]*LAYERS; gathered_rows=[None]*LAYERS
     for l in range(LAYERS-1,-1,-1):
         wa,w1,w2=gathered[l]
         x,normed,qkv,lse,mixed,attn,mid,ntwo,upper,activ,down,_=saved[l]
@@ -551,37 +728,47 @@
         low,grad_stream,dm2,db2=layer_bwd_attn(gmix,alow,gmid,modul[l],wa,qkv,lse,x)
         operands[l]=((dlow,ntwo,normed,mixed),(activ,ulow,low))
         dmod=jnp.concatenate([dm2[:,:2],dm1[:,2:6]],axis=1)
-        rows_all=lax.all_gather(dmod.astype(bf).reshape(LAT_DEV,6*D),ALL,axis=0,tiled=True)
-        ada_parts[l]=dot32("nd,ne->de",cond_own,rows_all)
-        grad_cond=grad_cond+dot32("ne,de->nd",rows_all,ada_own[l])
+        mod_rows=dmod.astype(bf).reshape(LAT_DEV,6*D)
+        if l==LAYERS-1: mod_rows=jnp.concatenate([mod_rows,grad_fin.astype(bf)],axis=1)
+        mod_rows=lax.all_gather(mod_rows,ALL,axis=0,tiled=True)
+        gathered_rows[l]=mod_rows
         bias_grads[l]=jnp.concatenate([db2[0:2],db1[2:7],jnp.sum(dmod,axis=0),db1[13:14]],axis=0)
-    ops1,grad_stream=lax.optimization_barrier((operands[1],grad_stream))
+    ops1,late=lax.optimization_barrier((operands[1],gathered_rows[1]))
+    fin_mine=lax.dynamic_slice_in_dim(late,6*D+shard*fin_cols,fin_cols,1)
+    final_main=dot32("nd,ne->de",cond_all,fin_mine)
+    fin_part=dot32("ne,de->nd",fin_mine,final_low[:D])
+    fin_part,ops1=lax.optimization_barrier((fin_part,ops1))
+    grad_cond=lax.psum_scatter(fin_part,"shard",scatter_dimension=1,tiled=True)
     grads1=layer_grads(R,S,LAYERS+1,*ops1)
+    grads1,grad_cond,early=lax.optimization_barrier((grads1,grad_cond,gathered_rows[0]))
+    for l,mod_rows in ((0,early),(1,late[:,:6*D])):
+        ada_parts[l]=dot32("nd,ne->de",cond_own,mod_rows)
+        grad_cond=grad_cond+dot32("ne,de->nd",mod_rows,ada_own[l])
     gs=grad_stream.reshape(LAT_DEV,TOK,D)
     patch_grad=dot32("gpt,gtd->pd",patches,gs.astype(bf))
     patch_bias=jnp.sum(grad_stream,axis=0)
-    fin_bias=jnp.sum(grad_fin,axis=0).reshape(2,D)
+    fin_bias_sum=jnp.sum(grad_fin,axis=0).reshape(2,D)
     tail=jnp.zeros((1,D),f32).at[0,0].set(loss_part)
     head_flat=head_grad.reshape(-1)
     head_rows=-(-head_flat.shape[0]//D)
     head_flat=jnp.pad(head_flat,(0,head_rows*D-head_flat.shape[0])).reshape(head_rows,D)
-    sums=lax.psum(jnp.concatenate(bias_grads+[patch_grad,patch_bias[None],fin_bias,head_flat,tail],axis=0),ALL)
+    local_sums=(jnp.concatenate(bias_grads+[patch_grad,patch_bias[None],fin_bias_sum,head_flat,tail],axis=0))
+    grad_condition=silu_back(condition,grad_cond)
+    b2=jnp.sum(grad_condition,axis=0)
+    clow=grad_condition.astype(bf)
+    second=dot32("nd,ne->de",time_act,clow)
+    class_grad=jnp.einsum("nc,nd->cd",hot.astype(f32),grad_condition,precision=lax.Precision.HIGHEST)
+    time_part=dot32("ne,ed->nd",clow,second_w)
+    time_part,ops0,local_sums=lax.optimization_barrier((time_part,operands[0],local_sums))
+    sums=lax.psum(local_sums,ALL)
+    grad_time_act=lax.psum_scatter(time_part,"shard",scatter_dimension=1,tiled=True)
+    grads0=layer_grads(R,S,LAYERS,*ops0)
+    grads0,grad_time_act,sums=lax.optimization_barrier((grads0,grad_time_act,sums))
     o1=LAYERS*BIAS; o2=o1+P_SIZE+1; o3=o2+2; o4=o3+head_rows
     mean_loss=sums[o4,0]
     head_total=sums[o3:o4].reshape(-1)[:(D+1)*P_SIZE].reshape(D+1,P_SIZE)
     fin_bias_own=lax.dynamic_slice_in_dim(sums[o2:o3].reshape(2*D),shard*fin_cols,fin_cols,0)
     mine=lax.dynamic_slice_in_dim(sums[:o2],shard*own,own,1)
-    grad_cond,grads1=lax.optimization_barrier((grad_cond,grads1))
-    grad_condition=silu_back(condition,grad_cond)
-    b2=jnp.sum(grad_condition,axis=0)
-    clow=grad_condition.astype(bf)
-    second=dot32("nd,ne->de",time_act,clow)
-    class_grad=jnp.einsum("nc,nd->cd",hot.astype(f32),grad_condition,precision=lax.Precision.HIGHEST)
-    time_part=dot32("ne,de->nd",clow,embed_low[r2:r2+D])
-    time_part,ops0=lax.optimization_barrier((time_part,operands[0]))
-    grad_time_act=lax.psum_scatter(time_part,"shard",scatter_dimension=1,tiled=True)
-    grads0=layer_grads(R,S,LAYERS,*ops0)
-    grads0,grad_time_act=lax.optimization_barrier((grads0,grad_time_act))
     grad_time=silu_back(hidden,grad_time_act)
     first=dot32("nf,nd->fd",features,grad_time.astype(bf))
     embed_grad=jnp.concatenate([mine[o1:o2],first,jnp.sum(grad_time,axis=0)[None],second,b2[None],class_grad],axis=0)
@@ -594,7 +781,8 @@
     factor=jnp.minimum(1.0,clip_coef*math.sqrt(D/count)/grad_norm)
     out=[mean_loss,grad_norm]
     out.extend(inner_adam(factor.reshape(1),grads0,grads1,ada_grad,inner_weights,inner_moment,inner_square))
-    out.extend(outer_adam(factor.reshape(1),grads0,grads1,bias_grad,outer_weights,outer_moment,outer_square))
+    bias_turn=jnp.pad(bias_grad.transpose(0,2,1),((0,0),(0,0),(0,112)))
+    out.extend(outer_turn(a) for a in outer_adam(factor.reshape(1),grads0,grads1,bias_turn,outer_turn(outer_weights),outer_turn(outer_moment),outer_turn(outer_square)))
     for w,g,m,v in ((embed_table,embed_grad,embed_moment,embed_square),(final_mod,final_grad,final_moment,final_square),
                     (head_weights,head_total,head_moment,head_square)):
         out.extend(adam_update(w,g,m,v,factor))

time: 1030 us -> 919 us (0.89)
  blocking collectives: 145 us -> 14.4 us
  local copies, waits for them, and re-layouts: 79.2 us -> 112 us
  Pallas kernels: 594 us -> 573 us
    all_gather x5 -> x0, blocking collectives: 130 us -> none  [the longest x1 43.4 us: per_device(): fin_rows = lax.all_gather(grad_fin.astype(bf), ALL, axis=0, tiled=True)]
    psum x1, waiting for transfers between devices: 0.02 us -> 47.9 us  [per_device(): sums = lax.psum(local_sums, ALL)]
    pallas_call x2 -> x1, Pallas kernels: 71.2 us -> 35.5 us  [layer_fwd(): pl.pallas_call(fwd_kernel, grid=(n,), in_specs=[rows(D), pl.BlockSpec((1,...]
    reduce_scatter x2 -> x0, waiting for transfers between devices: 27.8 us -> none  [the longest x1 27.8 us: per_device(): lax.psum_scatter(dot32('ne,de->nd', fin_mine, final_low[:D]), 'shard', sc...]
    slice x8 -> x22, local copies, waits for them, and re-layouts: 14.1 us -> 36.1 us  [the longest x2 23.4 us: unit_blocks(): return [out[u] for u in range(U)]]
    all_gather x2, waiting for transfers between devices: 77.2 us -> 58.5 us  [per_device(): mod_rows = lax.all_gather(mod_rows, ALL, axis=0, tiled=True)]
    unnamed x122 -> x115, local copies, waits for them, and re-layouts: 30.3 us -> 12 us
    pallas_call x2, Pallas kernels: 147 us -> 163 us  [the longest x1 86.6 us: first_call(): pl.pallas_call(functools.partial(first_kernel, R, nz, U, own), in_specs=[...]
  transfers between devices with their start and end apart: 7 -> 5, of which waited for: 3 -> 3; matrix products, arithmetic and copies ran while one was open for 6% -> 8% of each run, Pallas kernels for 35% -> 24%
where the time goes in v3:
time: 919 us; the launch traced here: 908 us
  Pallas kernels  573 us (62%)
  local copies, waits for them, and re-layouts  112 us (12%)
  waiting for transfers between devices  107 us (12%)
  other arithmetic  52.8 us (6%)
  matrix products  25.6 us (3%)
  between operations  22.7 us (2%)
  blocking collectives  14.4 us (2%)
    pallas_call x2, Pallas kernels, layer_grads(): pl.pallas_call(functools.partial(grad_kernel, R, nz, own, T), in_specs=[a...  215 us
    pallas_call x1, Pallas kernels, first_call(): pl.pallas_call(functools.partial(first_kernel, R, nz, U, own), in_specs=[...  86.6 us
    pallas_call x1, Pallas kernels, layer_fwd_gather(): pl.pallas_call(functools.partial(fwd_gather_kernel, R, nz, U), grid=(n,),...  76.4 us
    pallas_call x2, Pallas kernels, layer_bwd_attn(): pl.pallas_call(bwd_attn_kernel, grid=(n,), in_specs=[rows(D), rows(D), ro...  64.1 us
    all_gather x2, waiting for transfers between devices, per_device(): mod_rows = lax.all_gather(mod_rows, ALL, axis=0, tiled=True)  58.5 us
    pallas_call x2, Pallas kernels, layer_bwd_mlp(): pl.pallas_call(bwd_mlp_kernel, grid=(n,), in_specs=[rows(D), m3, pl.Block...  52.4 us
    psum x1, waiting for transfers between devices, per_device(): sums = lax.psum(local_sums, ALL)  47.9 us
    pallas_call x1, Pallas kernels, layer_fwd(): pl.pallas_call(fwd_kernel, grid=(n,), in_specs=[rows(D), pl.BlockSpec((1,...  35.5 us
  transfers between devices with their start and end apart: 5, of which 3 were waited for; matrix products, arithmetic and copies ran while one was open for 8% of the time, Pallas kernels for 24%

profile of v3, /device:TPU:0, one launch (start us, length us, event | category | flops | bytes accessed | tf_op | source)
XLA Modules:
  0.0 907.9 jit_solution(1829602509818924843)
XLA Ops:
  15.3 3.7 convert_element_type.150
  25.4 1.6 pad_maximum_fusion.1
  29.9 86.6 %shard_map.354 = (bf16[3,4,4,2,96,768]{5,4,3,2,1,0:T(8,128)(2,1)}, f32[8,4,8,384]{3,2,1,0:T(8,128)}, bf16[8,48,96]{2,1,0:T(8,128)(2,1)}, f32[256,96]{1,0:T(8,128...) custom-call(bf16[3,4,96,768]{3,2,1,0:T(8,128)(2,1)} %bitcast.145, ...), custom_call_target="tpu_custom_call" | custom-call | tf_op jit(solution)/shard_map/pallas_call | solution.py:371
  123.2 11.7 %fusion.67 = (bf16[1,4,4,2,96,768]{5,4,3,2,1,0:T(8,128)(2,1)}, bf16[1,4,4,2,96,768]{5,4,3,2,1,0:T(8,128)(2,1)}, bf16[1,4,4,2,96,768]{5,4,3,2,1,0:T(8,128)(2,1)}) fusion(bf16[3,4,4,2,96,768]{5,4,3,2,1,0:T(8,128)(2,1)} %get-tuple-element.129), kind=kLoop, calls=%fused_computation.162 | loop fusion | bytes 28311552 | tf_op jit(solution)/shard_map/slice | solution.py:284
  134.9 1.9 multiply_sine_fusion.1
  137.2 2.2 add_add_fusion.1
  139.4 76.4 %shard_map.355 = (bf16[1024,768]{1,0:T(8,128)(2,1)}, bf16[1024,2304]{1,0:T(8,128)(2,1)}, f32[1024,128]{1,0:T(8,128)}, bf16[1024,768]{1,0:T(8,128)(2,1)}, f32[102...) custom-call(f32[1024,768]{1,0:T(8,128)} %bitcast.162, ...), custom_call_target="tpu_custom_call" | custom-call | flops 15300820992 | bytes 60000000 | tf_op jit(solution)/shard_map/pallas_call | solution.py:404
  215.8 11.7 %fusion.66 = (bf16[1,4,4,2,96,768]{5,4,3,2,1,0:T(8,128)(2,1)}, bf16[1,4,4,2,96,768]{5,4,3,2,1,0:T(8,128)(2,1)}, bf16[1,4,4,2,96,768]{5,4,3,2,1,0:T(8,128)(2,1)}) fusion(bf16[3,4,4,2,96,768]{5,4,3,2,1,0:T(8,128)(2,1)} %get-tuple-element.131), kind=kLoop, calls=%fused_computation.161 | loop fusion | bytes 28311552 | tf_op jit(solution)/shard_map/slice | solution.py:284
  227.5 35.5 %shard_map.356 = (bf16[1024,768]{1,0:T(8,128)(2,1)}, bf16[1024,2304]{1,0:T(8,128)(2,1)}, f32[1024,128]{1,0:T(8,128)}, bf16[1024,768]{1,0:T(8,128)(2,1)}, f32[102...) custom-call(f32[1024,768]{1,0:T(8,128)} %get-tuple-element.130.x_ref, ...), custom_call_target="tpu_custom_call" | custom-call | flops 15300820992 | bytes 60000000 | tf_op jit(solution)/shard_map/pallas_call | solution.py:85
  263.0 2.3 reduce_sum.195
  274.3 2.3 multiply_reduce_fusion.9
  278.2 2.2 multiply_reduce_fusion.3
  280.4 2.3 broadcast_add_fusion
  282.7 26.3 %shard_map.357 = (bf16[1024,768]{1,0:T(8,128)(2,1)}, bf16[1024,3072]{1,0:T(8,128)(2,1)}, f32[1024,768]{1,0:T(8,128)}, bf16[1024,768]{1,0:T(8,128)(2,1)}, bf16[10...) custom-call(f32[1024,768]{1,0:T(8,128)} %bitcast.161, f32[4,8,768]{2,1,0:T(8,128)} %get-tuple-element.370.mod_ref, ...), custom_call_target="tpu_custom_call" | custom-call | flops 10871635968 | bytes 50000000 | tf_op jit(solution)/shard_map/pallas_call | solution.py:132
  309.0 32.0 %shard_map.358 = (bf16[1024,3072]{1,0:T(8,128)(2,1)}, f32[1024,768]{1,0:T(8,128)}, f32[4,8,768]{2,1,0:T(8,128)}, f32[8,768]{1,0:T(8,128)}) custom-call(bf16[1024,768]{1,0:T(8,128)(2,1)} %get-tuple-element.144.gmix_ref, bf16[1024,768]{1,0:T(8,128)(2,1)} %get-tuple-element.145.alow_ref, f32[1024,768]{1,0:T(8,128)} %get-tuple-element.146.gmid_ref, ...), custom_call_target="tpu_custom_call" | custom-call | flops 5637144576 | bytes 25000000 | tf_op jit(solution)/shard_map/pallas_call | solution.py:182
  341.0 26.1 %shard_map.360 = (bf16[1024,768]{1,0:T(8,128)(2,1)}, bf16[1024,3072]{1,0:T(8,128)(2,1)}, f32[1024,768]{1,0:T(8,128)}, bf16[1024,768]{1,0:T(8,128)(2,1)}, bf16[10...) custom-call(f32[1024,768]{1,0:T(8,128)} %get-tuple-element.168.g_ref, ...), custom_call_target="tpu_custom_call" | custom-call | flops 10871635968 | bytes 50000000 | tf_op jit(solution)/shard_map/pallas_call | solution.py:132
  367.1 32.1 %shard_map.361 = (bf16[1024,3072]{1,0:T(8,128)(2,1)}, f32[1024,768]{1,0:T(8,128)}, f32[4,8,768]{2,1,0:T(8,128)}, f32[8,768]{1,0:T(8,128)}) custom-call(bf16[1024,768]{1,0:T(8,128)(2,1)} %get-tuple-element.173.gmix_ref, bf16[1024,768]{1,0:T(8,128)(2,1)} %get-tuple-element.174.alow_ref, f32[1024,768]{1,0:T(8,128)} %get-tuple-element.175.gmid_ref, ...), custom_call_target="tpu_custom_call" | custom-call | flops 5637144576 | bytes 25000000 | tf_op jit(solution)/shard_map/pallas_call | solution.py:182
  414.5 1.6 copy.343
  420.9 1.7 reshape.334
  424.7 1.8 copy.360
  428.7 1.8 copy.370
  431.8 1.6 convolution_bitcast_fusion.3
  446.9 3.4 fusion.69
  451.2 2.2 convolution_bitcast_fusion.2
  453.4 4.3 concatenate.52
  458.7 2.9 all-gather.7.cloned.1.call-done
  462.9 55.7 %all-gather.5.cloned.1.call-done = bf16[32,4,6144]{2,1,0:T(4,128)(2,1)} async-done(((bf16[1,4,6144]{2,1,0:T(4,128)(2,1)}), bf16[32,4,6144]{2,1,0:T(4,128)(2,1)}) %all-gather.5.cloned.1.call-update) | async-done | bytes 1572880 | tf_op jit(solution)/shard_map/all_gather | solution.py:733
  518.6 2.7 reshape.345
  523.0 107.2 %shard_map.359.g1_ref = f32[3,8,96,384]{3,2,1,0:T(8,128)} custom-call(bf16[1024,768]{1,0:T(8,128)(2,1)} %get-tuple-element.160.xa, bf16[1024,768]{1,0:T(8,128)(2,1)} %get-tuple-element.161.xb, bf16[1024,768]{1,0:T(8,128)(2,1)} %get-tuple-element.162.xc, bf16[1024,768]{1,0:T(8,128)(2,1)} %get-tuple-element.163.xd, bf16[1024,3072]{1,0:T(8,128)(2,1)} %get-tuple-element.164.da, ...), custom_call_target="tpu_custom_call" | custom-call | flops 14495514624 | bytes 40000000 | tf_op jit(solution)/shard_map/pallas_call | solution.py:561
  630.3 1.6 convolution_bitcast_fusion
  634.0 1.7 convolution_add_fusion.2
  635.7 1.8 fusion.72
  638.2 2.3 fusion.37
  640.4 1.9 copy.381
  642.6 2.9 convolution_bitcast_fusion.1
  645.5 2.0 fusion.5
  650.0 107.5 %shard_map.362.g0_ref = f32[3,8,96,384]{3,2,1,0:T(8,128)} custom-call(bf16[1024,768]{1,0:T(8,128)(2,1)} %get-tuple-element.195.xa, bf16[1024,768]{1,0:T(8,128)(2,1)} %get-tuple-element.196.xb, bf16[1024,768]{1,0:T(8,128)(2,1)} %get-tuple-element.197.xc, bf16[1024,768]{1,0:T(8,128)(2,1)} %get-tuple-element.198.xd, bf16[1024,3072]{1,0:T(8,128)(2,1)} %get-tuple-element.199.da, ...), custom_call_target="tpu_custom_call" | custom-call | flops 14495514624 | bytes 40000000 | tf_op jit(solution)/shard_map/pallas_call | solution.py:561
  757.5 5.4 pad_maximum_fusion
  765.1 47.9 %all-reduce.13.cloned.1.call-done = f32[65,768]{0,1:T(8,128)} async-done(((f32[65,768]{0,1:T(8,128)}), f32[65,768]{0,1:T(8,128)}) %all-reduce.13.cloned.1.call-update) | async-done | bytes 199696 | tf_op jit(solution)/shard_map/psum | solution.py:763
  814.3 1.9 slice.284
  816.2 1.9 slice.283
  824.5 1.6 concatenate.53
  833.6 14.4 %psum.15 = f32[]{:T(128)} all-reduce(f32[]{:T(128)S(6)} %add.237), channel_id=1, replica_groups=mesh['rep'=4,'shard'=8] {'shard'}, use_global_device_ids=true, to_apply=%region_25.26 | all-reduce | flops 1 | bytes 8 | tf_op jit(solution)/shard_map/psum | solution.py:779
  850.4 1.6 fusion.58
  852.0 3.1 fusion.60
  855.1 2.0 fusion.62
  857.1 32.4 %shard_map.363 = (f32[2,96,10752]{2,1,0:T(8,128)}, f32[2,96,10752]{2,1,0:T(8,128)}, f32[2,96,10752]{2,1,0:T(8,128)}, bf16[2,96,10752]{2,1,0:T(8,128)(2,1)}) custom-call(f32[1]{0:T(128)} %bitcast.58.f_ref, f32[3,8,96,384]{3,2,1,0:T(8,128)} %shard_map.362.g0_ref, f32[3,8,96,384]{3,2,1,0:T(8,128)} %shard_map.359.g1_ref, ...), custom_call_target="tpu_custom_call" | custom-call | tf_op jit(solution)/shard_map/pallas_call | solution.py:599
  889.4 10.6 %shard_map.364 = (f32[2,96,3086]{2,1,0:T(8,128)}, f32[2,96,3086]{2,1,0:T(8,128)}, f32[2,96,3086]{2,1,0:T(8,128)}, bf16[2,96,3086]{2,1,0:T(8,128)(2,1)}) custom-call(f32[1]{0:T(128)} %bitcast.58.f_ref, f32[3,8,96,384]{3,2,1,0:T(8,128)} %shard_map.362.g0_ref, f32[3,8,96,384]{3,2,1,0:T(8,128)} %shard_map.359.g1_ref, f32[2,96,128]{2,1,0:T(8,128)} %pad.60.b_ref, ...), custom_call_target="tpu_custom_call" | custom-call | tf_op jit(solution)/shard_map/pallas_call | solution.py:623
  (276 shorter events, 97.3 us)
Async XLA Ops:
  7.2 6.8 copy-start.5
  7.2 454.3 %all-gather.7.cloned.1.call-start = ((), (), s32[]{:S(2)}) async-start(), calls=%async_computation.4 | async-start | bytes 1216512 | tf_op jit(solution)/shard_map/all_gather | solution.py:733
  9.6 4.5 copy-start.9
  19.0 2.7 copy-start.3
  20.4 3.5 slice-start
  20.4 3.7 copy-start.16
  27.1 1.5 copy-start.44
  27.1 1.5 copy-start.45
  28.5 90.6 %copy-start.48 = (s32[4]{0:T(128)S(1)}, s32[4]{0:T(128)}, u32[]{:S(2)}) copy-start(s32[4]{0:T(128)} %param.24) | copy-start | bytes 52
  116.5 5.9 copy-start.27
  123.2 11.7 %copy-start.46 = (f32[192]{0:T(256)S(1)}, f32[192]{0:T(256)}, u32[]{:S(2)}) copy-start(f32[192]{0:T(256)} %multiply_exponential_fusion) | copy-start | bytes 2308
  123.2 13.6 %copy-start.34 = (f32[4,16,256]{2,1,0:T(8,128)S(1)}, f32[4,16,256]{2,1,0:T(8,128)}, u32[]{:S(2)}) copy-start(f32[4,16,256]{2,1,0:T(8,128)} %param.21) | copy-start | bytes 196612
  123.2 13.6 %copy-start.35 = (f32[4,16,256]{2,1,0:T(8,128)S(1)}, f32[4,16,256]{2,1,0:T(8,128)}, u32[]{:S(2)}) copy-start(f32[4,16,256]{2,1,0:T(8,128)} %param.22) | copy-start | bytes 196612
  136.9 2.5 copy-start.21
  263.0 2.9 copy-start
  265.9 1.7 copy-start.41
  273.6 3.0 copy-start.29
  273.6 3.0 copy-start.30
  274.3 6.1 copy-start.33
  276.6 1.6 copy-start.22
  276.6 1.6 copy-start.38
  367.1 33.0 %copy-start.40 = (f32[4,8,768]{2,1,0:T(8,128)S(1)}, f32[4,8,768]{2,1,0:T(8,128)}, u32[]{:S(2)}) copy-start(f32[4,8,768]{2,1,0:T(8,128)} %get-tuple-element.179) | copy-start | bytes 294916
  403.4 115.2 %all-gather.5.cloned.1.call-start = ((), (), s32[]{:S(2)}) async-start(), calls=%async_computation.3 | async-start | bytes 1622016 | tf_op jit(solution)/shard_map/all_gather | solution.py:733
  404.4 1.6 copy-start.26
  407.4 225.7 %reduce-scatter.7.cloned.1.call-start = ((), (), s32[]{:S(2)}) async-start(), calls=%async_computation.5 | async-start | bytes 442368
  431.8 1.6 copy-start.39
  433.4 6.9 copy-start.32
  433.4 7.8 copy-start.31
  433.4 11.6 %copy-start.43 = (f32[1,768]{1,0:T(1,128)S(1)}, f32[1,768]{1,0:T(1,128)}, u32[]{:S(2)}) copy-start(f32[1,768]{1,0:T(1,128)} %slice.272) | copy-start | bytes 9220
  433.4 12.5 %copy-start.42 = (f32[1,768]{1,0:T(1,128)S(1)}, f32[1,768]{1,0:T(1,128)}, u32[]{:S(2)}) copy-start(f32[1,768]{1,0:T(1,128)} %slice.269) | copy-start | bytes 9220
  462.9 171.1 %copy-start.4 = (bf16[128,4608]{1,0:T(8,128)(2,1)}, bf16[128,4608]{1,0:T(8,128)(2,1)S(1)}, u32[]{:S(2)}) copy-start(bf16[128,4608]{1,0:T(8,128)(2,1)S(1)} %reshape.347) | copy-start | bytes 3538948
  522.6 107.7 %copy-start.12 = (bf16[128,8,96]{0,2,1:T(8,128)(2,1)S(1)}, bf16[128,8,96]{0,2,1:T(8,128)(2,1)}, u32[]{:S(2)}) copy-start(bf16[128,8,96]{0,2,1:T(8,128)(2,1)} %copy.360) | copy-start | bytes 589828
  522.6 241.1 %reduce-scatter.9.cloned.1.call-start = ((), (), s32[]{:S(2)}) async-start(), calls=%async_computation.6 | async-start | bytes 442368
  630.3 5.5 copy-start.37
  637.5 10.9 %copy-start.1 = (f32[3,8,96,384]{3,2,1,0:T(8,128)S(1)}, f32[3,8,96,384]{3,2,1,0:T(8,128)}, u32[]{:S(2)}) copy-start(f32[3,8,96,384]{3,2,1,0:T(8,128)} %shard_map.359.g1_ref) | copy-start | bytes 10616836
  642.4 170.7 %all-reduce.13.cloned.1.call-start = ((), (), s32[]{:S(2)}) async-start(), calls=%async_computation.2 | async-start | bytes 786432 | tf_op jit(solution)/shard_map/psum | solution.py:763
  642.6 4.9 copy-start.15
  642.6 4.9 copy-start.20
  757.5 60.6 %copy-start.2 = (f32[3,8,96,384]{3,2,1,0:T(8,128)S(1)}, f32[3,8,96,384]{3,2,1,0:T(8,128)}, u32[]{:S(2)}) copy-start(f32[3,8,96,384]{3,2,1,0:T(8,128)} %shard_map.362.g0_ref) | copy-start | bytes 10616836
  819.7 8.7 copy-start.11
  819.7 12.3 %copy-start.6 = (f32[768,192]{0,1:T(8,128)S(1)}, f32[768,192]{0,1:T(8,128)}, u32[]{:S(2)}) copy-start(f32[768,192]{0,1:T(8,128)} %fusion.17) | copy-start | bytes 1769476
  819.7 13.8 %copy-start.10 = (f32[17,768]{0,1:T(8,128)S(1)}, f32[17,768]{0,1:T(8,128)}, u32[]{:S(2)}) copy-start(f32[17,768]{0,1:T(8,128)} %slice.284) | copy-start | bytes 156676
  824.5 25.9 %copy-start.24 = (f32[769,16]{0,1:T(8,128)S(1)}, f32[769,16]{0,1:T(8,128)}, u32[]{:S(2)}) copy-start(f32[769,16]{0,1:T(8,128)} %param.29) | copy-start | bytes 147652
  824.5 25.9 %copy-start.36 = (f32[769,16]{0,1:T(8,128)S(1)}, f32[769,16]{0,1:T(8,128)}, u32[]{:S(2)}) copy-start(f32[769,16]{0,1:T(8,128)} %param.38) | copy-start | bytes 147652
  824.5 27.5 %copy-start.8 = (f32[769,192]{0,1:T(8,128)S(1)}, f32[769,192]{0,1:T(8,128)}, u32[]{:S(2)}) copy-start(f32[769,192]{0,1:T(8,128)} %param.28) | copy-start | bytes 1771780
  848.2 6.9 copy-start.7
  850.4 4.7 copy-start.13
  850.4 4.7 copy-start.14
  (10 other events, 9.7 us)
Sparse Core Ops, SparseCore 0:
  403.5 57.9 all-gather.6
  464.5 54.0 all-gather.4
  522.7 29.5 reduce-scatter.6
  642.5 29.5 reduce-scatter.8
  677.2 135.8 all-reduce.12

commit v4 on v3

--- a/solution.py
+++ b/solution.py
@@ -34,9 +34,9 @@
     xh,_=ln_parts(x)
     normed=(xh*(1.0+mod(1))+mod(0)).astype(bf)
     normed_ref[...]=normed
-    qkv_ref[:, :D]=(mm(normed, wa_ref[0])+bias(0)).astype(bf)
-    qkv_ref[:, D:2*D]=mm(normed, wa_ref[1]).astype(bf)
-    qkv_ref[:, 2*D:]=(mm(normed, wa_ref[2])+bias(1)).astype(bf)
+    qkv_ref[:, :D]=(mm(normed, wa_ref[0,0])+bias(0)).astype(bf)
+    qkv_ref[:, D:2*D]=mm(normed, wa_ref[0,1]).astype(bf)
+    qkv_ref[:, 2*D:]=(mm(normed, wa_ref[0,2])+bias(1)).astype(bf)
     lo=half_masks()
     for hp in range(HEADS//2):
         hook(1+hp)
@@ -55,7 +55,7 @@
             outs.append(mm(p,v))
         mixed_ref[:, c:c+128]=jnp.where(lo, outs[0], outs[1]).astype(bf)
     hook(7)
-    attn=mm(mixed_ref[...], wa_ref[3])+bias(2)
+    attn=mm(mixed_ref[...], wa_ref[0,3])+bias(2)
     attn_ref[...]=attn
     mid=x+mod(2)*attn
     mid_ref[...]=mid
@@ -65,30 +65,31 @@
     down=jnp.broadcast_to(bias(13),(TOK,D))
     for j in range(4):
         hook(8+j)
-        up=mm(ntwo, w1_ref[j])+bias(3+j)
+        up=mm(ntwo, w1_ref[0,j])+bias(3+j)
         upper_ref[:, j*D:(j+1)*D]=up
         t=jnp.tanh(C0*(up+C1*(up*up*up)))
         act=(0.5*up*(1.0+t)).astype(bf)
         activ_ref[:, j*D:(j+1)*D]=act
-        down=down+mm_nt(act, w2_ref[j])
+        down=down+mm_nt(act, w2_ref[0,j])
     down_ref[...]=down
     out_ref[...]=mid_ref[...]+mod(5)*down
 
 def full(shape):
     n=len(shape)
     return pl.BlockSpec(shape, lambda i: (0,)*n, pipeline_mode=pl.Buffered(1))
+def unit(u,n=4): return pl.BlockSpec((1,n,D,D),lambda i:(u,0,0,0),pipeline_mode=pl.Buffered(1))
 def rows(width): return pl.BlockSpec((TOK,width), lambda i:(i,0))
-def layer_fwd(x, mod, bias, wa, w1, w2):
+def layer_fwd(x, mod, bias, w):
     T=x.shape[0]; n=T//TOK
     sd=jax.ShapeDtypeStruct
     widths=[(D,bf),(3*D,bf),(128,f32),(D,bf),(D,f32),(D,f32),(D,bf),(FF,f32),(FF,bf),(D,f32),(D,f32)]
     return pl.pallas_call(fwd_kernel, grid=(n,),
-        in_specs=[rows(D), pl.BlockSpec((1,8,D),lambda i:(i,0,0)), full((16,D)), full((4,D,D)), full((4,D,D)), full((4,D,D))],
+        in_specs=[rows(D), pl.BlockSpec((1,8,D),lambda i:(i,0,0)), full((16,D)), unit(0), unit(1), unit(2)],
         out_specs=[rows(w) for w,_ in widths],
         out_shape=[sd((T,w),t) for w,t in widths],
         compiler_params=pltpu.CompilerParams(vmem_limit_bytes=VLIM),
         cost_estimate=pl.CostEstimate(flops=2*T*(9216*D+2*TOK*D), bytes_accessed=60_000_000, transcendentals=T*FF*2),
-    )(x,mod,bias,wa,w1,w2)
+    )(x,mod,bias,w,w,w)
 
 def bwd_mlp_kernel(g_ref, mod_ref, wa3_ref, w1_ref, w2_ref, down_ref, upper_ref, mid_ref, attn_ref,
                    dlow_ref, ulow_ref, gmid_ref, alow_ref, gmix_ref, dmod_ref, db_ref):
@@ -105,7 +106,7 @@
     db_ref[13:14,:]+=s0(gd)
     gn=jnp.zeros((TOK,D),f32)
     for j in range(4):
-        ga=mm(dl, w2_ref[j])
+        ga=mm(dl, w2_ref[0,j])
         up=upper_ref[:, j*D:(j+1)*D]
         u2=up*up
         t=jnp.tanh(C0*(up+C1*(u2*up)))
@@ -113,7 +114,7 @@
         db_ref[3+j:4+j,:]+=s0(gu)
         ul=gu.astype(bf)
         ulow_ref[:, j*D:(j+1)*D]=ul
-        gn=gn+mm_nt(ul, w1_ref[j])
+        gn=gn+mm_nt(ul, w1_ref[0,j])
     xh,r=ln_parts(mid_ref[...])
     dmod_ref[0,3:4,:]=s0(gn)
     dmod_ref[0,4:5,:]=s0(gn*xh)
@@ -124,18 +125,19 @@
     db_ref[2:3,:]+=s0(ga)
     al=ga.astype(bf)
     alow_ref[...]=al
-    gmix_ref[...]=mm_nt(al, wa3_ref[0]).astype(bf)
-def layer_bwd_mlp(g, mod, wa, w1, w2, down, upper, mid, attn):
+    gmix_ref[...]=mm_nt(al, wa3_ref[0,0]).astype(bf)
+def bwd_mlp_parts(g, mod, w, down, upper, mid, attn):
     T=g.shape[0]; n=T//TOK
     sd=jax.ShapeDtypeStruct
     m3=pl.BlockSpec((1,8,D),lambda i:(i,0,0))
-    return pl.pallas_call(bwd_mlp_kernel, grid=(n,),
-        in_specs=[rows(D), m3, pl.BlockSpec((1,D,D),lambda i:(3,0,0),pipeline_mode=pl.Buffered(1)), full((4,D,D)), full((4,D,D)), rows(D), rows(FF), rows(D), rows(D)],
-        out_specs=[rows(D),rows(FF),rows(D),rows(D),rows(D),m3,pl.BlockSpec((16,D),lambda i:(0,0))],
-        out_shape=[sd((T,D),bf),sd((T,FF),bf),sd((T,D),f32),sd((T,D),bf),sd((T,D),bf),sd((n,8,D),f32),sd((16,D),f32)],
-        compiler_params=pltpu.CompilerParams(vmem_limit_bytes=VLIM),
-        cost_estimate=pl.CostEstimate(flops=2*T*D*(2*FF+D), bytes_accessed=50_000_000, transcendentals=T*FF),
-    )(g,mod,wa,w1,w2,down,upper,mid,attn)
+    return (bwd_mlp_kernel,(g,mod,w,w,w,down,upper,mid,attn),
+        [rows(D), m3, pl.BlockSpec((1,1,D,D),lambda i:(0,3,0,0),pipeline_mode=pl.Buffered(1)), unit(1), unit(2), rows(D), rows(FF), rows(D), rows(D)],
+        [sd((T,D),bf),sd((T,FF),bf),sd((T,D),f32),sd((T,D),bf),sd((T,D),bf),sd((n,8,D),f32),sd((16,D),f32)],
+        [rows(D),rows(FF),rows(D),rows(D),rows(D),m3,pl.BlockSpec((16,D),lambda i:(0,0))],
+        pl.CostEstimate(flops=2*T*D*(2*FF+D), bytes_accessed=50_000_000, transcendentals=T*FF))
+def plain(kernel,args,specs,shapes,ospecs,cost):
+    return pl.pallas_call(kernel,grid=(args[0].shape[0]//TOK,),in_specs=specs,out_specs=ospecs,out_shape=shapes,
+        compiler_params=pltpu.CompilerParams(vmem_limit_bytes=VLIM),cost_estimate=cost)(*args)
 
 def bwd_attn_kernel(gmix_ref, alow_ref, gmid_ref, mod_ref, wa_ref, qkv_ref, lse_ref, x_ref,
                     low_ref, gin_ref, dmod_ref, db_ref):
@@ -169,24 +171,21 @@
             if j!=1:
                 row=0 if j==0 else 1
                 db_ref[row:row+1, c:c+128]+=s0(ol.astype(f32))
-    gn=mm_nt(low_ref[:, :D], wa_ref[0])+mm_nt(low_ref[:, D:2*D], wa_ref[1])+mm_nt(low_ref[:, 2*D:3*D], wa_ref[2])
+    gn=mm_nt(low_ref[:, :D], wa_ref[0,0])+mm_nt(low_ref[:, D:2*D], wa_ref[0,1])+mm_nt(low_ref[:, 2*D:3*D], wa_ref[0,2])
     xh,r=ln_parts(x_ref[...])
     dmod_ref[...]=jnp.zeros_like(dmod_ref)
     dmod_ref[0,0:1,:]=s0(gn)
     dmod_ref[0,1:2,:]=s0(gn*xh)
     gin_ref[...]=gmid_ref[...]+ln_back(gn,xh,r,mod(1))
-def layer_bwd_attn(gmix, alow, gmid, mod, wa, qkv, lse, x):
+def bwd_attn_parts(gmix, alow, gmid, mod, w, qkv, lse, x):
     T=gmix.shape[0]; n=T//TOK
     sd=jax.ShapeDtypeStruct
     m3=pl.BlockSpec((1,8,D),lambda i:(i,0,0))
-    return pl.pallas_call(bwd_attn_kernel, grid=(n,),
-        in_specs=[rows(D),rows(D),rows(D),m3,full((3,D,D)),rows(3*D),rows(128),rows(D)],
-        out_specs=[rows(4*D),rows(D),m3,pl.BlockSpec((8,D),lambda i:(0,0))],
-        out_shape=[sd((T,4*D),bf),sd((T,D),f32),sd((n,8,D),f32),sd((8,D),f32)],
-        compiler_params=pltpu.CompilerParams(vmem_limit_bytes=VLIM),
-        cost_estimate=pl.CostEstimate(flops=2*T*D*(3*D+5*TOK), bytes_accessed=25_000_000, transcendentals=T*TOK*HEADS),
-    )(gmix,alow,gmid,mod,wa,qkv,lse,x)
-
+    return (bwd_attn_kernel,(gmix,alow,gmid,mod,w,qkv,lse,x),
+        [rows(D),rows(D),rows(D),m3,unit(0,3),rows(3*D),rows(128),rows(D)],
+        [sd((T,4*D),bf),sd((T,D),f32),sd((n,8,D),f32),sd((8,D),f32)],
+        [rows(4*D),rows(D),m3,pl.BlockSpec((8,D),lambda i:(0,0))],
+        pl.CostEstimate(flops=2*T*D*(3*D+5*TOK), bytes_accessed=25_000_000, transcendentals=T*TOK*HEADS))
 MESH=pl.DeviceIdType.MESH
 class Gather:
     def __init__(self,R,nz,U,w_ref,out_ref,zs,zr,xs,xr,cs,cr,ls):
@@ -281,9 +280,9 @@
 def unit_blocks(out,R):
     U=out.shape[0]; W=out.shape[-1]
     out=out.reshape(U,R,D,W)
-    if R==4: return [out[u] for u in range(U)]
+    if R==4: return out
     m=R//4
-    return [out[u].reshape(4,m,D,W).transpose(0,2,1,3).reshape(4,D,D) for u in range(U)]
+    return out.reshape(U,4,m,D,W).transpose(0,1,3,2,4).reshape(U,4,D,D)
 def meet(peers):
     bar=pltpu.get_barrier_semaphore()
     for p in peers: pl.semaphore_signal(bar,inc=1,device_id=p,device_id_type=MESH)
@@ -397,18 +396,18 @@
             if n not in used: t()
         ga.finish()
 FWD_WIDTHS=[(D,bf),(3*D,bf),(128,f32),(D,bf),(D,f32),(D,f32),(D,bf),(FF,f32),(FF,bf),(D,f32),(D,f32)]
-def layer_fwd_gather(x,mod,bias,wa,w1,w2,w,R,S,cid):
+def layer_fwd_gather(x,mod,bias,full_w,w,R,S,cid):
     T=x.shape[0]; n=T//TOK; U,_,own,W=w.shape; nz=S//2
     sd=jax.ShapeDtypeStruct
     any_=pl.BlockSpec(memory_space=pl.ANY)
     o=pl.pallas_call(functools.partial(fwd_gather_kernel,R,nz,U),grid=(n,),
-        in_specs=[rows(D),pl.BlockSpec((1,8,D),lambda i:(i,0,0)),full((16,D)),full((4,D,D)),full((4,D,D)),full((4,D,D)),pl.BlockSpec(memory_space=pltpu.VMEM)],
+        in_specs=[rows(D),pl.BlockSpec((1,8,D),lambda i:(i,0,0)),full((16,D)),unit(0),unit(1),unit(2),pl.BlockSpec(memory_space=pltpu.VMEM)],
         out_specs=[rows(v) for v,_ in FWD_WIDTHS]+[any_],
         out_shape=[sd((T,v),t) for v,t in FWD_WIDTHS]+[sd((U,R,nz,2,own,W),bf)],
         scratch_shapes=gather_sems(R,nz,U),
         compiler_params=pltpu.CompilerParams(collective_id=cid,has_side_effects=True,vmem_limit_bytes=VLIM),
         cost_estimate=pl.CostEstimate(flops=2*T*(9216*D+2*TOK*D),bytes_accessed=60_000_000,transcendentals=T*FF*2),
-    )(x,mod,bias,wa,w1,w2,w)
+    )(x,mod,bias,full_w,full_w,full_w,w)
     return o[:11],o[11]
 CW=384; NCH=8
 def bit_orders(R):
@@ -433,139 +432,465 @@
                 if not any(m&b for b in orders[g][:i+1]): recv[g,i,m]=len(recv)
     return orders,n,pos,send,keep,recv
 
-def grad_kernel(R,nz,own,T, xa,xb,xc,xd, da,db,dc, out_ref, xin,xt,dy,sbuf,obuf,rbuf,sb,rb,kf,zs,zr,az,
-                xsem,dsem,csend,crecv,ssem,rsem,zss,zrs,ass,ars,als):
-    orders,n,pos,send,keep,recv=grad_plan(R)
-    G=NCH//R
-    MESH=pl.DeviceIdType.MESH
-    rep=lax.axis_index("rep"); shard=lax.axis_index("shard")
-    z=shard//2; c=lax.rem(shard,2)
-    xor=lambda m: jnp.bitwise_xor(rep,m)
-    mate=(rep,2*z+1-c)
-    zdev=lambda k: (rep, 2*lax.rem(z+k,nz)+c)
-    rdev=lambda m: (xor(m), shard)
-    bar=pltpu.get_barrier_semaphore()
-    peers=[mate]+[zdev(k) for k in range(1,nz)]+[rdev(m) for m in range(1,R)]
-    for p in peers: pl.semaphore_signal(bar,inc=1,device_id=p,device_id_type=MESH)
-    xs=(xa,xb,xc,xd)
-    xcopy=lambda i: pltpu.make_async_copy(xs[i],xin.at[i%2],xsem.at[i%2])
-    chunk=lambda k: pos[k][0]*R+xor(pos[k][1])
-    def dstart(u,k):
-        for i,ref in enumerate((da,db,dc)):
+def remote(src,dst,ssem,rsem,dev): return pltpu.make_async_remote_copy(src_ref=src,dst_ref=dst,send_sem=ssem,recv_sem=rsem,device_id=dev,device_id_type=MESH)
+def everyone(R,nz):
+    rep=lax.axis_index("rep"); shard=lax.axis_index("shard"); z=shard//2; c=lax.rem(shard,2)
+    return [(rep,2*z+1-c)]+[(rep,2*lax.rem(z+k,nz)+c) for k in range(1,nz)]+[(jnp.bitwise_xor(rep,m),shard) for m in range(1,R)]
+class Sums:
+    def __init__(self,R,nz,own,nu,xi,xs,dys,out_ref,scr):
+        (self.xin,self.xt,self.dy,self.sbuf,self.obuf,self.rbuf,self.sb,self.rb,self.kf,
+         self.xsem,self.dsem,self.csend,self.crecv,self.ssem,self.rsem)=scr
+        self.R,self.nz,self.own,self.nu,self.xi,self.xs,self.dys,self.out=R,nz,own,nu,xi,xs,dys,out_ref
+        self.orders,self.n,self.pos,self.send,self.keep,self.recv=grad_plan(R)
+        self.G=NCH//R
+        self.rep=lax.axis_index("rep"); self.shard=lax.axis_index("shard")
+        self.z=self.shard//2; self.c=lax.rem(self.shard,2)
+        self.mate=(self.rep,2*self.z+1-self.c)
+    def xor(self,m): return jnp.bitwise_xor(self.rep,m)
+    def rdev(self,m): return (self.xor(m),self.shard)
+    def chunk(self,k): return self.pos[k][0]*self.R+self.xor(self.pos[k][1])
+    def xcopy(self,i): return pltpu.make_async_copy(self.xs[i],self.xin.at[i],self.xsem.at[i])
+    def dstart(self,u,k):
+        for i,ref in enumerate(self.dys):
             @pl.when(u==i)
-            def _(): pltpu.make_async_copy(ref.at[:,pl.ds(pl.multiple_of(chunk(k)*CW,128),CW)],dy.at[k%4],dsem.at[k%4]).start()
-    def dwait(k): pltpu.make_async_copy(da.at[:,pl.ds(0,CW)],dy.at[k%4],dsem.at[k%4]).wait()
-    ccopy=lambda k: pltpu.make_async_remote_copy(src_ref=sbuf.at[k%2],dst_ref=rbuf.at[k%4],send_sem=csend.at[k%2],recv_sem=crecv.at[k%4],device_id=mate,device_id_type=MESH)
-    def scopy(u,g,m):
-        i=next(i for i,b in enumerate(orders[g]) if m&b); b=orders[g][i]
-        a=send[g,m]; d=recv[g,i,m^b]
-        return pltpu.make_async_remote_copy(src_ref=sb.at[u,a],dst_ref=rb.at[u,d],send_sem=ssem.at[u,a],recv_sem=rsem.at[u,d],device_id=rdev(b),device_id_type=MESH)
-    def rwait(u,g,i,m):
-        d=recv[g,i,m]
-        pltpu.make_async_remote_copy(src_ref=sb.at[u,0],dst_ref=rb.at[u,d],send_sem=ssem.at[u,0],recv_sem=rsem.at[u,d],device_id=rdev(1),device_id_type=MESH).wait_recv()
-    zcopy=lambda u,g,k: pltpu.make_async_remote_copy(src_ref=zs.at[u,g,lax.rem(z+k,nz)],dst_ref=zr.at[u,g,k-1],send_sem=zss.at[u,g,k-1],recv_sem=zrs.at[u,g,k-1],device_id=zdev(k),device_id_type=MESH)
-    def acopy(u,g,m): return pltpu.make_async_remote_copy(src_ref=az.at[u,g],dst_ref=out_ref.at[u,g*R+rep],send_sem=ass.at[u,g,m-1],recv_sem=ars.at[u,g,m-1],device_id=rdev(m),device_id_type=MESH)
-    alocal=lambda u,g: pltpu.make_async_copy(az.at[u,g],out_ref.at[u,g*R+rep],als.at[u,g])
-    def arecv(u,g,m):
-        return pltpu.make_async_remote_copy(src_ref=az.at[u,g],dst_ref=out_ref.at[u,g*R+xor(m)],send_sem=ass.at[u,g,m-1],recv_sem=ars.at[u,g,m-1],device_id=rdev(m),device_id_type=MESH)
-    xcopy(0).start(); xcopy(1).start(); dstart(0,0); dstart(0,1)
-    for i in range(4):
-        xcopy(i).wait()
-        xt[i]=xin[i%2].T
-        if i+2<4: xcopy(i+2).start()
-    pl.semaphore_wait(bar,len(peers))
-    def consume(u,k):
-        g,m,i=pos[k]
-        ccopy(k).wait_recv()
-        total=obuf[k%2]+rbuf[k%4]
+            def _(): pltpu.make_async_copy(ref.at[:,pl.ds(pl.multiple_of(self.chunk(k)*CW,128),CW)],self.dy.at[k%4],self.dsem.at[k%4]).start()
+    def dwait(self,k): pltpu.make_async_copy(self.dys[0].at[:,pl.ds(0,CW)],self.dy.at[k%4],self.dsem.at[k%4]).wait()
+    def ccopy(self,k): return remote(self.sbuf.at[k%2],self.rbuf.at[k%4],self.csend.at[k%2],self.crecv.at[k%4],self.mate)
+    def scopy(self,u,g,m):
+        i=next(i for i,b in enumerate(self.orders[g]) if m&b); b=self.orders[g][i]
+        a=self.send[g,m]; d=self.recv[g,i,m^b]
+        return remote(self.sb.at[u,a],self.rb.at[u,d],self.ssem.at[u,a],self.rsem.at[u,d],self.rdev(b))
+    def rwait(self,u,g,i,m):
+        d=self.recv[g,i,m]
+        remote(self.sb.at[u,0],self.rb.at[u,d],self.ssem.at[u,0],self.rsem.at[u,d],self.rdev(1)).wait_recv()
+    def load(self):
+        self.xcopy(0).start(); self.xcopy(1).start(); self.dstart(0,0); self.dstart(0,1)
+        for i in range(2):
+            self.xcopy(i).wait()
+            self.xt[i]=self.xin[i].T
+    def consume(self,u,k):
+        g,m,i=self.pos[k]
+        self.ccopy(k).wait_recv()
+        total=self.obuf[k%2]+self.rbuf[k%4]
         if i==0 and m:
-            sb[u,send[g,m]]=total.astype(bf)
-            scopy(u,g,m).start()
-        else: kf[u,keep[g,m]]=total.reshape(nz,own,CW)
-    def products(u):
+            self.sb[u,self.send[g,m]]=total.astype(bf)
+            self.scopy(u,g,m).start()
+        else: self.kf[u,self.keep[g,m]]=total.reshape(self.nz,self.own,CW)
+    def products(self,u):
+        nz,own=self.nz,self.own
         for k in range(NCH):
-            if k+2<NCH: dstart(u,k+2)
+            if k+2<NCH: self.dstart(u,k+2)
             else:
-                @pl.when(u<2)
-                def _(): dstart(u+1,k+2-NCH)
-            dwait(k)
-            xi=u+(u//2)*(chunk(k)//6)
-            p=mm(xt[xi],dy[k%4]).reshape(nz,2,own,CW)
+                @pl.when(u<self.nu-1)
+                def _(): self.dstart(u+1,k+2-NCH)
+            self.dwait(k)
+            p=mm(self.xt[self.xi(u,self.chunk(k))],self.dy[k%4]).reshape(nz,2,own,CW)
             even=p[:,0].reshape(nz*own,CW); odd=p[:,1].reshape(nz*own,CW)
-            if k>=2: ccopy(k).wait_send()
+            if k>=2: self.ccopy(k).wait_send()
             else:
                 @pl.when(u>0)
-                def _(): ccopy(k).wait_send()
-            sbuf[k%2]=jnp.where(c==0,odd,even)
-            obuf[k%2]=jnp.where(c==0,even,odd)
-            ccopy(k).start()
-            if k>0: consume(u,k-1)
+                def _(): self.ccopy(k).wait_send()
+            self.sbuf[k%2]=jnp.where(self.c==0,odd,even)
+            self.obuf[k%2]=jnp.where(self.c==0,even,odd)
+            self.ccopy(k).start()
+            if k>0: self.consume(u,k-1)
             else:
                 @pl.when(u>0)
-                def _(): consume(u-1,NCH-1)
-    def middle(u,i):
-        for g,m,j in pos:
+                def _(): self.consume(u-1,NCH-1)
+    def middle(self,u,i):
+        for g,m,j in self.pos:
             if m and j==i:
-                v=kf[u,keep[g,m]].reshape(nz*own,CW)
+                v=self.kf[u,self.keep[g,m]].reshape(self.nz*self.own,CW)
                 for i2 in range(i):
-                    rwait(u,g,i2,m); v=v+rb[u,recv[g,i2,m]].astype(f32)
-                sb[u,send[g,m]]=v.astype(bf)
-                scopy(u,g,m).start()
-    def along(u):
-        for g in range(G):
-            v=kf[u,keep[g,0]]
-            for i2 in range(n):
-                rwait(u,g,i2,0); v=v+rb[u,recv[g,i2,0]].astype(f32).reshape(nz,own,CW)
-            kf[u,keep[g,0]]=v
-            zs[u,g]=v.astype(bf)
-            for k in range(1,nz): zcopy(u,g,k).start()
-    def spread(u):
-        for g in range(G):
-            v=kf[u,keep[g,0],z]
-            for k in range(1,nz):
-                zcopy(u,g,k).wait_recv(); v=v+zr[u,g,k-1].astype(f32)
-            az[u,g]=v
-            alocal(u,g).start()
-            for m in range(1,R): acopy(u,g,m).start()
-    depth=max(n-1,0)
-    def step(t,_):
-        @pl.when(t<3)
-        def _(): products(t)
-        @pl.when(t==3)
-        def _(): consume(2,NCH-1)
-        for i in range(1,n):
-            @pl.when(jnp.logical_and(t>=i,t<3+i))
-            def _(): middle(t-i,i)
-        @pl.when(jnp.logical_and(t>=1+depth,t<4+depth))
-        def _(): along(t-1-depth)
-        @pl.when(jnp.logical_and(t>=2+depth,t<5+depth))
-        def _(): spread(t-2-depth)
-        return 0
-    lax.fori_loop(0,5+depth,step,0)
-    def finish(u,_):
-        for g in range(G):
-            alocal(u,g).wait()
-            for m in range(1,R): arecv(u,g,m).wait_recv(); acopy(u,g,m).wait_send()
-            for k in range(1,nz): zcopy(u,g,k).wait_send()
-            for m in range(1,R): scopy(u,g,m).wait_send()
-        return 0
-    lax.fori_loop(0,3,finish,0)
-    ccopy(NCH-2).wait_send(); ccopy(NCH-1).wait_send()
-
-def layer_grads(R,S,cid,xs,dys):
-    T=xs[0].shape[0]; nz=S//2; own=D//S; G=NCH//R
+                    self.rwait(u,g,i2,m); v=v+self.rb[u,self.recv[g,i2,m]].astype(f32)
+                self.sb[u,self.send[g,m]]=v.astype(bf)
+                self.scopy(u,g,m).start()
+    def form(self):
+        def one(t,_):
+            self.products(t)
+            if self.n>1:
+                @pl.when(t>=1)
+                def _(): self.middle(t-1,1)
+            return 0
+        lax.fori_loop(0,self.nu,one,0)
+        self.consume(self.nu-1,NCH-1)
+    def stage(self,i):
+        if i<self.n:
+            for u in range(self.nu-1 if i==1 else 0,self.nu): self.middle(u,i)
+    def hold(self):
+        for u in range(self.nu):
+            for g in range(self.G):
+                v=self.kf[u,self.keep[g,0]]
+                for i2 in range(self.n):
+                    self.rwait(u,g,i2,0); v=v+self.rb[u,self.recv[g,i2,0]].astype(f32).reshape(self.nz,self.own,CW)
+                self.out[u,g]=v
+    def finish(self):
+        for u in range(self.nu):
+            for g in range(self.G):
+                for m in range(1,self.R): self.scopy(u,g,m).wait_send()
+        self.ccopy(NCH-2).wait_send(); self.ccopy(NCH-1).wait_send()
+class Tail:
+    def __init__(self,R,nz,own,nu,fin,out_ref,scr):
+        (self.zs,self.zr,self.az,self.zss,self.zrs,self.ass,self.ars,self.als)=scr
+        self.R,self.nz,self.own,self.nu,self.fin,self.out,self.G=R,nz,own,nu,fin,out_ref,NCH//R
+        self.rep=lax.axis_index("rep"); self.shard=lax.axis_index("shard")
+        self.z=self.shard//2; self.c=lax.rem(self.shard,2)
+    def xor(self,m): return jnp.bitwise_xor(self.rep,m)
+    def zdev(self,k): return (self.rep,2*lax.rem(self.z+k,self.nz)+self.c)
+    def rdev(self,m): return (self.xor(m),self.shard)
+    def each(self): return [(u,g) for u in range(self.nu) for g in range(self.G)]
+    def zcopy(self,u,g,k): return remote(self.zs.at[u,g,lax.rem(self.z+k,self.nz)],self.zr.at[u,g,k-1],self.zss.at[u,g,k-1],self.zrs.at[u,g,k-1],self.zdev(k))
+    def acopy(self,u,g,m): return remote(self.az.at[u,g],self.out.at[u,g*self.R+self.rep],self.ass.at[u,g,m-1],self.ars.at[u,g,m-1],self.rdev(m))
+    def arecv(self,u,g,m): return remote(self.az.at[u,g],self.out.at[u,g*self.R+self.xor(m)],self.ass.at[u,g,m-1],self.ars.at[u,g,m-1],self.rdev(m))
+    def alocal(self,u,g): return pltpu.make_async_copy(self.az.at[u,g],self.out.at[u,g*self.R+self.rep],self.als.at[u,g])
+    def along(self):
+        for u,g in self.each():
+            self.zs[u,g]=self.fin[u,g].astype(bf)
+            for k in range(1,self.nz): self.zcopy(u,g,k).start()
+    def spread(self):
+        for u,g in self.each():
+            v=self.fin[u,g,self.z]
+            for k in range(1,self.nz):
+                self.zcopy(u,g,k).wait_recv(); v=v+self.zr[u,g,k-1].astype(f32)
+            self.az[u,g]=v
+            self.alocal(u,g).start()
+            for m in range(1,self.R): self.acopy(u,g,m).start()
+    def finish(self):
+        for u,g in self.each():
+            self.alocal(u,g).wait()
+            for m in range(1,self.R): self.arecv(u,g,m).wait_recv(); self.acopy(u,g,m).wait_send()
+            for k in range(1,self.nz): self.zcopy(u,g,k).wait_send()
+    def squares(self):
+        v=jnp.zeros((8,128),f32)
+        for u,g in self.each():
+            b=self.az[u,g]; b=b*b
+            for q in range(CW//128): v=v+jnp.sum(b[:,q*128:(q+1)*128].reshape(self.own//8,8,128),axis=0)
+        return v
+def sums_scratch(R,nz,own,T,nu):
     orders,n,pos,send,keep,recv=grad_plan(R)
     dma=pltpu.SemaphoreType.DMA; V=pltpu.VMEM
-    any_=pl.BlockSpec(memory_space=pl.ANY)
     ns,nk,nr=max(len(send),1),len(keep),max(len(recv),1)
-    return pl.pallas_call(functools.partial(grad_kernel,R,nz,own,T),
-        in_specs=[any_]*7, out_specs=any_, out_shape=jax.ShapeDtypeStruct((3,NCH,own,CW),f32),
-        scratch_shapes=[V((2,T,D),bf),V((4,D,T),bf),V((4,T,CW),bf),V((2,D//2,CW),f32),V((2,D//2,CW),f32),V((4,D//2,CW),f32),
-            V((3,ns,D//2,CW),bf),V((3,nr,D//2,CW),bf),V((3,nk,nz,own,CW),f32),V((3,G,nz,own,CW),bf),V((3,G,nz-1,own,CW),bf),V((3,G,own,CW),f32),
-            dma((2,)),dma((4,)),dma((2,)),dma((4,)),dma((3,ns)),dma((3,nr)),dma((3,G,nz-1)),dma((3,G,nz-1)),dma((3,G,R-1)),dma((3,G,R-1)),dma((3,G))],
+    return [V((2,T,D),bf),V((2,D,T),bf),V((4,T,CW),bf),V((2,D//2,CW),f32),V((2,D//2,CW),f32),V((4,D//2,CW),f32),
+            V((nu,ns,D//2,CW),bf),V((nu,nr,D//2,CW),bf),V((nu,nk,nz,own,CW),f32),
+            dma((2,)),dma((4,)),dma((2,)),dma((4,)),dma((nu,ns)),dma((nu,nr))]
+def tail_scratch(R,nz,own,nu):
+    G=NCH//R; dma=pltpu.SemaphoreType.DMA; V=pltpu.VMEM
+    return [V((nu,G,nz,own,CW),bf),V((nu,G,nz-1,own,CW),bf),V((nu,G,own,CW),f32),dma((nu,G,nz-1)),dma((nu,G,nz-1)),dma((nu,G,R-1)),dma((nu,G,R-1)),dma((nu,G))]
+NSUM=15; NTAIL=8
+def remote(src,dst,ssem,rsem,dev): return pltpu.make_async_remote_copy(src_ref=src,dst_ref=dst,send_sem=ssem,recv_sem=rsem,device_id=dev,device_id_type=MESH)
+def everyone(R,nz):
+    rep=lax.axis_index("rep"); shard=lax.axis_index("shard"); z=shard//2; c=lax.rem(shard,2)
+    return [(rep,2*z+1-c)]+[(rep,2*lax.rem(z+k,nz)+c) for k in range(1,nz)]+[(jnp.bitwise_xor(rep,m),shard) for m in range(1,R)]
+MLP_X=lambda u,ch: u
+ATTN_X=lambda u,ch: ch//6
+def carrier_kernel(R,nz,own,nu,xi,nt,compute,ci,co,extra,ei,eo,*refs):
+    p=0; parts=[]
+    t1=1 if nt else 0
+    for cnt in (ci,2+nu,t1,ei,co,1,2*t1,eo,NSUM,NTAIL*t1,len(refs)): parts.append(refs[p:p+cnt]); p+=cnt
+    cin,rin,tin,ein,cout,(hold_ref,),tout,eout,scr,tscr,escr=parts
+    S_=Sums(R,nz,own,nu,xi,rin[:2],rin[2:],hold_ref,scr)
+    T_=Tail(R,nz,own,nt,tin[0],tout[0],tscr) if nt else None
+    events=extra(R,nz,ein,eout,escr) if extra else {}
+    i=pl.program_id(0); last=pl.num_programs(0)-1
+    @pl.when(i==0)
+    def _():
+        S_.load()
+        meet(everyone(R,nz))
+        if T_: T_.along()
+        for f in events.get(0,[]): f()
+        S_.form()
+    for q in (1,2,3):
+        @pl.when(i==q)
+        def _():
+            S_.stage(q)
+            if T_ and q==2: T_.spread()
+            for f in events.get(q,[]): f()
+    compute(*cin,*cout)
+    @pl.when(i==last)
+    def _():
+        S_.hold(); S_.finish()
+        if T_:
+            T_.finish(); tout[1][...]=T_.squares()
+        for f in events.get(99,[]): f()
+def carry(R,S,cid,xs,dys,xi,tail,compute,cargs,cspecs,coshapes,cospecs,cost,extra=None):
+    T=xs[0].shape[0]; nz=S//2; own=D//S; nu=len(dys); G=NCH//R
+    any_=pl.BlockSpec(memory_space=pl.ANY); sd=jax.ShapeDtypeStruct
+    f,eargs,especs,eshapes,eospecs,escratch=extra or (None,[],[],[],[],[])
+    nt=tail[0].shape[0] if tail else 0
+    held=(nu,G,nz,own,CW)
+    o=pl.pallas_call(functools.partial(carrier_kernel,R,nz,own,nu,xi,nt,compute,len(cargs),len(coshapes),f,len(eargs),len(eshapes)),grid=(T//TOK,),
+        in_specs=list(cspecs)+[any_]*(2+nu)+[full(t.shape) for t in tail]+especs,
+        out_specs=list(cospecs)+[full(held)]+([any_,full((8,128))] if nt else [])+eospecs,
+        out_shape=list(coshapes)+[sd(held,f32)]+([sd((nt,NCH,own,CW),f32),sd((8,128),f32)] if nt else [])+eshapes,
+        scratch_shapes=sums_scratch(R,nz,own,T,nu)+(tail_scratch(R,nz,own,nt) if nt else [])+escratch,
         compiler_params=pltpu.CompilerParams(collective_id=cid,has_side_effects=True,vmem_limit_bytes=VLIM),
-        cost_estimate=pl.CostEstimate(flops=2*T*D*9216,bytes_accessed=40_000_000,transcendentals=0),
-    )(*xs,*dys)
+        cost_estimate=cost)(*cargs,*xs,*dys,*tail,*eargs)
+    a=len(coshapes); b=a+1+(2 if nt else 0)
+    return o[:a],o[a],o[a+1:b],o[b:]
+def last_kernel(R,nz,own,sums,nt,extra,ei,eo,*refs):
+    k=1 if sums else 0; p=0; parts=[]
+    for cnt in (3*k,k,ei,4*k,eo,NSUM*k,k,NTAIL*k,NTAIL*k,len(refs)): parts.append(refs[p:p+cnt]); p+=cnt
+    rin,tin,ein,rout,eout,scr,held,t1scr,t2scr,escr=parts
+    if sums:
+        S_=Sums(R,nz,own,1,ATTN_X,rin[:2],rin[2:],held[0],scr)
+        T1=Tail(R,nz,own,nt,tin[0],rout[0],t1scr); T2=Tail(R,nz,own,1,held[0],rout[2],t2scr)
+    def squares():
+        return T1.squares()+T2.squares()
+    events=extra(R,nz,ein,eout,escr,squares if sums else None)
+    run=lambda q: [f() for f in events.get(q,[])]
+    if sums: S_.load()
+    meet(everyone(R,nz))
+    if sums: T1.along()
+    run(0)
+    if sums: S_.form(); S_.stage(1)
+    run(1)
+    if sums:
+        for i in range(2,S_.n): S_.stage(i)
+        T1.spread(); S_.hold(); T2.along()
+    run(2)
+    run(3)
+    if sums: T2.spread()
+    run(4)
+    if sums:
+        S_.finish(); T1.finish(); T2.finish()
+        rout[1][...]=T1.squares(); rout[3][...]=T2.squares()
+    run(99)
+def last_call(R,S,cid,xs,dys,tail,extra):
+    nz=S//2; own=D//S; sums=bool(xs); G=NCH//R
+    any_=pl.BlockSpec(memory_space=pl.ANY); sd=jax.ShapeDtypeStruct; vm=pl.BlockSpec(memory_space=pltpu.VMEM)
+    f,eargs,especs,eshapes,eospecs,escratch=extra
+    nt=tail[0].shape[0] if sums else 0
+    mine=[]
+    if sums: mine=sums_scratch(R,nz,own,xs[0].shape[0],1)+[pltpu.VMEM((1,G,nz,own,CW),f32)]+tail_scratch(R,nz,own,nt)+tail_scratch(R,nz,own,1)
+    return pl.pallas_call(functools.partial(last_kernel,R,nz,own,sums,nt,f,len(eargs),len(eshapes)),
+        in_specs=[any_]*(len(xs)+len(dys))+[vm]*len(tail)+especs,out_specs=([any_,vm,any_,vm] if sums else [])+eospecs,
+        out_shape=([sd((nt,NCH,own,CW),f32),sd((8,128),f32),sd((1,NCH,own,CW),f32),sd((8,128),f32)] if sums else [])+eshapes,
+        scratch_shapes=mine+escratch,
+        compiler_params=pltpu.CompilerParams(collective_id=cid,has_side_effects=True,vmem_limit_bytes=VLIM))(*xs,*dys,*tail,*eargs)
+def sums_call(R,S,cid,xs,dys,tail):
+    none=lambda R,nz,ins,outs,scr,squares: {}
+    return last_call(R,S,cid,xs,dys,tail,(none,[],[],[],[],[]))
+
+def rows_events(R,nz,ins,outs,scr):
+    (w,),(g,)=ins,outs; rs,rr,zs,zr,cs,cr,ls=scr
+    rep=lax.axis_index("rep"); shard=lax.axis_index("shard"); z=shard//2; c=lax.rem(shard,2)
+    loc=lambda: pltpu.make_async_copy(w,g.at[rep,z,c],ls)
+    rc=lambda m: remote(w,g.at[rep,z,c],rs.at[m-1],rr.at[m-1],(jnp.bitwise_xor(rep,m),shard))
+    zc=lambda k: remote(g.at[:,z,c],g.at[:,z,c],zs.at[k-1],zr.at[k-1],(rep,2*lax.rem(z+k,nz)+c))
+    cc=lambda: remote(g.at[:,:,c],g.at[:,:,c],cs,cr,(rep,2*z+1-c))
+    def a():
+        loc().start()
+        for m in range(1,R): rc(m).start()
+    def b():
+        loc().wait()
+        for m in range(1,R): rc(m).wait_recv()
+        for k in range(1,nz): zc(k).start()
+    def d():
+        for k in range(1,nz): zc(k).wait_recv()
+        cc().start()
+    def e():
+        cc().wait()
+        for m in range(1,R): rc(m).wait_send()
+        for k in range(1,nz): zc(k).wait_send()
+    return {0:[a],1:[b],2:[d],99:[e]}
+def rows_extra(w,R,S):
+    nz=S//2; dma=pltpu.SemaphoreType.DMA
+    return (rows_events,[w],[full(w.shape)],[jax.ShapeDtypeStruct((R,nz,2)+w.shape,bf)],[pl.BlockSpec(memory_space=pl.ANY)],
+        [dma((R-1,)),dma((R-1,)),dma((nz-1,)),dma((nz-1,)),dma(()),dma(()),dma(())])
+
+class ShardSum:
+    def __init__(self,nz,x,mr,ps,zr,ms,mrs,zs,zrs):
+        self.nz,self.x,self.mr,self.ps,self.zr=nz,x,mr,ps,zr
+        self.ms,self.mrs,self.zs,self.zrs=ms,mrs,zs,zrs
+        self.rep=lax.axis_index("rep"); shard=lax.axis_index("shard"); self.z=shard//2; self.c=lax.rem(shard,2)
+    def mate(self): return remote(self.x.at[:,1-self.c],self.mr,self.ms,self.mrs,(self.rep,2*self.z+1-self.c))
+    def far(self,k):
+        t=lax.rem(self.z+k,self.nz)
+        return remote(self.ps.at[t],self.zr.at[k-1],self.zs.at[k-1],self.zrs.at[k-1],(self.rep,2*t+self.c))
+    def one(self): self.mate().start()
+    def two(self):
+        self.mate().wait_recv()
+        self.ps[...]=self.x[:,self.c]+self.mr[...]
+        for k in range(1,self.nz): self.far(k).start()
+    def three(self):
+        v=self.ps[self.z]
+        for k in range(1,self.nz): self.far(k).wait_recv(); v=v+self.zr[k-1]
+        return v
+    def end(self):
+        self.mate().wait_send()
+        for k in range(1,self.nz): self.far(k).wait_send()
+def shard_sum_scratch(nz,shape,own_input):
+    V=pltpu.VMEM; dma=pltpu.SemaphoreType.DMA
+    return ([V((nz,2)+shape,f32)] if own_input else [])+[V((nz,)+shape,f32),V((nz,)+shape,f32),V((nz-1,)+shape,f32),dma(()),dma(()),dma((nz-1,)),dma((nz-1,))]
+
+def sig_back(v,g):
+    t=1.0/(1.0+jnp.exp(-v))
+    return g*(t*(1.0+v*(1.0-t)))
+def fold(v):
+    v=v*v; r,c=v.shape
+    if r%8: v=jnp.concatenate([v,jnp.zeros((8-r%8,c),f32)],axis=0)
+    v=jnp.sum(v.reshape(-1,8,c),axis=0)
+    if c%128: v=jnp.concatenate([v,jnp.zeros((8,128-c%128),f32)],axis=1)
+    t=v[:,:128]
+    for q in range(1,v.shape[1]//128): t=t+v[:,q*128:(q+1)*128]
+    return t
+HEAD_ROWS=24
+FIN_ROW=45
+def cond_events(R,nz,ins,outs,scr,squares):
+    (rows_ref,fin_ref,cond_ref,call_ref,act_ref,pre_ref,lab_ref,feat_ref,ada_ref,finw_ref,t2_ref,w_ref)=ins[:12]
+    pieces=ins[12:-1]; sq1_ref=ins[-1]
+    adag,fing,secg,clsg,firg,vec,sumo,headg,norm_ref=outs
+    S=2*nz
+    fx,tx,sx,asm=scr[0],scr[8],scr[16],scr[24]
+    fs=ShardSum(nz,*scr[0:8]); ts=ShardSum(nz,*scr[8:16]); ss=ShardSum(nz,*scr[16:24])
+    g0=scr[25]
+    re=rows_events(R,nz,(w_ref,),(g0,),scr[26:33])
+    tot,rr,rsem,rrs,gc_s,hs,hr,hcs,hcr,nv,n1,n2,n3,nsem,nrec=scr[33:]
+    rep=lax.axis_index("rep"); shard=lax.axis_index("shard"); z=shard//2; c=lax.rem(shard,2)
+    nr=sumo.shape[0]; own=sumo.shape[1]; nb=nr-HEAD_ROWS; FC=fin_ref.shape[1]
+    mate=(rep,2*z+1-c); zdev=lambda k: (rep,2*lax.rem(z+k,nz)+c); rdev=lambda m: (jnp.bitwise_xor(rep,m),shard)
+    rc=lambda m: remote(tot,rr.at[rep],rsem.at[m-1],rrs.at[m-1],rdev(m))
+    hz=lambda k: remote(headg.at[z,c],headg.at[z,c],hs.at[k-1],hr.at[k-1],zdev(k))
+    hc=lambda: remote(headg.at[:,c],headg.at[:,c],hcs,hcr,mate)
+    M6=6*D
+    def gather():
+        asm[...]=jnp.zeros(asm.shape,f32)
+        for l in range(2):
+            db1,db2,dm1,dm2=pieces[4*l:4*l+4]; o=14*l
+            asm[o:o+2]=db2[0:2]; asm[o+2:o+7]=db1[2:7]; asm[o+13:o+14]=db1[13:14]
+            t1=jnp.sum(dm1[...],axis=0); t2=jnp.sum(dm2[...],axis=0)
+            asm[o+7:o+9]=t2[0:2]; asm[o+9:o+13]=t1[2:6]
+        pg,pb,gfm,hd=pieces[8:]
+        asm[28:44]=pg[...]; asm[44:45]=pb[...]
+        asm[FIN_ROW:FIN_ROW+2]=jnp.sum(gfm[...],axis=0)
+        asm[nb:]=hd[...]
+        for s in range(S):
+            sx[s//2,s%2]=asm[:,s*own:(s+1)*own]
+            for r in range(FC//own):
+                p=s*FC+r*own; row=FIN_ROW+p//D
+                sx[s//2,s%2,FIN_ROW+r:FIN_ROW+r+1,:]=asm[row:row+1,p%D:p%D+own]
+        ss.one()
+        fin=fin_ref[...]
+        for s in range(S): fx[s//2,s%2]=mm_nt(finw_ref[s],fin)
+        fs.one()
+    def layer1():
+        gc=jnp.zeros(gc_s.shape,f32)
+        for q in range(6):
+            o=slice(q*D,(q+1)*D); r=rows_ref[:,o]
+            adag[1,:,o]=mm(cond_ref[...],r)
+            gc=gc+mm_nt(ada_ref[1,:,o],r)
+        gc_s[...]=gc
+        fing[...]=mm_tn(fin_ref[...],call_ref[...])
+        fs.two(); ss.two()
+    def total():
+        tot[...]=ss.three()
+        rr[rep]=tot[...]
+        for m in range(1,R): rc(m).start()
+    def layer0():
+        for f in re[99]: f()
+        N=cond_ref.shape[1]; M=4*N; B=M6//4
+        g=g0[...].reshape(M,B)
+        wide=jnp.zeros((own,M),f32)
+        at=lax.broadcasted_iota(jnp.int32,(1,M),1)
+        n_of=lax.broadcasted_iota(jnp.int32,(N,1),0)
+        for j in range(4):
+            o=slice(j*B,(j+1)*B)
+            spot=jnp.where(at==4*n_of+j,1.0,0.0).astype(bf)
+            adag[0,:,o]=mm(mm(cond_ref[...],spot).astype(bf),g)
+            wide=wide+jnp.where(at-4*(at//4)==j,mm_nt(ada_ref[0,:,o],g),0.0)
+        pick=jnp.where(lax.broadcasted_iota(jnp.int32,(M,1),0)//4==lax.broadcasted_iota(jnp.int32,(1,N),1),1.0,0.0)
+        gc=gc_s[...]+lax.dot_general(wide,pick,(((1,),(0,)),((),())),precision=lax.Precision.HIGHEST,preferred_element_type=f32)
+        g=sig_back(pre_ref[1],gc+fs.three())
+        low=g.astype(bf)
+        for s in range(S): tx[s//2,s%2]=mm_tn(t2_ref[s],low)
+        ts.one()
+        vec[0]=jnp.broadcast_to(jnp.sum(g,axis=1,keepdims=True),vec.shape[1:])
+        secg[...]=mm(low,act_ref[...])
+        hot=jnp.where(lab_ref[...]==lax.broadcasted_iota(jnp.int32,(1,clsg.shape[1]),1).astype(f32),1.0,0.0)
+        clsg[...]=lax.dot_general(g,hot,(((1,),(0,)),((),())),precision=lax.Precision.HIGHEST,preferred_element_type=f32)
+    def time_and_sums():
+        ts.two()
+        for m in range(1,R): rc(m).wait_recv()
+        v=rr[0]
+        for r in range(1,R): v=v+rr[r]
+        sumo[...]=v
+        headg[z,c]=v[nb:]
+        for k in range(1,nz): hz(k).start()
+        first=lax.broadcasted_iota(jnp.int32,(1,128),1)<1
+        p=fold(v[:nb])+fold(jnp.where(first,vec[0],0.0))
+        for q in range(2): p=p+fold(adag[q])
+        for ref in (fing,secg,clsg): p=p+fold(ref[...])
+        g=sig_back(pre_ref[0],ts.three())
+        b=jnp.broadcast_to(jnp.sum(g,axis=1,keepdims=True),vec.shape[1:])
+        vec[1]=b
+        f=mm(g.astype(bf),feat_ref[...])
+        firg[...]=f
+        p=p+fold(f)+fold(jnp.where(first,b,0.0))
+        nv[...]=jnp.where(rep==0,p,0.0)
+        for k in range(1,nz): hz(k).wait_recv()
+        hc().start()
+    def end():
+        hc().wait()
+        for k in range(1,nz): hz(k).wait_send()
+        for m in range(1,R): rc(m).wait_send()
+        fs.end(); ts.end(); ss.end()
+        nv[...]=nv[...]+sq1_ref[...]+(squares() if squares else 0.0)
+        cp=remote(nv,n1,nsem.at[0],nrec.at[0],mate)
+        cp.start(); cp.wait()
+        n2[z]=nv[...]+n1[...]
+        nz_=lambda k: remote(n2.at[z],n2.at[z],nsem.at[k],nrec.at[k],zdev(k))
+        for k in range(1,nz): nz_(k).start()
+        for k in range(1,nz): nz_(k).wait()
+        v=n2[0]
+        for q in range(1,nz): v=v+n2[q]
+        n3[rep]=v
+        nr_=lambda m: remote(n3.at[rep],n3.at[rep],nsem.at[nz-1+m],nrec.at[nz-1+m],rdev(m))
+        for m in range(1,R): nr_(m).start()
+        for m in range(1,R): nr_(m).wait()
+        v=n3[0]
+        for r in range(1,R): v=v+n3[r]
+        for s in range(S): v=v+fold(headg[s//2,s%2,:HEAD_ROWS-1])
+        norm_ref[...]=v
+    return {0:re[0]+[gather],1:re[1]+[layer1],2:re[2]+[total],3:[layer0],4:[time_and_sums],99:[end]}
+def cond_extra(args,R,S):
+    nz=S//2; own=D//S; N=args[2].shape[1]; nr=48+HEAD_ROWS; FC=args[1].shape[1]; w=args[11]
+    vm=pl.BlockSpec(memory_space=pltpu.VMEM); sd=jax.ShapeDtypeStruct; dma=pltpu.SemaphoreType.DMA; V=pltpu.VMEM
+    shapes=[sd((2,own,6*D),f32),sd((FC,D),f32),sd((own,D),f32),sd((own,1024),f32),sd((own,256),f32),sd((2,own,128),f32),sd((nr,own),f32),sd((nz,2,HEAD_ROWS,own),f32),sd((8,128),f32)]
+    scratch=shard_sum_scratch(nz,(own,N),True)*2+shard_sum_scratch(nz,(nr,own),True)+[V((nr,D),f32),V((R,nz,2)+w.shape,bf)]
+    scratch+=[dma((R-1,)),dma((R-1,)),dma((nz-1,)),dma((nz-1,)),dma(()),dma(()),dma(())]
+    scratch+=[V((nr,own),f32),V((R,nr,own),f32),dma((R-1,)),dma((R-1,)),V((own,N),f32),
+        dma((nz-1,)),dma((nz-1,)),dma(()),dma(()),V((8,128),f32),V((8,128),f32),V((nz,8,128),f32),V((R,8,128),f32),dma((nz+R,)),dma((nz+R,))]
+    return (cond_events,list(args),[vm]*len(args),shapes,[vm]*len(shapes),scratch)
+
+def head_kernel(inv,x_ref,fm_ref,hw_ref,hb_ref,tn_ref,gx_ref,gfm_ref,hg_ref):
+    i=pl.program_id(0)
+    x=x_ref[...]
+    sh=fm_ref[0,0:1,:]; sc=fm_ref[0,1:2,:]
+    xh,r=ln_parts(x)
+    nrm=(xh*(1.0+sc)+sh).astype(bf)
+    diff=mm(nrm,hw_ref[...])+hb_ref[0:1,:]-tn_ref[0].T
+    g=2.0*(diff*inv)
+    low=g.astype(bf)
+    @pl.when(i==0)
+    def _():
+        hg_ref[...]=jnp.zeros_like(hg_ref)
+    p=low.shape[1]
+    hg_ref[:p]+=mm_tn(low,nrm)
+    hg_ref[p:p+1,:p]+=jnp.sum(g,axis=0,keepdims=True)
+    hg_ref[HEAD_ROWS-1:HEAD_ROWS,:p]+=jnp.sum(diff*diff,axis=0,keepdims=True)
+    gn=mm_nt(low,hw_ref[...])
+    gfm_ref[0,0:1,:]=jnp.sum(gn,axis=0,keepdims=True)
+    gfm_ref[0,1:2,:]=jnp.sum(gn*xh,axis=0,keepdims=True)
+    gx_ref[...]=ln_back(gn,xh,r,sc)
+def head(x,fm,hw,hb,tn,inv):
+    T=x.shape[0]; n=T//TOK; sd=jax.ShapeDtypeStruct; p=hw.shape[1]
+    m2=pl.BlockSpec((1,2,D),lambda i:(i,0,0))
+    fixed=lambda *s: pl.BlockSpec(s,lambda i:(0,)*len(s))
+    return pl.pallas_call(functools.partial(head_kernel,inv),grid=(n,),
+        in_specs=[rows(D),m2,fixed(D,p),fixed(1,p),pl.BlockSpec((1,p,TOK),lambda i:(i,0,0))],
+        out_specs=[rows(D),m2,fixed(HEAD_ROWS,D)],
+        out_shape=[sd((T,D),f32),sd((n,2,D),f32),sd((HEAD_ROWS,D),f32)],
+        compiler_params=pltpu.CompilerParams(vmem_limit_bytes=VLIM))(x,fm,hw,hb,tn)
 LAYERS=2
 beta_one=0.9; beta_two=0.999; adam_eps=1e-8; learn_rate=0.01; weight_decay=0.01; step_count=10.0
 def adam_update(w,g,m,v,factor):
@@ -576,30 +901,31 @@
     vh=v2/(1.0-beta_two**step_count)
     w2=w-learn_rate*(mh/(jnp.sqrt(vh)+adam_eps)+weight_decay*w)
     return (w2,m2,v2,w2.astype(bf))
-def inner_adam_kernel(f_ref,g0_ref,g1_ref,ada_ref,w_ref,m_ref,v_ref,*outs):
+def inner_adam_kernel(f_ref,a0_ref,m0_ref,a1_ref,m1_ref,ada_ref,w_ref,m_ref,v_ref,*outs):
     factor=f_ref[0]; l=pl.program_id(0); j=pl.program_id(1)
     def put(sl,g):
         for o,val in zip(outs,adam_update(w_ref[0,:,sl],g,m_ref[0,:,sl],v_ref[0,:,sl],factor)): o[0,:,sl]=val
     for a in range(2):
         sl=slice(a*CW,(a+1)*CW)
-        for layer,ref in enumerate((g0_ref,g1_ref)):
-            @pl.when(jnp.logical_and(j<8,l==layer))
-            def _(): put(sl,ref[0,a])
+        for layer,refs in enumerate(((a0_ref,m0_ref),(a1_ref,m1_ref))):
+            for part,ref in enumerate(refs):
+                @pl.when(jnp.logical_and(j//4==part,l==layer))
+                def _(): put(sl,ref[0,a])
         @pl.when(j>=8)
         def _(): put(sl,ada_ref[0,:,sl])
-def inner_adam(factor,g0,g1,ada,w,m,v):
+def inner_adam(factor,grads,ada,w,m,v):
     own=w.shape[1]; C=w.shape[2]; W=2*CW
     blk=pl.BlockSpec((1,own,W),lambda l,j:(l,0,j))
-    def gmap(layer):
+    def gmap(layer,part):
         def index(l,j):
-            jj=jnp.minimum(j,7); on=jnp.where(l==layer,jj,7*(l>layer))
-            return (2-on//4, on%4, 0, 0)
+            jj=jnp.clip(j-4*part,0,3); on=jnp.where(l==layer,jj,3*(l>layer))
+            return (part,on,0,0)
         return pl.BlockSpec((1,2,own,CW),index)
     sd=jax.ShapeDtypeStruct
     return pl.pallas_call(inner_adam_kernel,grid=(LAYERS,C//W),
-        in_specs=[pl.BlockSpec(memory_space=pltpu.SMEM),gmap(0),gmap(1),pl.BlockSpec((1,own,W),lambda l,j:(l,0,jnp.maximum(j-8,0))),blk,blk,blk],
+        in_specs=[pl.BlockSpec(memory_space=pltpu.SMEM)]+[gmap(l,p) for l in range(2) for p in range(2)]+[pl.BlockSpec((1,own,W),lambda l,j:(l,0,jnp.maximum(j-8,0))),blk,blk,blk],
         out_specs=[blk]*4,out_shape=[sd(w.shape,f32)]*3+[sd(w.shape,bf)],
-        compiler_params=pltpu.CompilerParams(vmem_limit_bytes=VLIM))(factor,g0,g1,ada,w,m,v)
+        compiler_params=pltpu.CompilerParams(vmem_limit_bytes=VLIM))(factor,*grads,ada,w,m,v)
 def outer_adam_kernel(f_ref,g0_ref,g1_ref,b_ref,w_ref,m_ref,v_ref,*outs):
     factor=f_ref[0]; l=pl.program_id(0); j=pl.program_id(1)
     def put(sl,g):
@@ -639,12 +965,7 @@
     freq=jnp.exp(-math.log(10000.0)*jnp.arange(half,dtype=f32)/half)
     ang=steps.astype(f32)[:,None]*freq[None,:]
     return jnp.concatenate([jnp.cos(ang),jnp.sin(ang)],axis=1)
-def modulate(x, sh, sc):
-    c=x-jnp.mean(x,axis=-1,keepdims=True)
-    v=jnp.mean(c*c,axis=-1,keepdims=True)
-    return c*lax.rsqrt(v+norm_eps)*(1.0+sc[:,None,:])+sh[:,None,:]
 def dot32(pattern,a,b): return jnp.einsum(pattern,a,b,preferred_element_type=f32)
-def silu_back(v,g): return jax.vjp(jax.nn.silu,v)[1](g)[0]
 ALL=("rep","shard")
 
 def per_device(latents,target_noise,labels,time_steps,inner_weights,outer_weights,embed_table,final_mod,head_weights,
@@ -678,17 +999,17 @@
         return jnp.swapaxes(a,-4,-3).reshape(a.shape[:-4]+(N,a.shape[-1]))
     rows_all=latent_order(rows_all.reshape(S*R*8,384))
     features=rows_all[:,:FREQ].astype(bf)
-    hot=rows_all[:,FREQ:FREQ+1]==jnp.arange(NCLASS,dtype=jnp.int32).astype(f32)[None,:]
-    hidden=latent_order(hidden); condition=latent_order(condition)
-    wide=lambda a: latent_order(a).transpose(1,0,2).reshape(N,D)
-    time_act=wide(time_act); cond_all=wide(cond_all)
-    cond_own=lax.dynamic_slice_in_dim(cond_all,shard*own,own,1)
+    label_col=rows_all[:,FREQ:FREQ+1]
+    before=latent_order(jnp.stack([hidden,condition])).transpose(0,2,1)
+    wide=latent_order(jnp.stack([time_act,cond_all])).transpose(0,2,1,3).reshape(2,N,D)
+    time_act=wide[0]; cond_all=wide[1]
+    cond_own=lax.dynamic_slice_in_dim(cond_all,shard*own,own,1).T
     small=small.transpose(1,0,2).reshape(48,D)
     biases=small[:LAYERS*BIAS].reshape(LAYERS,BIAS,D).astype(f32)
     patch_w=small[LAYERS*BIAS:LAYERS*BIAS+P_SIZE]; patch_b=small[LAYERS*BIAS+P_SIZE].astype(f32)
     modul=modul.reshape(LAYERS,LAT_DEV,6,D)+biases[:,None,7:13]
     modul=jnp.pad(modul,((0,0),(0,0),(0,2),(0,0)))
-    fin_mod=fin_mod[:,:LAT_DEV].transpose(1,0,2).reshape(LAT_DEV,2*D)
+    fin_mod=fin_mod[:,:LAT_DEV].transpose(1,0,2).reshape(LAT_DEV,2,D)
     ramp=0.0001+(0.02-0.0001)*jnp.arange(1000,dtype=f32)/999.0
     upto=jnp.arange(1000,dtype=jnp.int32)[None,:]<=time_steps[:,None]
     abar=jnp.exp(jnp.sum(jnp.where(upto,jnp.log(1.0-ramp)[None,:],0.0),axis=1))
@@ -698,92 +1019,58 @@
     saved=[]
     gathered=[unit_blocks(gather0,R)]
     for l in range(LAYERS):
-        wa,w1,w2=gathered[l]
+        full_w=gathered[l]
         bias=jnp.pad(biases[l],((0,2),(0,0)))
         if l==0:
-            o,gather1=layer_fwd_gather(stream,modul[l],bias,wa,w1,w2,slab(1),R,S,1)
+            o,gather1=layer_fwd_gather(stream,modul[l],bias,full_w,slab(1),R,S,1)
             gathered.append(unit_blocks(gather1,R))
-        else: o=layer_fwd(stream,modul[l],bias,wa,w1,w2)
+        else: o=layer_fwd(stream,modul[l],bias,full_w)
         saved.append((stream,)+tuple(o))
         stream=o[-1]
-    stream3=stream.reshape(LAT_DEV,TOK,D)
-    fin_shift,fin_scale=jnp.split(fin_mod,2,axis=1)
-    fin_normed=modulate(stream3,fin_shift,fin_scale).astype(bf)
-    output=dot32("gtd,dp->gtp",fin_normed,head_low[:D])+head_low[D].astype(f32)
-    differ=output-jnp.swapaxes(target_noise,1,2)
-    loss_part=jnp.sum(differ*differ)/count
-    grad_output=2.0*(differ*(1.0/count))
-    head_bias=jnp.sum(grad_output,axis=(0,1))
-    output_low=grad_output.astype(bf)
-    head_grad=jnp.concatenate([dot32("gtd,gtp->dp",fin_normed,output_low),head_bias[None]],axis=0)
-    grad_fin_normed=dot32("gtp,dp->gtd",output_low,head_low[:D])
-    grad_stream,g_shift,g_scale=jax.vjp(modulate,stream3,fin_shift,fin_scale)[1](grad_fin_normed)
-    grad_stream=grad_stream.reshape(LAT_DEV*TOK,D)
-    grad_fin=jnp.concatenate([g_shift,g_scale],axis=1)
-    ada_parts=[None]*LAYERS; bias_grads=[None]*LAYERS; operands=[None]*LAYERS; gathered_rows=[None]*LAYERS
-    for l in range(LAYERS-1,-1,-1):
-        wa,w1,w2=gathered[l]
+    grad_stream,grad_fin,head_rows=head(stream,fin_mod,head_low[:D],head_low[D:].astype(f32),target_noise,1.0/count)
+    def mlp_parts(l,g):
         x,normed,qkv,lse,mixed,attn,mid,ntwo,upper,activ,down,_=saved[l]
-        dlow,ulow,gmid,alow,gmix,dm1,db1=layer_bwd_mlp(grad_stream,modul[l],wa,w1,w2,down,upper,mid,attn)
-        low,grad_stream,dm2,db2=layer_bwd_attn(gmix,alow,gmid,modul[l],wa,qkv,lse,x)
-        operands[l]=((dlow,ntwo,normed,mixed),(activ,ulow,low))
-        dmod=jnp.concatenate([dm2[:,:2],dm1[:,2:6]],axis=1)
-        mod_rows=dmod.astype(bf).reshape(LAT_DEV,6*D)
-        if l==LAYERS-1: mod_rows=jnp.concatenate([mod_rows,grad_fin.astype(bf)],axis=1)
-        mod_rows=lax.all_gather(mod_rows,ALL,axis=0,tiled=True)
-        gathered_rows[l]=mod_rows
-        bias_grads[l]=jnp.concatenate([db2[0:2],db1[2:7],jnp.sum(dmod,axis=0),db1[13:14]],axis=0)
-    ops1,late=lax.optimization_barrier((operands[1],gathered_rows[1]))
+        return bwd_mlp_parts(g,modul[l],gathered[l],down,upper,mid,attn)
+    def attn_parts(l,gmix,alow,gmid):
+        x,normed,qkv,lse,mixed,attn,mid,ntwo,upper,activ,down,_=saved[l]
+        return bwd_attn_parts(gmix,alow,gmid,modul[l],gathered[l],qkv,lse,x)
+    mod_grad=lambda dm1,dm2: jnp.concatenate([dm2[:,:2],dm1[:,2:6]],axis=1).astype(bf).reshape(LAT_DEV,6*D)
+    def mlp_sums(l,dlow,ulow): return (dlow,saved[l][7]),(saved[l][9],ulow)
+    def attn_sums(l,low): return (saved[l][1],saved[l][4]),(low,)
+    dlow,ulow,gmid,alow,gmix,dm1_1,db1_1=plain(*mlp_parts(1,grad_stream))
+    (low,grad_stream,dm2_1,db2_1),held,_,_=carry(R,S,2,*mlp_sums(1,dlow,ulow),MLP_X,(),*attn_parts(1,gmix,alow,gmid))
+    late=jnp.concatenate([mod_grad(dm1_1,dm2_1),grad_fin.astype(bf).reshape(LAT_DEV,2*D)],axis=1)
+    (dlow,ulow,gmid,alow,gmix,dm1_0,db1_0),held,(mlp1,sq_a),(late,)=carry(R,S,3,*attn_sums(1,low),ATTN_X,(held,),*mlp_parts(0,grad_stream),
+        extra=rows_extra(late.reshape(16,8*D*LAT_DEV//16),R,S))
+    (low,grad_stream,dm2_0,db2_0),held,(attn1,sq_b),_=carry(R,S,4,*mlp_sums(0,dlow,ulow),MLP_X,(held,),*attn_parts(0,gmix,alow,gmid))
+    late=late.reshape(N,8*D)
     fin_mine=lax.dynamic_slice_in_dim(late,6*D+shard*fin_cols,fin_cols,1)
-    final_main=dot32("nd,ne->de",cond_all,fin_mine)
-    fin_part=dot32("ne,de->nd",fin_mine,final_low[:D])
-    fin_part,ops1=lax.optimization_barrier((fin_part,ops1))
-    grad_cond=lax.psum_scatter(fin_part,"shard",scatter_dimension=1,tiled=True)
-    grads1=layer_grads(R,S,LAYERS+1,*ops1)
-    grads1,grad_cond,early=lax.optimization_barrier((grads1,grad_cond,gathered_rows[0]))
-    for l,mod_rows in ((0,early),(1,late[:,:6*D])):
-        ada_parts[l]=dot32("nd,ne->de",cond_own,mod_rows)
-        grad_cond=grad_cond+dot32("ne,de->nd",mod_rows,ada_own[l])
     gs=grad_stream.reshape(LAT_DEV,TOK,D)
     patch_grad=dot32("gpt,gtd->pd",patches,gs.astype(bf))
-    patch_bias=jnp.sum(grad_stream,axis=0)
-    fin_bias_sum=jnp.sum(grad_fin,axis=0).reshape(2,D)
-    tail=jnp.zeros((1,D),f32).at[0,0].set(loss_part)
-    head_flat=head_grad.reshape(-1)
-    head_rows=-(-head_flat.shape[0]//D)
-    head_flat=jnp.pad(head_flat,(0,head_rows*D-head_flat.shape[0])).reshape(head_rows,D)
-    local_sums=(jnp.concatenate(bias_grads+[patch_grad,patch_bias[None],fin_bias_sum,head_flat,tail],axis=0))
-    grad_condition=silu_back(condition,grad_cond)
-    b2=jnp.sum(grad_condition,axis=0)
-    clow=grad_condition.astype(bf)
-    second=dot32("nd,ne->de",time_act,clow)
-    class_grad=jnp.einsum("nc,nd->cd",hot.astype(f32),grad_condition,precision=lax.Precision.HIGHEST)
-    time_part=dot32("ne,ed->nd",clow,second_w)
-    time_part,ops0,local_sums=lax.optimization_barrier((time_part,operands[0],local_sums))
-    sums=lax.psum(local_sums,ALL)
-    grad_time_act=lax.psum_scatter(time_part,"shard",scatter_dimension=1,tiled=True)
-    grads0=layer_grads(R,S,LAYERS,*ops0)
-    grads0,grad_time_act,sums=lax.optimization_barrier((grads0,grad_time_act,sums))
-    o1=LAYERS*BIAS; o2=o1+P_SIZE+1; o3=o2+2; o4=o3+head_rows
-    mean_loss=sums[o4,0]
-    head_total=sums[o3:o4].reshape(-1)[:(D+1)*P_SIZE].reshape(D+1,P_SIZE)
-    fin_bias_own=lax.dynamic_slice_in_dim(sums[o2:o3].reshape(2*D),shard*fin_cols,fin_cols,0)
-    mine=lax.dynamic_slice_in_dim(sums[:o2],shard*own,own,1)
-    grad_time=silu_back(hidden,grad_time_act)
-    first=dot32("nf,nd->fd",features,grad_time.astype(bf))
-    embed_grad=jnp.concatenate([mine[o1:o2],first,jnp.sum(grad_time,axis=0)[None],second,b2[None],class_grad],axis=0)
-    final_grad=jnp.concatenate([final_main,fin_bias_own[None]],axis=0)
-    ada_grad=jnp.stack(ada_parts)
-    bias_grad=jnp.pad(mine[:o1].reshape(LAYERS,BIAS,own),((0,0),(0,2),(0,0)))
-    sq=lambda a: jnp.sum(a*a)
-    square=lax.psum(sq(grads0)+sq(grads1)+sq(ada_grad)+sq(bias_grad)+sq(embed_grad)+sq(final_grad),"shard")
-    grad_norm=jnp.sqrt(square+sq(head_total))
+    patch_bias=jnp.sum(grad_stream,axis=0)[None]
+    o1=LAYERS*BIAS; o2=o1+P_SIZE+1
+    cond_back=lambda squares: cond_extra((late,fin_mine,cond_own,cond_all,time_act,before,label_col,features,ada_own,final_low[:D].reshape(S,own,fin_cols),
+        second_w.reshape(own,S,own).transpose(1,0,2),mod_grad(dm1_0,dm2_0).reshape(16,6*D*LAT_DEV//16),
+        db1_0,db2_0,dm1_0,dm2_0,db1_1,db2_1,dm1_1,dm2_1,patch_grad,patch_bias,grad_fin,head_rows,squares),R,S)
+    squares=sq_a+sq_b
+    if N<=256: mlp0,_,attn0,_,*rest=last_call(R,S,5,*attn_sums(0,low),(held,),cond_back(squares))
+    else:
+        mlp0,sq_c,attn0,sq_d=sums_call(R,S,5,*attn_sums(0,low),(held,))
+        rest=last_call(R,S,6,(),(),(),cond_back(squares+sq_c+sq_d))
+    ada_grad,final_turn,second,class_grad,first_grad,vectors,mine,head_total,norm_parts=rest
+    head_total=head_total.transpose(2,0,1,3).reshape(HEAD_ROWS,D)
+    mean_loss=jnp.sum(head_total[HEAD_ROWS-1,:P_SIZE])/count
+    head_total=jnp.concatenate([head_total[:P_SIZE],head_total[P_SIZE,:P_SIZE][:,None]],axis=1).T
+    embed_grad=jnp.concatenate([mine[o1:o2].T,first_grad,vectors[1,:,:1],second,vectors[0,:,:1],class_grad[:,:NCLASS]],axis=1)
+    final_turn=jnp.concatenate([final_turn,mine[o2:o2+fin_cols//own].reshape(fin_cols)[:,None]],axis=1)
+    bias_grad=mine[:o1].reshape(LAYERS,BIAS,own)
+    grad_norm=jnp.sqrt(jnp.sum(norm_parts))
     factor=jnp.minimum(1.0,clip_coef*math.sqrt(D/count)/grad_norm)
     out=[mean_loss,grad_norm]
-    out.extend(inner_adam(factor.reshape(1),grads0,grads1,ada_grad,inner_weights,inner_moment,inner_square))
-    bias_turn=jnp.pad(bias_grad.transpose(0,2,1),((0,0),(0,0),(0,112)))
-    out.extend(outer_turn(a) for a in outer_adam(factor.reshape(1),grads0,grads1,bias_turn,outer_turn(outer_weights),outer_turn(outer_moment),outer_turn(outer_square)))
-    for w,g,m,v in ((embed_table,embed_grad,embed_moment,embed_square),(final_mod,final_grad,final_moment,final_square),
+    out.extend(inner_adam(factor.reshape(1),(attn0,mlp0,attn1,mlp1),ada_grad,inner_weights,inner_moment,inner_square))
+    bias_turn=jnp.pad(bias_grad.transpose(0,2,1),((0,0),(0,0),(0,128-BIAS)))
+    out.extend(outer_turn(a) for a in outer_adam(factor.reshape(1),mlp0,mlp1,bias_turn,outer_turn(outer_weights),outer_turn(outer_moment),outer_turn(outer_square)))
+    for w,g,m,v in ((embed_table,embed_grad.T,embed_moment,embed_square),(final_mod,final_turn.T,final_moment,final_square),
                     (head_weights,head_total,head_moment,head_square)):
         out.extend(adam_update(w,g,m,v,factor))
     return tuple(out)

time: 919 us -> 666 us (0.72)
  waiting for transfers between devices: 107 us -> 0 us
  local copies, waits for them, and re-layouts: 112 us -> 45.2 us
  other arithmetic: 52.8 us -> 29.4 us
  matrix products: 25.6 us -> 3.21 us
  between operations: 22.7 us -> 5.29 us
  blocking collectives: 14.4 us -> 0 us
    all_gather x2 -> x0, waiting for transfers between devices: 58.5 us -> none  [per_device(): mod_rows = lax.all_gather(mod_rows, ALL, axis=0, tiled=True)]
    psum x1 -> x0, waiting for transfers between devices: 47.9 us -> none  [per_device(): sums = lax.psum(local_sums, ALL)]
    slice x33 -> x15, local copies, waits for them, and re-layouts: 50.9 us -> 9.04 us  [the longest x2 1.81 us: per_device(): dm1[:, 2:6]]
    dot_general x14 -> x2, matrix products: 23.6 us -> 3.21 us  [dot32(): return jnp.einsum(pattern, a, b, preferred_element_type=f32)]
    psum x1 -> x0, blocking collectives: 14.4 us -> none  [per_device(): lax.psum(sq(grads0) + sq(grads1) + sq(ada_grad) + sq(bias_grad) + sq(embe...]
    reduce_sum x13 -> x2, other arithmetic: 17.5 us -> 4.63 us  [the longest x1 3.21 us: per_device(): patch_bias = jnp.sum(grad_stream, axis=0)[None]]
    unnamed x115 -> x39, local copies, waits for them, and re-layouts: 12 us -> 2.2 us
  transfers between devices with their start and end apart: 5 -> 0, of which waited for: 3 -> 0; matrix products, arithmetic and copies ran while one was open for 8% -> 0% of each run, Pallas kernels for 24% -> 0%
where the time goes in v4:
time: 666 us; the launch traced here: 655 us
  Pallas kernels  572 us (86%)
  local copies, waits for them, and re-layouts  45.2 us (7%)
  other arithmetic  29.4 us (4%)
    pallas_call x3, Pallas kernels, carry(): pl.pallas_call(functools.partial(carrier_kernel, R, nz, own, nu, xi, nt,...  206 us
    pallas_call x1, Pallas kernels, last_call(): pl.pallas_call(functools.partial(last_kernel, R, nz, own, sums, nt, f, le...  90.5 us
    pallas_call x1, Pallas kernels, first_call(): pl.pallas_call(functools.partial(first_kernel, R, nz, U, own), in_specs=[...  86.6 us
    pallas_call x1, Pallas kernels, layer_fwd_gather(): pl.pallas_call(functools.partial(fwd_gather_kernel, R, nz, U), grid=(n,),...  76.5 us
    pallas_call x1, Pallas kernels, layer_fwd(): pl.pallas_call(fwd_kernel, grid=(n,), in_specs=[rows(D), pl.BlockSpec((1,...  36.4 us
    pallas_call x1, Pallas kernels, inner_adam(): pl.pallas_call(inner_adam_kernel, grid=(LAYERS, C // W), in_specs=[pl.Blo...  32.6 us
    pallas_call x1, Pallas kernels, plain(): pl.pallas_call(kernel, grid=(args[0].shape[0] // TOK,), in_specs=specs, o...  25.9 us

profile of v4, /device:TPU:0, one launch (start us, length us, event | category | flops | bytes accessed | tf_op | source)
XLA Modules:
  0.0 654.8 jit_solution(6524354265519879541)
XLA Ops:
  3.0 0.8 select_reduce_fusion
  3.9 1.0 add_convert_fusion
  4.8 0.9 slice.229
  6.4 1.0 copy.128
  8.6 1.1 slice.228
  9.7 0.9 copy.160
  13.8 1.1 reshape.197
  15.7 1.9 multiply_sine_fusion.1
  17.6 1.1 pad_maximum_fusion.2
  20.3 3.7 convert_element_type.115
  24.0 1.3 slice.227.ada_ref.refs_12_
  26.0 1.4 copy.158
  27.4 1.4 copy.157
  28.8 86.6 %shard_map.354 = (bf16[3,4,4,2,96,768]{5,4,3,2,1,0:T(8,128)(2,1)}, f32[8,4,8,384]{3,2,1,0:T(8,128)}, bf16[8,48,96]{2,1,0:T(8,128)(2,1)}, f32[256,96]{1,0:T(8,128...) custom-call(bf16[3,4,96,768]{3,2,1,0:T(8,128)(2,1)} %bitcast.136, ...), custom_call_target="tpu_custom_call" | custom-call | tf_op jit(solution)/shard_map/pallas_call | solution.py:370
  117.2 0.9 slice_convert_fusion.1
  118.1 0.8 slice_bitcast_fusion.3
  121.3 1.0 pad_maximum_fusion.4
  126.9 0.8 copy.138.refs_8_
  128.5 0.8 copy.137.refs_7_
  129.4 2.3 add_add_fusion
  131.6 76.5 %shard_map.355 = (bf16[1024,768]{1,0:T(8,128)(2,1)}, bf16[1024,2304]{1,0:T(8,128)(2,1)}, f32[1024,128]{1,0:T(8,128)}, bf16[1024,768]{1,0:T(8,128)(2,1)}, f32[102...) custom-call(f32[1024,768]{1,0:T(8,128)} %bitcast.131, ...), custom_call_target="tpu_custom_call" | custom-call | flops 15300820992 | bytes 60000000 | tf_op jit(solution)/shard_map/pallas_call | solution.py:403
  208.1 36.4 %shard_map.356 = (bf16[1024,768]{1,0:T(8,128)(2,1)}, bf16[1024,2304]{1,0:T(8,128)(2,1)}, f32[1024,128]{1,0:T(8,128)}, bf16[1024,768]{1,0:T(8,128)(2,1)}, f32[102...) custom-call(f32[1024,768]{1,0:T(8,128)} %get-tuple-element.111.x_ref, ...), custom_call_target="tpu_custom_call" | custom-call | flops 15300820992 | bytes 60000000 | tf_op jit(solution)/shard_map/pallas_call | solution.py:86
  244.5 6.9 %shard_map.357 = (f32[1024,768]{1,0:T(8,128)}, f32[4,2,768]{2,1,0:T(2,128)}, f32[24,768]{1,0:T(8,128)}) custom-call(f32[1024,768]{1,0:T(8,128)} %get-tuple-element.113.x_ref, f32[4,2,768]{2,1,0:T(2,128)} %reshape.204.fm_ref, bf16[768,16]{1,0:T(8,128)(2,1)} %slice.239.hw_ref, f32[1,16]{1,0:T(1,128)} %slice_convert_fusion.7.hb_ref, f32[4,16,256]{2,1,0:T(8,128)} %tn_ref.1), custom_call_target="tpu_custom_call" | custom-call | tf_op jit(solution)/shard_map/pallas_call | solution.py:889
  251.5 25.9 %shard_map.358 = (bf16[1024,768]{1,0:T(8,128)(2,1)}, bf16[1024,3072]{1,0:T(8,128)(2,1)}, f32[1024,768]{1,0:T(8,128)}, bf16[1024,768]{1,0:T(8,128)(2,1)}, bf16[10...) custom-call(f32[1024,768]{1,0:T(8,128)} %get-tuple-element.115.g_ref, ...), custom_call_target="tpu_custom_call" | custom-call | flops 10871635968 | bytes 50000000 | tf_op jit(solution)/shard_map/pallas_call | solution.py:139
  277.4 68.8 %shard_map.359 = (bf16[1024,3072]{1,0:T(8,128)(2,1)}, f32[1024,768]{1,0:T(8,128)}, f32[4,8,768]{2,1,0:T(8,128)}, f32[8,768]{1,0:T(8,128)}, f32[2,2,4,96,384]{4,3,2,1,0:T(8,128)}) custom-call(bf16[1024,768]{1,0:T(8,128)(2,1)} %get-tuple-element.120.refs_0_, bf16[1024,768]{1,0:T(8,128)(2,1)} %get-tuple-element.121.refs_1_, ...), custom_call_target="tpu_custom_call" | custom-call | flops 5637144576 | bytes 25000000 | tf_op jit(solution)/shard_map/pallas_call | solution.py:621
  346.1 0.9 slice.283
  347.1 0.9 slice.281
  348.7 67.5 %shard_map.360 = (bf16[1024,768]{1,0:T(8,128)(2,1)}, bf16[1024,3072]{1,0:T(8,128)(2,1)}, f32[1024,768]{1,0:T(8,128)}, bf16[1024,768]{1,0:T(8,128)(2,1)}, bf16[10...) custom-call(f32[1024,768]{1,0:T(8,128)} %get-tuple-element.129.refs_, ...), custom_call_target="tpu_custom_call" | custom-call | flops 10871635968 | bytes 50000000 | tf_op jit(solution)/shard_map/pallas_call | solution.py:621
  416.3 69.4 %shard_map.361 = (bf16[1024,3072]{1,0:T(8,128)(2,1)}, f32[1024,768]{1,0:T(8,128)}, f32[4,8,768]{2,1,0:T(8,128)}, f32[8,768]{1,0:T(8,128)}, f32[2,2,4,96,384]{4,3...) custom-call(bf16[1024,768]{1,0:T(8,128)(2,1)} %get-tuple-element.141.refs_0_, ...), custom_call_target="tpu_custom_call" | custom-call | flops 5637144576 | bytes 25000000 | tf_op jit(solution)/shard_map/pallas_call | solution.py:621
  485.7 1.3 add.138.refs_28_
  487.0 0.9 slice.282
  487.9 0.9 slice.280
  489.5 2.7 reshape.207.refs_4_
  492.3 0.8 constant_dynamic-slice_fusion.refs_5_
  493.1 3.2 fusion.26
  496.9 0.9 convolution_bitcast_fusion.refs_24_
  497.9 90.5 %shard_map.362 = (f32[2,8,96,384]{3,2,1,0:T(8,128)}, f32[8,128]{1,0:T(8,128)}, f32[1,8,96,384]{3,2,1,0:T(8,128)}, f32[8,128]{1,0:T(8,128)}, f32[2,96,4608]{2,1,0...) custom-call(bf16[1024,768]{1,0:T(8,128)(2,1)} %get-tuple-element.109, ...), custom_call_target="tpu_custom_call" | custom-call | tf_op jit(solution)/shard_map/pallas_call | solution.py:665
  588.4 1.4 reduce_sum.39
  593.4 0.8 slice.250
  594.3 0.9 copy.139
  598.3 0.8 broadcast_in_dim_reshape.4
  599.1 1.5 slice_bitcast_fusion.1
  600.6 1.6 concatenate.46
  602.2 1.6 fusion.18
  603.8 3.3 fusion.20
  607.1 1.9 fusion.22
  609.0 10.6 %shard_map.364 = (f32[2,96,3086]{2,1,0:T(8,128)}, f32[2,96,3086]{2,1,0:T(8,128)}, f32[2,96,3086]{2,1,0:T(8,128)}, bf16[2,96,3086]{2,1,0:T(8,128)(2,1)}) custom-call(f32[1]{0:T(128)} %bitcast.36.f_ref, f32[2,8,96,384]{3,2,1,0:T(8,128)} %get-tuple-element.172.m0_ref.g0_ref, f32[2,8,96,384]{3,2,1,0:T(8,128)} %get-tuple-element.174.m1_ref.g1_ref, ...), custom_call_target="tpu_custom_call" | custom-call | tf_op jit(solution)/shard_map/pallas_call | solution.py:949
  619.6 32.6 %shard_map.363 = (f32[2,96,10752]{2,1,0:T(8,128)}, f32[2,96,10752]{2,1,0:T(8,128)}, f32[2,96,10752]{2,1,0:T(8,128)}, bf16[2,96,10752]{2,1,0:T(8,128)(2,1)}) custom-call(f32[1]{0:T(128)} %bitcast.36.f_ref, f32[1,8,96,384]{3,2,1,0:T(8,128)} %get-tuple-element.171.a0_ref, f32[2,8,96,384]{3,2,1,0:T(8,128)} %get-tuple-element.172.m0_ref.g0_ref, ...), custom_call_target="tpu_custom_call" | custom-call | tf_op jit(solution)/shard_map/pallas_call | solution.py:925
  (121 shorter events, 27.0 us)
Async XLA Ops:
  0.7 10.0 %copy-start.2 = (f32[2043,96]{0,1:T(8,128)S(1)}, f32[2043,96]{0,1:T(8,128)}, u32[]{:S(2)}) copy-start(f32[2043,96]{0,1:T(8,128)} %param.25) | copy-start | bytes 2353540
  10.7 2.3 copy-start.4
  10.7 8.0 %copy-start = (f32[2,3086,96]{1,2,0:T(8,128)S(1)}, f32[2,3086,96]{1,2,0:T(8,128)}, u32[]{:S(2)}) copy-start(f32[2,3086,96]{1,2,0:T(8,128)} %param.24) | copy-start | bytes 7110148
  18.7 0.7 slice-start
  115.4 7.7 %copy-start.12 = (f32[8,4608]{1,0:T(8,128)S(1)}, f32[8,4608]{1,0:T(8,128)}, u32[]{:S(2)}) copy-start(f32[8,4608]{1,0:T(8,128)} %get-tuple-element.107) | copy-start | bytes 442372
  115.4 8.4 %copy-start.14 = (f32[8,4,8,384]{3,2,1,0:T(8,128)S(1)}, f32[8,4,8,384]{3,2,1,0:T(8,128)}, u32[]{:S(2)}) copy-start(f32[8,4,8,384]{3,2,1,0:T(8,128)} %get-tuple-element.158) | copy-start | bytes 1179652
  119.6 5.6 copy-start.11
  120.6 5.3 copy-start.10
  125.9 3.5 copy-start.3
  277.4 69.7 %copy-start.13 = (f32[4,2,768]{2,1,0:T(2,128)S(1)}, f32[4,2,768]{2,1,0:T(2,128)}, u32[]{:S(2)}) copy-start(f32[4,2,768]{2,1,0:T(2,128)} %get-tuple-element.140.refs_26_) | copy-start | bytes 73732
  416.3 69.5 %copy-start.15 = (f32[8,128]{1,0:T(8,128)S(1)}, f32[8,128]{1,0:T(8,128)}, u32[]{:S(2)}) copy-start(f32[8,128]{1,0:T(8,128)} %get-tuple-element.167) | copy-start | bytes 12292
  492.3 5.6 copy-start.1
  588.4 15.4 %copy-start.5 = (f32[769,192]{0,1:T(8,128)S(1)}, f32[769,192]{0,1:T(8,128)}, u32[]{:S(2)}) copy-start(f32[769,192]{0,1:T(8,128)} %param.26) | copy-start | bytes 1771780
  588.4 15.3 %copy-start.8 = (f32[769,192]{0,1:T(8,128)S(1)}, f32[769,192]{0,1:T(8,128)}, u32[]{:S(2)}) copy-start(f32[769,192]{0,1:T(8,128)} %param.34) | copy-start | bytes 1771780
  588.4 15.3 %copy-start.9 = (f32[192,768]{1,0:T(8,128)S(1)}, f32[192,768]{1,0:T(8,128)}, u32[]{:S(2)}) copy-start(f32[192,768]{1,0:T(8,128)} %get-tuple-element.189) | copy-start | bytes 1769476
  603.8 3.3 copy-start.6
  603.8 3.3 copy-start.7

commit v5 on v4

--- a/solution.py
+++ b/solution.py
@@ -290,48 +290,53 @@
 
 def first_kernel(R,nz,U,own, w_ref,fo_ref,sm_ref,t1_ref,t2_ref,cls_ref,tb_ref,ada_ref,fin_ref,finb_ref,
                  out_ref,f_ref,sg_ref,hid_ref,act_ref,con_ref,call_ref,mod_ref,fm_ref,
-                 cgs,pm,mr,ps,zrv,fps, fs1,fr1,fs2,fr2,ss,sr,as_,ar,cs_,cr_,ms,mrs,pz,pzr,vs,vr, *gsems):
-    S=2*nz; NP=S*R*8
+                 cgs,pm,mr,ps,zrv,fps, fs1,fr1,ms,mrs,pz,pzr,vs,vr, sz,szr,sc_,scr, *gsems):
+    S=2*nz; N=S*R*4
     ga=Gather(R,nz,U,w_ref,out_ref,*gsems)
     rep=lax.axis_index("rep"); shard=lax.axis_index("shard"); z=shard//2; c=lax.rem(shard,2)
     rpeer=lambda m: (jnp.bitwise_xor(rep,m),shard)
     speer=lambda k: (rep,lax.rem(shard+k,S))
+    zpeer=lambda k: (rep,2*lax.rem(z+k,nz)+c)
     mate=(rep,2*z+1-c)
     peers=[rpeer(m) for m in range(1,R)]+[speer(k) for k in range(1,S)]
     def send(src,dst,s,r,dev): return pltpu.make_async_remote_copy(src_ref=src,dst_ref=dst,send_sem=s,recv_sem=r,device_id=dev,device_id_type=MESH)
+    def far(n,ref,k): return send(ref.at[z,c],ref.at[z,c],sz.at[n,k-1],szr.at[n,k-1],zpeer(k))
+    def near(n,ref): return send(ref.at[:,c],ref.at[:,c],sc_.at[n],scr.at[n],mate)
+    def go(n,ref):
+        for k in range(1,nz): far(n,ref,k).start()
+    def turn(n,ref):
+        for k in range(1,nz): far(n,ref,k).wait_recv()
+        near(n,ref).start()
+    def got(n,ref): near(n,ref).wait_recv()
+    small=((0,f_ref),(1,sg_ref),(2,act_ref),(3,call_ref))
     meet(peers)
-    f1=lambda m: send(fo_ref,f_ref.at[shard,rep],fs1.at[m-1],fr1.at[m-1],rpeer(m))
+    f1=lambda m: send(fo_ref,f_ref.at[z,c,rep],fs1.at[m-1],fr1.at[m-1],rpeer(m))
     for m in range(1,R): f1(m).start()
-    smc=lambda k: send(sm_ref,sg_ref.at[shard],ss.at[k-1],sr.at[k-1],speer(k))
+    f_ref[z,c,rep]=fo_ref[...]
+    sg_ref[z,c]=sm_ref[...]
+    for m in range(1,R): f1(m).wait_recv()
+    go(*small[0]); go(*small[1])
     ga.start(); ticks=ga.ticks()
-    f_ref[shard,rep]=fo_ref[...]
-    sg_ref[shard]=sm_ref[...]
-    for m in range(1,R): f1(m).wait_recv()
-    f2=lambda k: send(f_ref.at[shard],f_ref.at[shard],fs2.at[k-1],fr2.at[k-1],speer(k))
-    for k in range(1,S): f2(k).start()
-    for k in range(1,S): smc(k).start()
-    for t in ticks[:U]: t()
-    for k in range(1,S): f2(k).wait_recv()
-    feats=f_ref[...].reshape(NP,384)
+    turn(*small[0]); turn(*small[1])
+    got(*small[0])
+    feats=jnp.concatenate([f_ref[s//2,s%2,r,:4] for s in range(S) for r in range(R)],axis=0)
     hidden=mm_nt(feats[:,:256].astype(bf),t1_ref[...])+tb_ref[0:1,:]
     hid_ref[...]=hidden
-    act_ref[shard]=(hidden/(1.0+jnp.exp(-hidden))).astype(bf)
-    ac=lambda k: send(act_ref.at[shard],act_ref.at[shard],as_.at[k-1],ar.at[k-1],speer(k))
-    for k in range(1,S): ac(k).start()
+    act_ref[z,c]=(hidden/(1.0+jnp.exp(-hidden))).astype(bf)
+    go(*small[2])
+    for t in ticks[:U]: t()
     hot=(feats[:,256:257].astype(jnp.int32)==lax.broadcasted_iota(jnp.int32,(1,cls_ref.shape[1]),1))
     con=mm_nt(jnp.where(hot,1.0,0.0).astype(bf),cls_ref[...])
-    for t in ticks[U:2*U]: t()
-    for k in range(1,S): ac(k).wait_recv()
-    sec=mm_nt(act_ref[0],t2_ref[0])
-    for s in range(1,S): sec=sec+mm_nt(act_ref[s],t2_ref[s])
+    turn(*small[2]); got(*small[2])
+    sec=mm_nt(act_ref[0,0],t2_ref[0])
+    for s in range(1,S): sec=sec+mm_nt(act_ref[s//2,s%2],t2_ref[s])
     con=(sec+tb_ref[1:2,:])+con
     con_ref[...]=con
     cond=con/(1.0+jnp.exp(-con))
-    call_ref[shard]=cond.astype(bf)
-    cc=lambda k: send(call_ref.at[shard],call_ref.at[shard],cs_.at[k-1],cr_.at[k-1],speer(k))
-    for k in range(1,S): cc(k).start()
-    cgs[...]=cond.reshape(S,R,8,own)
-    cg=cgs[:,rep].reshape(S*8,own).astype(bf)
+    call_ref[z,c]=cond.astype(bf)
+    go(*small[3])
+    cgs[...]=cond.reshape(S,R,4,own)
+    cg=jnp.concatenate([v for s in range(S) for v in (cgs[s,rep],)*2],axis=0).astype(bf)
     first=lax.rem(lax.broadcasted_iota(jnp.int32,(S*8,1),0),8)<4
     for b in range(6):
         sl=slice(b*D,(b+1)*D)
@@ -339,39 +344,42 @@
         pm[:,:,:,sl]=v.reshape(nz,2,8,D)
     mc=send(pm.at[:,1-c],mr,ms,mrs,mate)
     mc.start()
-    for t in ticks[2*U:4*U]: t()
+    for t in ticks[U:U+2]: t()
     mc.wait_recv()
     ps[...]=pm[:,c]+mr[...]
-    zc=lambda k: send(ps.at[lax.rem(z+k,nz)],zrv.at[k-1],pz.at[k-1],pzr.at[k-1],(rep,2*lax.rem(z+k,nz)+c))
+    zc=lambda k: send(ps.at[lax.rem(z+k,nz)],zrv.at[k-1],pz.at[k-1],pzr.at[k-1],zpeer(k))
     for k in range(1,nz): zc(k).start()
-    for k in range(1,S): cc(k).wait_recv()
-    fp=mm(call_ref[0],fin_ref[0])
-    for s in range(1,S): fp=fp+mm(call_ref[s],fin_ref[s])
-    fps[...]=(fp+finb_ref[0:1,:]).reshape(S,R,8,fin_ref.shape[2])
+    for t in ticks[U+2:3*U]: t()
+    turn(*small[3]); got(*small[3])
+    fp=mm(call_ref[0,0],fin_ref[0])
+    for s in range(1,S): fp=fp+mm(call_ref[s//2,s%2],fin_ref[s])
+    fps[...]=(fp+finb_ref[0:1,:]).reshape(S,R,4,fin_ref.shape[2])
     vc=lambda k: send(fps.at[lax.rem(shard+k,S),rep],fm_ref.at[shard],vs.at[k-1],vr.at[k-1],speer(k))
     for k in range(1,S): vc(k).start()
     fm_ref[shard]=fps[shard,rep]
-    for t in ticks[4*U:]: t()
+    for t in ticks[3*U:]: t()
     total=ps[z]
     for k in range(1,nz): zc(k).wait_recv(); total=total+zrv[k-1]
     mod_ref[...]=total
-    for k in range(1,S): vc(k).wait_recv(); smc(k).wait_recv()
+    got(*small[1])
+    for k in range(1,S): vc(k).wait_recv(); vc(k).wait_send()
     for m in range(1,R): f1(m).wait_send()
-    for k in range(1,S):
-        for cp in (f2,smc,ac,cc,vc): cp(k).wait_send()
+    for n,ref in small:
+        near(n,ref).wait_send()
+        for k in range(1,nz): far(n,ref,k).wait_send()
     mc.wait_send()
     for k in range(1,nz): zc(k).wait_send()
     ga.finish()
 
 def first_call(w,fo,sm,t1,t2,cls,tb,ada,fin,finb,R,S,cid):
-    U,_,own,W=w.shape; nz=S//2; NP=S*R*8; FC=fin.shape[2]
+    U,_,own,W=w.shape; nz=S//2; N=S*R*4; FC=fin.shape[2]
     dma=pltpu.SemaphoreType.DMA; V=pltpu.VMEM; sd=jax.ShapeDtypeStruct
     any_=pl.BlockSpec(memory_space=pl.ANY); vm=pl.BlockSpec(memory_space=pltpu.VMEM)
     return pl.pallas_call(functools.partial(first_kernel,R,nz,U,own),
         in_specs=[vm]*10, out_specs=[any_]+[vm]*8,
-        out_shape=[sd((U,R,nz,2,own,W),bf),sd((S,R,8,384),f32),sd((S,)+sm.shape,bf),sd((NP,own),f32),sd((S,NP,own),bf),sd((NP,own),f32),sd((S,NP,own),bf),sd((8,6*D),f32),sd((S,8,FC),f32)],
-        scratch_shapes=[V((S,R,8,own),f32),V((nz,2,8,6*D),f32),V((nz,8,6*D),f32),V((nz,8,6*D),f32),V((max(nz-1,1),8,6*D),f32),V((S,R,8,FC),f32),
-            dma((R-1,)),dma((R-1,))]+[dma((S-1,))]*8+[dma(()),dma(()),dma((nz-1,)),dma((nz-1,)),dma((S-1,)),dma((S-1,))]+gather_sems(R,nz,U),
+        out_shape=[sd((U,R,nz,2,own,W),bf),sd((nz,2,R,8,384),f32),sd((nz,2)+sm.shape,bf),sd((N,own),f32),sd((nz,2,N,own),bf),sd((N,own),f32),sd((nz,2,N,own),bf),sd((8,6*D),f32),sd((S,4,FC),f32)],
+        scratch_shapes=[V((S,R,4,own),f32),V((nz,2,8,6*D),f32),V((nz,8,6*D),f32),V((nz,8,6*D),f32),V((max(nz-1,1),8,6*D),f32),V((S,R,4,FC),f32),
+            dma((R-1,)),dma((R-1,)),dma(()),dma(()),dma((nz-1,)),dma((nz-1,)),dma((S-1,)),dma((S-1,)),dma((4,nz-1)),dma((4,nz-1)),dma((4,)),dma((4,))]+gather_sems(R,nz,U),
         compiler_params=pltpu.CompilerParams(collective_id=cid,has_side_effects=True,vmem_limit_bytes=VLIM),
     )(w,fo,sm,t1,t2,cls,tb,ada,fin,finb)
 
@@ -674,10 +682,10 @@
 def rows_events(R,nz,ins,outs,scr):
     (w,),(g,)=ins,outs; rs,rr,zs,zr,cs,cr,ls=scr
     rep=lax.axis_index("rep"); shard=lax.axis_index("shard"); z=shard//2; c=lax.rem(shard,2)
-    loc=lambda: pltpu.make_async_copy(w,g.at[rep,z,c],ls)
-    rc=lambda m: remote(w,g.at[rep,z,c],rs.at[m-1],rr.at[m-1],(jnp.bitwise_xor(rep,m),shard))
-    zc=lambda k: remote(g.at[:,z,c],g.at[:,z,c],zs.at[k-1],zr.at[k-1],(rep,2*lax.rem(z+k,nz)+c))
-    cc=lambda: remote(g.at[:,:,c],g.at[:,:,c],cs,cr,(rep,2*z+1-c))
+    loc=lambda: pltpu.make_async_copy(w,g.at[z,c,rep],ls)
+    rc=lambda m: remote(w,g.at[z,c,rep],rs.at[m-1],rr.at[m-1],(jnp.bitwise_xor(rep,m),shard))
+    zc=lambda k: remote(g.at[z,c],g.at[z,c],zs.at[k-1],zr.at[k-1],(rep,2*lax.rem(z+k,nz)+c))
+    cc=lambda: remote(g.at[:,c],g.at[:,c],cs,cr,(rep,2*z+1-c))
     def a():
         loc().start()
         for m in range(1,R): rc(m).start()
@@ -695,7 +703,7 @@
     return {0:[a],1:[b],2:[d],99:[e]}
 def rows_extra(w,R,S):
     nz=S//2; dma=pltpu.SemaphoreType.DMA
-    return (rows_events,[w],[full(w.shape)],[jax.ShapeDtypeStruct((R,nz,2)+w.shape,bf)],[pl.BlockSpec(memory_space=pl.ANY)],
+    return (rows_events,[w],[full(w.shape)],[jax.ShapeDtypeStruct((nz,2,R)+w.shape,bf)],[pl.BlockSpec(memory_space=pl.ANY)],
         [dma((R-1,)),dma((R-1,)),dma((nz-1,)),dma((nz-1,)),dma(()),dma(()),dma(())])
 
 class ShardSum:
@@ -734,20 +742,21 @@
     t=v[:,:128]
     for q in range(1,v.shape[1]//128): t=t+v[:,q*128:(q+1)*128]
     return t
-HEAD_ROWS=24
+HEAD_ROWS=24; P_SIZE=16; FREQ=256; NCLASS=1000
+ROW_SECOND=P_SIZE+2+FREQ; ROW_CLASS=P_SIZE+3+FREQ+D
 FIN_ROW=45
 def cond_events(R,nz,ins,outs,scr,squares):
     (rows_ref,fin_ref,cond_ref,call_ref,act_ref,pre_ref,lab_ref,feat_ref,ada_ref,finw_ref,t2_ref,w_ref)=ins[:12]
     pieces=ins[12:-1]; sq1_ref=ins[-1]
-    adag,fing,secg,clsg,firg,vec,sumo,headg,norm_ref=outs
+    adag,fin_t,emb_t,bias_t,head_t,norm_ref=outs
     S=2*nz
     fx,tx,sx,asm=scr[0],scr[8],scr[16],scr[24]
     fs=ShardSum(nz,*scr[0:8]); ts=ShardSum(nz,*scr[8:16]); ss=ShardSum(nz,*scr[16:24])
     g0=scr[25]
     re=rows_events(R,nz,(w_ref,),(g0,),scr[26:33])
-    tot,rr,rsem,rrs,gc_s,hs,hr,hcs,hcr,nv,n1,n2,n3,nsem,nrec=scr[33:]
+    tot,rr,rsem,rrs,gc_s,hs,hr,hcs,hcr,nv,n1,n2,n3,nsem,nrec,headg=scr[33:]
     rep=lax.axis_index("rep"); shard=lax.axis_index("shard"); z=shard//2; c=lax.rem(shard,2)
-    nr=sumo.shape[0]; own=sumo.shape[1]; nb=nr-HEAD_ROWS; FC=fin_ref.shape[1]
+    nr,own=tot.shape; nb=nr-HEAD_ROWS; FC=fin_ref.shape[1]
     mate=(rep,2*z+1-c); zdev=lambda k: (rep,2*lax.rem(z+k,nz)+c); rdev=lambda m: (jnp.bitwise_xor(rep,m),shard)
     rc=lambda m: remote(tot,rr.at[rep],rsem.at[m-1],rrs.at[m-1],rdev(m))
     hz=lambda k: remote(headg.at[z,c],headg.at[z,c],hs.at[k-1],hr.at[k-1],zdev(k))
@@ -780,7 +789,9 @@
             adag[1,:,o]=mm(cond_ref[...],r)
             gc=gc+mm_nt(ada_ref[1,:,o],r)
         gc_s[...]=gc
-        fing[...]=mm_tn(fin_ref[...],call_ref[...])
+        f=mm_tn(fin_ref[...],call_ref[...])
+        fin_t[:,:D]=f
+        nv[...]=fold(f)
         fs.two(); ss.two()
     def total():
         tot[...]=ss.three()
@@ -804,29 +815,33 @@
         low=g.astype(bf)
         for s in range(S): tx[s//2,s%2]=mm_tn(t2_ref[s],low)
         ts.one()
-        vec[0]=jnp.broadcast_to(jnp.sum(g,axis=1,keepdims=True),vec.shape[1:])
-        secg[...]=mm(low,act_ref[...])
-        hot=jnp.where(lab_ref[...]==lax.broadcasted_iota(jnp.int32,(1,clsg.shape[1]),1).astype(f32),1.0,0.0)
-        clsg[...]=lax.dot_general(g,hot,(((1,),(0,)),((),())),precision=lax.Precision.HIGHEST,preferred_element_type=f32)
+        b=jnp.sum(g,axis=1,keepdims=True)
+        second=mm(low,act_ref[...])
+        emb_t[:,ROW_SECOND:ROW_SECOND+D]=second; emb_t[:,ROW_SECOND+D:ROW_SECOND+D+1]=b
+        hot=jnp.where(lab_ref[...]==lax.broadcasted_iota(jnp.int32,(1,1024),1).astype(f32),1.0,0.0)
+        table=lax.dot_general(g,hot,(((1,),(0,)),((),())),precision=lax.Precision.HIGHEST,preferred_element_type=f32)
+        emb_t[:,ROW_CLASS:ROW_CLASS+NCLASS]=table[:,:NCLASS]
+        nv[...]=nv[...]+fold(second)+fold(table)+fold(column(b))
+    def column(b):
+        return jnp.where(lax.broadcasted_iota(jnp.int32,(1,128),1)<1,jnp.broadcast_to(b,(b.shape[0],128)),0.0)
     def time_and_sums():
         ts.two()
         for m in range(1,R): rc(m).wait_recv()
         v=rr[0]
         for r in range(1,R): v=v+rr[r]
-        sumo[...]=v
         headg[z,c]=v[nb:]
         for k in range(1,nz): hz(k).start()
-        first=lax.broadcasted_iota(jnp.int32,(1,128),1)<1
-        p=fold(v[:nb])+fold(jnp.where(first,vec[0],0.0))
+        p=nv[...]+fold(v[:nb])
         for q in range(2): p=p+fold(adag[q])
-        for ref in (fing,secg,clsg): p=p+fold(ref[...])
+        for l in range(2): bias_t[l,:,0:14]=v[14*l:14*l+14].T
+        emb_t[:,0:P_SIZE+1]=v[28:28+P_SIZE+1].T
+        last=v[FIN_ROW:FIN_ROW+FC//own].T
+        for r in range(FC//own): fin_t[r*own:(r+1)*own,D:D+1]=last[:,r:r+1]
         g=sig_back(pre_ref[0],ts.three())
-        b=jnp.broadcast_to(jnp.sum(g,axis=1,keepdims=True),vec.shape[1:])
-        vec[1]=b
+        b=jnp.sum(g,axis=1,keepdims=True)
         f=mm(g.astype(bf),feat_ref[...])
-        firg[...]=f
-        p=p+fold(f)+fold(jnp.where(first,b,0.0))
-        nv[...]=jnp.where(rep==0,p,0.0)
+        emb_t[:,P_SIZE+1:P_SIZE+1+FREQ]=f; emb_t[:,P_SIZE+1+FREQ:P_SIZE+2+FREQ]=b
+        nv[...]=jnp.where(rep==0,p+fold(f)+fold(column(b)),0.0)
         for k in range(1,nz): hz(k).wait_recv()
         hc().start()
     def end():
@@ -849,17 +864,24 @@
         for m in range(1,R): nr_(m).wait()
         v=n3[0]
         for r in range(1,R): v=v+n3[r]
-        for s in range(S): v=v+fold(headg[s//2,s%2,:HEAD_ROWS-1])
-        norm_ref[...]=v
+        for s in range(S):
+            h=headg[s//2,s%2]
+            v=v+fold(h[:HEAD_ROWS-1])
+            head_t[:,s*own:(s+1)*own]=h[:P_SIZE]
+        head_t[:,D:D+1]=headg[0,0][P_SIZE:P_SIZE+1,:P_SIZE].T
+        norm=jnp.sqrt(jnp.sum(jnp.sum(v,axis=1,keepdims=True),axis=0,keepdims=True))
+        loss=jnp.sum(headg[0,0][HEAD_ROWS-1:HEAD_ROWS,:P_SIZE],axis=1,keepdims=True)
+        norm_ref[0:1,:]=jnp.broadcast_to(norm,(1,128))
+        norm_ref[1:2,:]=jnp.broadcast_to(loss,(1,128))
     return {0:re[0]+[gather],1:re[1]+[layer1],2:re[2]+[total],3:[layer0],4:[time_and_sums],99:[end]}
 def cond_extra(args,R,S):
     nz=S//2; own=D//S; N=args[2].shape[1]; nr=48+HEAD_ROWS; FC=args[1].shape[1]; w=args[11]
     vm=pl.BlockSpec(memory_space=pltpu.VMEM); sd=jax.ShapeDtypeStruct; dma=pltpu.SemaphoreType.DMA; V=pltpu.VMEM
-    shapes=[sd((2,own,6*D),f32),sd((FC,D),f32),sd((own,D),f32),sd((own,1024),f32),sd((own,256),f32),sd((2,own,128),f32),sd((nr,own),f32),sd((nz,2,HEAD_ROWS,own),f32),sd((8,128),f32)]
-    scratch=shard_sum_scratch(nz,(own,N),True)*2+shard_sum_scratch(nz,(nr,own),True)+[V((nr,D),f32),V((R,nz,2)+w.shape,bf)]
+    shapes=[sd((2,own,6*D),f32),sd((FC,D+128),f32),sd((own,2048),f32),sd((2,own,128),f32),sd((P_SIZE,D+128),f32),sd((8,128),f32)]
+    scratch=shard_sum_scratch(nz,(own,N),True)*2+shard_sum_scratch(nz,(nr,own),True)+[V((nr,D),f32),V((nz,2,R)+w.shape,bf)]
     scratch+=[dma((R-1,)),dma((R-1,)),dma((nz-1,)),dma((nz-1,)),dma(()),dma(()),dma(())]
     scratch+=[V((nr,own),f32),V((R,nr,own),f32),dma((R-1,)),dma((R-1,)),V((own,N),f32),
-        dma((nz-1,)),dma((nz-1,)),dma(()),dma(()),V((8,128),f32),V((8,128),f32),V((nz,8,128),f32),V((R,8,128),f32),dma((nz+R,)),dma((nz+R,))]
+        dma((nz-1,)),dma((nz-1,)),dma(()),dma(()),V((8,128),f32),V((8,128),f32),V((nz,8,128),f32),V((R,8,128),f32),dma((nz+R,)),dma((nz+R,)),V((nz,2,HEAD_ROWS,own),f32)]
     return (cond_events,list(args),[vm]*len(args),shapes,[vm]*len(shapes),scratch)
 
 def head_kernel(inv,x_ref,fm_ref,hw_ref,hb_ref,tn_ref,gx_ref,gfm_ref,hg_ref):
@@ -892,65 +914,66 @@
         out_shape=[sd((T,D),f32),sd((n,2,D),f32),sd((HEAD_ROWS,D),f32)],
         compiler_params=pltpu.CompilerParams(vmem_limit_bytes=VLIM))(x,fm,hw,hb,tn)
 LAYERS=2
+NB=4
 beta_one=0.9; beta_two=0.999; adam_eps=1e-8; learn_rate=0.01; weight_decay=0.01; step_count=10.0
 def adam_update(w,g,m,v,factor):
     s=g*factor
     m2=beta_one*m+(1.0-beta_one)*s
     v2=beta_two*v+(1.0-beta_two)*s*s
-    mh=m2/(1.0-beta_one**step_count)
-    vh=v2/(1.0-beta_two**step_count)
+    mh=m2*(1.0/(1.0-beta_one**step_count))
+    vh=v2*(1.0/(1.0-beta_two**step_count))
     w2=w-learn_rate*(mh/(jnp.sqrt(vh)+adam_eps)+weight_decay*w)
     return (w2,m2,v2,w2.astype(bf))
 def inner_adam_kernel(f_ref,a0_ref,m0_ref,a1_ref,m1_ref,ada_ref,w_ref,m_ref,v_ref,*outs):
     factor=f_ref[0]; l=pl.program_id(0); j=pl.program_id(1)
     def put(sl,g):
         for o,val in zip(outs,adam_update(w_ref[0,:,sl],g,m_ref[0,:,sl],v_ref[0,:,sl],factor)): o[0,:,sl]=val
-    for a in range(2):
+    for a in range(NB):
         sl=slice(a*CW,(a+1)*CW)
         for layer,refs in enumerate(((a0_ref,m0_ref),(a1_ref,m1_ref))):
             for part,ref in enumerate(refs):
-                @pl.when(jnp.logical_and(j//4==part,l==layer))
+                @pl.when(jnp.logical_and(j//(NCH//NB)==part,l==layer))
                 def _(): put(sl,ref[0,a])
-        @pl.when(j>=8)
+        @pl.when(j>=2*NCH//NB)
         def _(): put(sl,ada_ref[0,:,sl])
 def inner_adam(factor,grads,ada,w,m,v):
-    own=w.shape[1]; C=w.shape[2]; W=2*CW
+    own=w.shape[1]; C=w.shape[2]; W=NB*CW
     blk=pl.BlockSpec((1,own,W),lambda l,j:(l,0,j))
     def gmap(layer,part):
         def index(l,j):
-            jj=jnp.clip(j-4*part,0,3); on=jnp.where(l==layer,jj,3*(l>layer))
+            jj=jnp.clip(j-(NCH//NB)*part,0,NCH//NB-1); on=jnp.where(l==layer,jj,(NCH//NB-1)*(l>layer))
             return (part,on,0,0)
-        return pl.BlockSpec((1,2,own,CW),index)
+        return pl.BlockSpec((1,NB,own,CW),index)
     sd=jax.ShapeDtypeStruct
     return pl.pallas_call(inner_adam_kernel,grid=(LAYERS,C//W),
-        in_specs=[pl.BlockSpec(memory_space=pltpu.SMEM)]+[gmap(l,p) for l in range(2) for p in range(2)]+[pl.BlockSpec((1,own,W),lambda l,j:(l,0,jnp.maximum(j-8,0))),blk,blk,blk],
+        in_specs=[pl.BlockSpec(memory_space=pltpu.SMEM)]+[gmap(l,p) for l in range(2) for p in range(2)]+[pl.BlockSpec((1,own,W),lambda l,j:(l,0,jnp.maximum(j-2*NCH//NB,0))),blk,blk,blk],
         out_specs=[blk]*4,out_shape=[sd(w.shape,f32)]*3+[sd(w.shape,bf)],
         compiler_params=pltpu.CompilerParams(vmem_limit_bytes=VLIM))(factor,*grads,ada,w,m,v)
 def outer_adam_kernel(f_ref,g0_ref,g1_ref,b_ref,w_ref,m_ref,v_ref,*outs):
     factor=f_ref[0]; l=pl.program_id(0); j=pl.program_id(1)
     def put(sl,g):
         for o,val in zip(outs,adam_update(w_ref[0,:,sl],g,m_ref[0,:,sl],v_ref[0,:,sl],factor)): o[0,:,sl]=val
-    for a in range(2):
+    for a in range(NB):
         sl=slice(a*CW,(a+1)*CW)
         for layer,ref in enumerate((g0_ref,g1_ref)):
-            @pl.when(jnp.logical_and(j<4,l==layer))
+            @pl.when(jnp.logical_and(j<NCH//NB,l==layer))
             def _(): put(sl,ref[0,a])
-    @pl.when(j==4)
+    @pl.when(j==NCH//NB)
     def _(): put(slice(0,128),b_ref[0])
 def outer_adam(factor,g0,g1,b,w,m,v):
-    own=w.shape[1]; W=2*CW
+    own=w.shape[1]; W=NB*CW
     blk=pl.BlockSpec((1,own,W),lambda l,j:(l,0,j))
     def gmap(layer):
         def index(l,j):
-            jj=jnp.minimum(j,3); on=jnp.where(l==layer,jj,3*(l>layer))
+            jj=jnp.minimum(j,NCH//NB-1); on=jnp.where(l==layer,jj,(NCH//NB-1)*(l>layer))
             return (0, on, 0, 0)
-        return pl.BlockSpec((1,2,own,CW),index)
+        return pl.BlockSpec((1,NB,own,CW),index)
     sd=jax.ShapeDtypeStruct
-    return pl.pallas_call(outer_adam_kernel,grid=(LAYERS,5),
+    return pl.pallas_call(outer_adam_kernel,grid=(LAYERS,NCH//NB+1),
         in_specs=[pl.BlockSpec(memory_space=pltpu.SMEM),gmap(0),gmap(1),pl.BlockSpec((1,own,128),lambda l,j:(l,0,0)),blk,blk,blk],
         out_specs=[blk]*4,out_shape=[sd(w.shape,f32)]*3+[sd(w.shape,bf)],
         compiler_params=pltpu.CompilerParams(vmem_limit_bytes=VLIM))(factor,g0,g1,b,w,m,v)
-P_SIZE=16; GRID=16; LAYERS=2; LAT_DEV=4; FREQ=256; NCLASS=1000
+GRID=16; LAT_DEV=4
 clip_coef=2.5
 BIAS=14
 def position_table(grid_side, feature_width):
@@ -994,22 +1017,20 @@
     fin_bias=jnp.pad(final_low[D:].astype(f32),((0,7),(0,0)))
     first=first_call(slab(0),mine_rows,small,embed_low[:,r1:r1+FREQ],second_w.reshape(own,S,own).transpose(1,0,2),table,biases2,ada_own,final_low[:D].reshape(S,own,fin_cols),fin_bias,R,S,0)
     gather0,rows_all,small,hidden,time_act,condition,cond_all,modul,fin_mod=first
-    def latent_order(a):
-        a=a.reshape(a.shape[:-2]+(S,R,8,a.shape[-1]))[...,:LAT_DEV,:]
-        return jnp.swapaxes(a,-4,-3).reshape(a.shape[:-4]+(N,a.shape[-1]))
-    rows_all=latent_order(rows_all.reshape(S*R*8,384))
+    rows_all=rows_all.reshape(S*R,8,384)[:,:LAT_DEV].reshape(N,384)
     features=rows_all[:,:FREQ].astype(bf)
     label_col=rows_all[:,FREQ:FREQ+1]
-    before=latent_order(jnp.stack([hidden,condition])).transpose(0,2,1)
-    wide=latent_order(jnp.stack([time_act,cond_all])).transpose(0,2,1,3).reshape(2,N,D)
-    time_act=wide[0]; cond_all=wide[1]
-    cond_own=lax.dynamic_slice_in_dim(cond_all,shard*own,own,1).T
+    before=jnp.stack([hidden,condition]).transpose(0,2,1)
+    cond_own=lax.dynamic_index_in_dim(cond_all.reshape(S,N,own),shard,0,False).T
+    time_act=time_act.reshape(S,N,own).transpose(1,0,2).reshape(N,D)
+    cond_all=cond_all.reshape(S,N,own).transpose(1,0,2).reshape(N,D)
+    small=small.reshape(S,48,own)
     small=small.transpose(1,0,2).reshape(48,D)
     biases=small[:LAYERS*BIAS].reshape(LAYERS,BIAS,D).astype(f32)
     patch_w=small[LAYERS*BIAS:LAYERS*BIAS+P_SIZE]; patch_b=small[LAYERS*BIAS+P_SIZE].astype(f32)
     modul=modul.reshape(LAYERS,LAT_DEV,6,D)+biases[:,None,7:13]
     modul=jnp.pad(modul,((0,0),(0,0),(0,2),(0,0)))
-    fin_mod=fin_mod[:,:LAT_DEV].transpose(1,0,2).reshape(LAT_DEV,2,D)
+    fin_mod=fin_mod.transpose(1,0,2).reshape(LAT_DEV,2,D)
     ramp=0.0001+(0.02-0.0001)*jnp.arange(1000,dtype=f32)/999.0
     upto=jnp.arange(1000,dtype=jnp.int32)[None,:]<=time_steps[:,None]
     abar=jnp.exp(jnp.sum(jnp.where(upto,jnp.log(1.0-ramp)[None,:],0.0),axis=1))
@@ -1048,7 +1069,6 @@
     gs=grad_stream.reshape(LAT_DEV,TOK,D)
     patch_grad=dot32("gpt,gtd->pd",patches,gs.astype(bf))
     patch_bias=jnp.sum(grad_stream,axis=0)[None]
-    o1=LAYERS*BIAS; o2=o1+P_SIZE+1
     cond_back=lambda squares: cond_extra((late,fin_mine,cond_own,cond_all,time_act,before,label_col,features,ada_own,final_low[:D].reshape(S,own,fin_cols),
         second_w.reshape(own,S,own).transpose(1,0,2),mod_grad(dm1_0,dm2_0).reshape(16,6*D*LAT_DEV//16),
         db1_0,db2_0,dm1_0,dm2_0,db1_1,db2_1,dm1_1,dm2_1,patch_grad,patch_bias,grad_fin,head_rows,squares),R,S)
@@ -1057,18 +1077,12 @@
     else:
         mlp0,sq_c,attn0,sq_d=sums_call(R,S,5,*attn_sums(0,low),(held,))
         rest=last_call(R,S,6,(),(),(),cond_back(squares+sq_c+sq_d))
-    ada_grad,final_turn,second,class_grad,first_grad,vectors,mine,head_total,norm_parts=rest
-    head_total=head_total.transpose(2,0,1,3).reshape(HEAD_ROWS,D)
-    mean_loss=jnp.sum(head_total[HEAD_ROWS-1,:P_SIZE])/count
-    head_total=jnp.concatenate([head_total[:P_SIZE],head_total[P_SIZE,:P_SIZE][:,None]],axis=1).T
-    embed_grad=jnp.concatenate([mine[o1:o2].T,first_grad,vectors[1,:,:1],second,vectors[0,:,:1],class_grad[:,:NCLASS]],axis=1)
-    final_turn=jnp.concatenate([final_turn,mine[o2:o2+fin_cols//own].reshape(fin_cols)[:,None]],axis=1)
-    bias_grad=mine[:o1].reshape(LAYERS,BIAS,own)
-    grad_norm=jnp.sqrt(jnp.sum(norm_parts))
+    ada_grad,final_turn,embed_grad,bias_turn,head_total,numbers=rest
+    embed_grad=embed_grad[:,:embed_table.shape[0]]; final_turn=final_turn[:,:D+1]; head_total=head_total[:,:D+1].T
+    grad_norm=numbers[0,0]; mean_loss=numbers[1,0]/count
     factor=jnp.minimum(1.0,clip_coef*math.sqrt(D/count)/grad_norm)
     out=[mean_loss,grad_norm]
     out.extend(inner_adam(factor.reshape(1),(attn0,mlp0,attn1,mlp1),ada_grad,inner_weights,inner_moment,inner_square))
-    bias_turn=jnp.pad(bias_grad.transpose(0,2,1),((0,0),(0,0),(0,128-BIAS)))
     out.extend(outer_turn(a) for a in outer_adam(factor.reshape(1),mlp0,mlp1,bias_turn,outer_turn(outer_weights),outer_turn(outer_moment),outer_turn(outer_square)))
     for w,g,m,v in ((embed_table,embed_grad.T,embed_moment,embed_square),(final_mod,final_turn.T,final_moment,final_square),
                     (head_weights,head_total,head_moment,head_square)):

time: 666 us -> 629 us (0.944)
  Pallas kernels: 572 us -> 551 us
  local copies, waits for them, and re-layouts: 45.2 us -> 36.8 us
    pallas_call x1, Pallas kernels: 76.5 us -> 68.8 us  [layer_fwd_gather(): pl.pallas_call(functools.partial(fwd_gather_kernel, R, nz, U), grid=(n,),...]
where the time goes in v5:
time: 629 us; the launch traced here: 621 us
  Pallas kernels  551 us (88%)
  local copies, waits for them, and re-layouts  36.8 us (6%)
  other arithmetic  25.6 us (4%)
    pallas_call x3, Pallas kernels, carry(): pl.pallas_call(functools.partial(carrier_kernel, R, nz, own, nu, xi, nt,...  206 us
    pallas_call x1, Pallas kernels, last_call(): pl.pallas_call(functools.partial(last_kernel, R, nz, own, sums, nt, f, le...  90.7 us
    pallas_call x1, Pallas kernels, first_call(): pl.pallas_call(functools.partial(first_kernel, R, nz, U, own), in_specs=[...  81 us
    pallas_call x1, Pallas kernels, layer_fwd_gather(): pl.pallas_call(functools.partial(fwd_gather_kernel, R, nz, U), grid=(n,),...  68.8 us
    pallas_call x1, Pallas kernels, layer_fwd(): pl.pallas_call(fwd_kernel, grid=(n,), in_specs=[rows(D), pl.BlockSpec((1,...  36.4 us
    pallas_call x1, Pallas kernels, inner_adam(): pl.pallas_call(inner_adam_kernel, grid=(LAYERS, C // W), in_specs=[pl.Blo...  26.6 us
    pallas_call x1, Pallas kernels, plain(): pl.pallas_call(kernel, grid=(args[0].shape[0] // TOK,), in_specs=specs, o...  25.9 us

profile of v5, /device:TPU:0, one launch (start us, length us, event | category | flops | bytes accessed | tf_op | source)
XLA Modules:
  0.0 620.5 jit_solution(1576062226132806665)
XLA Ops:
  0.7 0.7 convert_bitcast_fusion.2
  3.0 0.8 select_reduce_fusion
  3.9 1.0 add_convert_fusion
  4.8 0.9 slice.187
  6.4 1.0 copy.78
  8.6 1.1 slice.186
  9.7 0.9 copy.99
  12.2 0.8 slice.181
  13.8 1.1 reshape.190
  15.0 0.7 copy.97
  15.7 1.9 multiply_sine_fusion.1
  17.6 1.1 pad_maximum_fusion.2
  20.3 3.7 convert_element_type.113
  24.0 1.3 slice.185.ada_ref.refs_12_
  26.0 1.4 copy.96
  27.4 1.4 copy.95
  28.8 81.0 %shard_map.354 = (bf16[3,4,4,2,96,768]{5,4,3,2,1,0:T(8,128)(2,1)}, f32[4,2,4,8,384]{4,3,2,1,0:T(8,128)}, bf16[4,2,48,96]{3,2,1,0:T(8,128)(2,1)}, f32[128,96]{1,0...) custom-call(bf16[3,4,96,768]{3,2,1,0:T(8,128)(2,1)} %bitcast.125, ...), custom_call_target="tpu_custom_call" | custom-call | tf_op jit(solution)/shard_map/pallas_call | solution.py:378
  109.8 1.0 copy.98
  111.0 0.8 copy.77
  112.5 0.9 copy.82
  113.4 0.9 copy.83
  116.6 1.1 copy.79
  118.3 0.8 copy.84.refs_7_
  120.1 0.8 copy.85.refs_8_
  122.3 2.3 add_add_fusion
  124.5 68.8 %shard_map.355 = (bf16[1024,768]{1,0:T(8,128)(2,1)}, bf16[1024,2304]{1,0:T(8,128)(2,1)}, f32[1024,128]{1,0:T(8,128)}, bf16[1024,768]{1,0:T(8,128)(2,1)}, f32[102...) custom-call(f32[1024,768]{1,0:T(8,128)} %bitcast.120, ...), custom_call_target="tpu_custom_call" | custom-call | flops 15300820992 | bytes 60000000 | tf_op jit(solution)/shard_map/pallas_call | solution.py:411
  193.3 36.4 %shard_map.356 = (bf16[1024,768]{1,0:T(8,128)(2,1)}, bf16[1024,2304]{1,0:T(8,128)(2,1)}, f32[1024,128]{1,0:T(8,128)}, bf16[1024,768]{1,0:T(8,128)(2,1)}, f32[102...) custom-call(f32[1024,768]{1,0:T(8,128)} %get-tuple-element.108.x_ref, ...), custom_call_target="tpu_custom_call" | custom-call | flops 15300820992 | bytes 60000000 | tf_op jit(solution)/shard_map/pallas_call | solution.py:86
  229.7 6.9 %shard_map.357 = (f32[1024,768]{1,0:T(8,128)}, f32[4,2,768]{2,1,0:T(2,128)}, f32[24,768]{1,0:T(8,128)}) custom-call(f32[1024,768]{1,0:T(8,128)} %get-tuple-element.110.x_ref, f32[4,2,768]{2,1,0:T(2,128)} %reshape.198.fm_ref, bf16[768,16]{1,0:T(8,128)(2,1)} %slice.197.hw_ref, f32[1,16]{1,0:T(1,128)} %slice_convert_fusion.7.hb_ref, f32[4,16,256]{2,1,0:T(8,128)} %tn_ref.1), custom_call_target="tpu_custom_call" | custom-call | tf_op jit(solution)/shard_map/pallas_call | solution.py:911
  236.7 25.9 %shard_map.358 = (bf16[1024,768]{1,0:T(8,128)(2,1)}, bf16[1024,3072]{1,0:T(8,128)(2,1)}, f32[1024,768]{1,0:T(8,128)}, bf16[1024,768]{1,0:T(8,128)(2,1)}, bf16[10...) custom-call(f32[1024,768]{1,0:T(8,128)} %get-tuple-element.112.g_ref, ...), custom_call_target="tpu_custom_call" | custom-call | flops 10871635968 | bytes 50000000 | tf_op jit(solution)/shard_map/pallas_call | solution.py:139
  262.6 69.1 %shard_map.359 = (bf16[1024,3072]{1,0:T(8,128)(2,1)}, f32[1024,768]{1,0:T(8,128)}, f32[4,8,768]{2,1,0:T(8,128)}, f32[8,768]{1,0:T(8,128)}, f32[2,2,4,96,384]{4,3,2,1,0:T(8,128)}) custom-call(bf16[1024,768]{1,0:T(8,128)(2,1)} %get-tuple-element.117.refs_0_, bf16[1024,768]{1,0:T(8,128)(2,1)} %get-tuple-element.118.refs_1_, ...), custom_call_target="tpu_custom_call" | custom-call | flops 5637144576 | bytes 25000000 | tf_op jit(solution)/shard_map/pallas_call | solution.py:629
  331.7 0.9 slice.243
  332.6 0.9 slice.241
  334.3 66.8 %shard_map.360 = (bf16[1024,768]{1,0:T(8,128)(2,1)}, bf16[1024,3072]{1,0:T(8,128)(2,1)}, f32[1024,768]{1,0:T(8,128)}, bf16[1024,768]{1,0:T(8,128)(2,1)}, bf16[10...) custom-call(f32[1024,768]{1,0:T(8,128)} %get-tuple-element.126.refs_, ...), custom_call_target="tpu_custom_call" | custom-call | flops 10871635968 | bytes 50000000 | tf_op jit(solution)/shard_map/pallas_call | solution.py:629
  401.1 70.5 %shard_map.361 = (bf16[1024,3072]{1,0:T(8,128)(2,1)}, f32[1024,768]{1,0:T(8,128)}, f32[4,8,768]{2,1,0:T(8,128)}, f32[8,768]{1,0:T(8,128)}, f32[2,2,4,96,384]{4,3...) custom-call(bf16[1024,768]{1,0:T(8,128)(2,1)} %get-tuple-element.138.refs_0_, ...), custom_call_target="tpu_custom_call" | custom-call | flops 5637144576 | bytes 25000000 | tf_op jit(solution)/shard_map/pallas_call | solution.py:629
  471.6 1.3 add.137.refs_28_
  472.9 0.9 slice.242
  473.8 0.9 slice.240
  475.4 2.7 reshape.201.refs_4_
  478.1 0.8 constant_dynamic-slice_fusion.refs_5_
  479.0 3.2 fusion.27
  482.8 0.9 convolution_bitcast_fusion.refs_24_
  483.7 90.7 %shard_map.362 = (f32[2,8,96,384]{3,2,1,0:T(8,128)}, f32[8,128]{1,0:T(8,128)}, f32[1,8,96,384]{3,2,1,0:T(8,128)}, f32[8,128]{1,0:T(8,128)}, f32[2,96,4608]{2,1,0...) custom-call(bf16[1024,768]{1,0:T(8,128)(2,1)} %get-tuple-element.106, ...), custom_call_target="tpu_custom_call" | custom-call | tf_op jit(solution)/shard_map/pallas_call | solution.py:673
  574.5 1.3 fusion.30
  577.1 1.5 fusion.17
  578.6 3.4 fusion.20
  582.1 2.2 fusion.23
  584.3 8.1 %shard_map.364 = (f32[2,96,3086]{2,1,0:T(8,128)}, f32[2,96,3086]{2,1,0:T(8,128)}, f32[2,96,3086]{2,1,0:T(8,128)}, bf16[2,96,3086]{2,1,0:T(8,128)(2,1)}) custom-call(f32[1]{0:T(128)} %bitcast.34.f_ref, f32[2,8,96,384]{3,2,1,0:T(8,128)} %get-tuple-element.168.m0_ref.g0_ref, f32[2,8,96,384]{3,2,1,0:T(8,128)} %get-tuple-element.170.m1_ref.g1_ref, ...), custom_call_target="tpu_custom_call" | custom-call | tf_op jit(solution)/shard_map/pallas_call | solution.py:972
  592.3 26.6 %shard_map.363 = (f32[2,96,10752]{2,1,0:T(8,128)}, f32[2,96,10752]{2,1,0:T(8,128)}, f32[2,96,10752]{2,1,0:T(8,128)}, bf16[2,96,10752]{2,1,0:T(8,128)(2,1)}) custom-call(f32[1]{0:T(128)} %bitcast.34.f_ref, f32[1,8,96,384]{3,2,1,0:T(8,128)} %get-tuple-element.167.a0_ref, f32[2,8,96,384]{3,2,1,0:T(8,128)} %get-tuple-element.168.m0_ref.g0_ref, ...), custom_call_target="tpu_custom_call" | custom-call | tf_op jit(solution)/shard_map/pallas_call | solution.py:948
  (97 shorter events, 16.1 us)
Async XLA Ops:
  0.7 10.0 %copy-start.2 = (f32[2043,96]{0,1:T(8,128)S(1)}, f32[2043,96]{0,1:T(8,128)}, u32[]{:S(2)}) copy-start(f32[2043,96]{0,1:T(8,128)} %param.25) | copy-start | bytes 2353540
  10.7 2.3 copy-start.4
  10.7 8.0 %copy-start = (f32[2,3086,96]{1,2,0:T(8,128)S(1)}, f32[2,3086,96]{1,2,0:T(8,128)}, u32[]{:S(2)}) copy-start(f32[2,3086,96]{1,2,0:T(8,128)} %param.24) | copy-start | bytes 7110148
  18.7 0.7 slice-start
  109.8 9.3 %copy-start.11 = (f32[8,4608]{1,0:T(8,128)S(1)}, f32[8,4608]{1,0:T(8,128)}, u32[]{:S(2)}) copy-start(f32[8,4608]{1,0:T(8,128)} %get-tuple-element.104) | copy-start | bytes 442372
  109.8 10.1 %copy-start.9 = (bf16[4,2,128,96]{3,2,1,0:T(8,128)(2,1)S(1)}, bf16[4,2,128,96]{3,2,1,0:T(8,128)(2,1)}, u32[]{:S(2)}) copy-start(bf16[4,2,128,96]{3,2,1,0:T(8,128)(2,1)} %get-tuple-element.152) | copy-start | bytes 589828
  109.8 11.1 %copy-start.13 = (f32[4,2,4,8,384]{4,3,2,1,0:T(8,128)S(1)}, f32[4,2,4,8,384]{4,3,2,1,0:T(8,128)}, u32[]{:S(2)}) copy-start(f32[4,2,4,8,384]{4,3,2,1,0:T(8,128)} %get-tuple-element.155) | copy-start | bytes 1179652
  115.0 7.2 %copy-start.3 = (f32[256,768]{1,0:T(8,128)S(1)}, f32[256,768]{1,0:T(8,128)}, u32[]{:S(2)}) copy-start(f32[256,768]{1,0:T(8,128)} %pad_maximum_fusion.2) | copy-start | bytes 2359300
  262.6 70.0 %copy-start.12 = (f32[4,2,768]{2,1,0:T(2,128)S(1)}, f32[4,2,768]{2,1,0:T(2,128)}, u32[]{:S(2)}) copy-start(f32[4,2,768]{2,1,0:T(2,128)} %get-tuple-element.137.refs_26_) | copy-start | bytes 73732
  401.1 70.5 %copy-start.16 = (f32[8,128]{1,0:T(8,128)S(1)}, f32[8,128]{1,0:T(8,128)}, u32[]{:S(2)}) copy-start(f32[8,128]{1,0:T(8,128)} %get-tuple-element.164) | copy-start | bytes 12292
  478.1 5.6 copy-start.1
  483.7 93.4 %copy-start.10 = (f32[769,16]{0,1:T(8,128)S(1)}, f32[769,16]{0,1:T(8,128)}, u32[]{:S(2)}) copy-start(f32[769,16]{0,1:T(8,128)} %param.27) | copy-start | bytes 147652
  483.7 93.4 %copy-start.14 = (f32[769,16]{0,1:T(8,128)S(1)}, f32[769,16]{0,1:T(8,128)}, u32[]{:S(2)}) copy-start(f32[769,16]{0,1:T(8,128)} %param.36) | copy-start | bytes 147652
  483.7 93.4 %copy-start.15 = (f32[769,16]{0,1:T(8,128)S(1)}, f32[769,16]{0,1:T(8,128)}, u32[]{:S(2)}) copy-start(f32[769,16]{0,1:T(8,128)} %param.37) | copy-start | bytes 147652
  483.7 94.9 %copy-start.5 = (f32[769,192]{0,1:T(8,128)S(1)}, f32[769,192]{0,1:T(8,128)}, u32[]{:S(2)}) copy-start(f32[769,192]{0,1:T(8,128)} %param.26) | copy-start | bytes 1771780
  578.6 3.4 copy-start.6
  578.6 3.4 copy-start.7
  578.6 3.4 copy-start.8

commit v6 on v5

--- a/solution.py
+++ b/solution.py
@@ -289,8 +289,8 @@
     pl.semaphore_wait(bar,len(peers))
 
 def first_kernel(R,nz,U,own, w_ref,fo_ref,sm_ref,t1_ref,t2_ref,cls_ref,tb_ref,ada_ref,fin_ref,finb_ref,
-                 out_ref,f_ref,sg_ref,hid_ref,act_ref,con_ref,call_ref,mod_ref,fm_ref,
-                 cgs,pm,mr,ps,zrv,fps, fs1,fr1,ms,mrs,pz,pzr,vs,vr, sz,szr,sc_,scr, *gsems):
+                 out_ref,feat_ref,lab_ref,sg_ref,pre_ref,act_ref,cown_ref,call_ref,mod_ref,fm_ref,
+                 f_ref,cgs,pm,mr,ps,zrv,fps, fs1,fr1,ms,mrs,pz,pzr,vs,vr, sz,szr,sc_,scr, *gsems):
     S=2*nz; N=S*R*4
     ga=Gather(R,nz,U,w_ref,out_ref,*gsems)
     rep=lax.axis_index("rep"); shard=lax.axis_index("shard"); z=shard//2; c=lax.rem(shard,2)
@@ -321,7 +321,7 @@
     got(*small[0])
     feats=jnp.concatenate([f_ref[s//2,s%2,r,:4] for s in range(S) for r in range(R)],axis=0)
     hidden=mm_nt(feats[:,:256].astype(bf),t1_ref[...])+tb_ref[0:1,:]
-    hid_ref[...]=hidden
+    feat_ref[...]=feats[:,:256].astype(bf); lab_ref[...]=feats[:,256:257]
     act_ref[z,c]=(hidden/(1.0+jnp.exp(-hidden))).astype(bf)
     go(*small[2])
     for t in ticks[:U]: t()
@@ -331,7 +331,6 @@
     sec=mm_nt(act_ref[0,0],t2_ref[0])
     for s in range(1,S): sec=sec+mm_nt(act_ref[s//2,s%2],t2_ref[s])
     con=(sec+tb_ref[1:2,:])+con
-    con_ref[...]=con
     cond=con/(1.0+jnp.exp(-con))
     call_ref[z,c]=cond.astype(bf)
     go(*small[3])
@@ -344,6 +343,7 @@
         pm[:,:,:,sl]=v.reshape(nz,2,8,D)
     mc=send(pm.at[:,1-c],mr,ms,mrs,mate)
     mc.start()
+    pre_ref[0]=hidden.T; pre_ref[1]=con.T; cown_ref[...]=cond.T.astype(bf)
     for t in ticks[U:U+2]: t()
     mc.wait_recv()
     ps[...]=pm[:,c]+mr[...]
@@ -376,9 +376,9 @@
     dma=pltpu.SemaphoreType.DMA; V=pltpu.VMEM; sd=jax.ShapeDtypeStruct
     any_=pl.BlockSpec(memory_space=pl.ANY); vm=pl.BlockSpec(memory_space=pltpu.VMEM)
     return pl.pallas_call(functools.partial(first_kernel,R,nz,U,own),
-        in_specs=[vm]*10, out_specs=[any_]+[vm]*8,
-        out_shape=[sd((U,R,nz,2,own,W),bf),sd((nz,2,R,8,384),f32),sd((nz,2)+sm.shape,bf),sd((N,own),f32),sd((nz,2,N,own),bf),sd((N,own),f32),sd((nz,2,N,own),bf),sd((8,6*D),f32),sd((S,4,FC),f32)],
-        scratch_shapes=[V((S,R,4,own),f32),V((nz,2,8,6*D),f32),V((nz,8,6*D),f32),V((nz,8,6*D),f32),V((max(nz-1,1),8,6*D),f32),V((S,R,4,FC),f32),
+        in_specs=[vm]*10, out_specs=[any_]+[vm]*9,
+        out_shape=[sd((U,R,nz,2,own,W),bf),sd((N,256),bf),sd((N,1),f32),sd((nz,2)+sm.shape,bf),sd((2,own,N),f32),sd((nz,2,N,own),bf),sd((own,N),bf),sd((nz,2,N,own),bf),sd((8,6*D),f32),sd((S,4,FC),f32)],
+        scratch_shapes=[V((nz,2,R,8,384),f32),V((S,R,4,own),f32),V((nz,2,8,6*D),f32),V((nz,8,6*D),f32),V((nz,8,6*D),f32),V((max(nz-1,1),8,6*D),f32),V((S,R,4,FC),f32),
             dma((R-1,)),dma((R-1,)),dma(()),dma(()),dma((nz-1,)),dma((nz-1,)),dma((S-1,)),dma((S-1,)),dma((4,nz-1)),dma((4,nz-1)),dma((4,)),dma((4,))]+gather_sems(R,nz,U),
         compiler_params=pltpu.CompilerParams(collective_id=cid,has_side_effects=True,vmem_limit_bytes=VLIM),
     )(w,fo,sm,t1,t2,cls,tb,ada,fin,finb)
@@ -1016,12 +1016,7 @@
     ada_own=inner_low[:,:,4*D+FF:]
     fin_bias=jnp.pad(final_low[D:].astype(f32),((0,7),(0,0)))
     first=first_call(slab(0),mine_rows,small,embed_low[:,r1:r1+FREQ],second_w.reshape(own,S,own).transpose(1,0,2),table,biases2,ada_own,final_low[:D].reshape(S,own,fin_cols),fin_bias,R,S,0)
-    gather0,rows_all,small,hidden,time_act,condition,cond_all,modul,fin_mod=first
-    rows_all=rows_all.reshape(S*R,8,384)[:,:LAT_DEV].reshape(N,384)
-    features=rows_all[:,:FREQ].astype(bf)
-    label_col=rows_all[:,FREQ:FREQ+1]
-    before=jnp.stack([hidden,condition]).transpose(0,2,1)
-    cond_own=lax.dynamic_index_in_dim(cond_all.reshape(S,N,own),shard,0,False).T
+    gather0,features,label_col,small,before,time_act,cond_own,cond_all,modul,fin_mod=first
     time_act=time_act.reshape(S,N,own).transpose(1,0,2).reshape(N,D)
     cond_all=cond_all.reshape(S,N,own).transpose(1,0,2).reshape(N,D)
     small=small.reshape(S,48,own)

time: 629 us -> 624 us (level)
  no operation moved by 1% of the time
where the time goes in v6:
time: 624 us; the launch traced here: 616 us
  Pallas kernels  551 us (88%)
  local copies, waits for them, and re-layouts  33 us (5%)
  other arithmetic  25 us (4%)
    pallas_call x3, Pallas kernels, carry(): pl.pallas_call(functools.partial(carrier_kernel, R, nz, own, nu, xi, nt,...  206 us
    pallas_call x1, Pallas kernels, last_call(): pl.pallas_call(functools.partial(last_kernel, R, nz, own, sums, nt, f, le...  90.7 us
    pallas_call x1, Pallas kernels, first_call(): pl.pallas_call(functools.partial(first_kernel, R, nz, U, own), in_specs=[...  80.9 us
    pallas_call x1, Pallas kernels, layer_fwd_gather(): pl.pallas_call(functools.partial(fwd_gather_kernel, R, nz, U), grid=(n,),...  68.8 us
    pallas_call x1, Pallas kernels, layer_fwd(): pl.pallas_call(fwd_kernel, grid=(n,), in_specs=[rows(D), pl.BlockSpec((1,...  36.4 us
    pallas_call x1, Pallas kernels, inner_adam(): pl.pallas_call(inner_adam_kernel, grid=(LAYERS, C // W), in_specs=[pl.Blo...  26.6 us
    pallas_call x1, Pallas kernels, plain(): pl.pallas_call(kernel, grid=(args[0].shape[0] // TOK,), in_specs=specs, o...  25.9 us

profile of v6, /device:TPU:0, one launch (start us, length us, event | category | flops | bytes accessed | tf_op | source)
XLA Modules:
  0.0 615.9 jit_solution(7574832036083482549)
XLA Ops:
  0.7 0.7 convert_bitcast_fusion.2
  3.0 0.8 select_reduce_fusion
  3.9 1.0 add_convert_fusion
  4.8 0.9 slice.174
  6.4 1.0 copy.72
  8.6 1.1 slice.173
  9.7 0.9 copy.90
  11.5 0.7 slice.167.t1_ref
  12.2 0.8 slice.168
  13.1 0.7 pad.32.cls_ref
  13.8 1.1 reshape.183
  15.0 0.7 copy.88
  15.7 1.9 multiply_sine_fusion.1
  17.6 1.1 pad_maximum_fusion.2
  20.3 3.7 convert_element_type.112
  24.0 1.3 slice.172.ada_ref.refs_12_
  26.0 1.4 copy.87
  27.4 1.4 copy.86
  28.8 80.9 %shard_map.354 = (bf16[3,4,4,2,96,768]{5,4,3,2,1,0:T(8,128)(2,1)}, bf16[128,256]{1,0:T(8,128)(2,1)}, f32[128,1]{1,0:T(8,128)}, bf16[4,2,48,96]{3,2,1,0:T(8,128)(...) custom-call(bf16[3,4,96,768]{3,2,1,0:T(8,128)(2,1)} %bitcast.116, ...), custom_call_target="tpu_custom_call" | custom-call | tf_op jit(solution)/shard_map/pallas_call | solution.py:378
  109.7 1.0 copy.89
  111.0 0.8 copy.71
  114.0 1.0 reshape.187
  115.8 0.8 copy.75.refs_7_
  116.8 0.8 copy.76.refs_8_
  117.6 2.3 add_add_fusion
  119.9 68.8 %shard_map.355 = (bf16[1024,768]{1,0:T(8,128)(2,1)}, bf16[1024,2304]{1,0:T(8,128)(2,1)}, f32[1024,128]{1,0:T(8,128)}, bf16[1024,768]{1,0:T(8,128)(2,1)}, f32[102...) custom-call(f32[1024,768]{1,0:T(8,128)} %bitcast.111, ...), custom_call_target="tpu_custom_call" | custom-call | flops 15300820992 | bytes 60000000 | tf_op jit(solution)/shard_map/pallas_call | solution.py:411
  188.7 36.4 %shard_map.356 = (bf16[1024,768]{1,0:T(8,128)(2,1)}, bf16[1024,2304]{1,0:T(8,128)(2,1)}, f32[1024,128]{1,0:T(8,128)}, bf16[1024,768]{1,0:T(8,128)(2,1)}, f32[102...) custom-call(f32[1024,768]{1,0:T(8,128)} %get-tuple-element.109.x_ref, ...), custom_call_target="tpu_custom_call" | custom-call | flops 15300820992 | bytes 60000000 | tf_op jit(solution)/shard_map/pallas_call | solution.py:86
  225.1 7.0 %shard_map.357 = (f32[1024,768]{1,0:T(8,128)}, f32[4,2,768]{2,1,0:T(2,128)}, f32[24,768]{1,0:T(8,128)}) custom-call(f32[1024,768]{1,0:T(8,128)} %get-tuple-element.111.x_ref, f32[4,2,768]{2,1,0:T(2,128)} %reshape.191.fm_ref, bf16[768,16]{1,0:T(8,128)(2,1)} %slice.184.hw_ref, f32[1,16]{1,0:T(1,128)} %slice_convert_fusion.6.hb_ref, f32[4,16,256]{2,1,0:T(8,128)} %tn_ref.1), custom_call_target="tpu_custom_call" | custom-call | tf_op jit(solution)/shard_map/pallas_call | solution.py:911
  232.1 25.9 %shard_map.358 = (bf16[1024,768]{1,0:T(8,128)(2,1)}, bf16[1024,3072]{1,0:T(8,128)(2,1)}, f32[1024,768]{1,0:T(8,128)}, bf16[1024,768]{1,0:T(8,128)(2,1)}, bf16[10...) custom-call(f32[1024,768]{1,0:T(8,128)} %get-tuple-element.113.g_ref, ...), custom_call_target="tpu_custom_call" | custom-call | flops 10871635968 | bytes 50000000 | tf_op jit(solution)/shard_map/pallas_call | solution.py:139
  258.0 69.2 %shard_map.359 = (bf16[1024,3072]{1,0:T(8,128)(2,1)}, f32[1024,768]{1,0:T(8,128)}, f32[4,8,768]{2,1,0:T(8,128)}, f32[8,768]{1,0:T(8,128)}, f32[2,2,4,96,384]{4,3,2,1,0:T(8,128)}) custom-call(bf16[1024,768]{1,0:T(8,128)(2,1)} %get-tuple-element.118.refs_0_, bf16[1024,768]{1,0:T(8,128)(2,1)} %get-tuple-element.119.refs_1_, ...), custom_call_target="tpu_custom_call" | custom-call | flops 5637144576 | bytes 25000000 | tf_op jit(solution)/shard_map/pallas_call | solution.py:629
  327.1 0.9 slice.225
  328.1 0.9 slice.223
  329.7 66.8 %shard_map.360 = (bf16[1024,768]{1,0:T(8,128)(2,1)}, bf16[1024,3072]{1,0:T(8,128)(2,1)}, f32[1024,768]{1,0:T(8,128)}, bf16[1024,768]{1,0:T(8,128)(2,1)}, bf16[10...) custom-call(f32[1024,768]{1,0:T(8,128)} %get-tuple-element.127.refs_, ...), custom_call_target="tpu_custom_call" | custom-call | flops 10871635968 | bytes 50000000 | tf_op jit(solution)/shard_map/pallas_call | solution.py:629
  396.5 70.5 %shard_map.361 = (bf16[1024,3072]{1,0:T(8,128)(2,1)}, f32[1024,768]{1,0:T(8,128)}, f32[4,8,768]{2,1,0:T(8,128)}, f32[8,768]{1,0:T(8,128)}, f32[2,2,4,96,384]{4,3...) custom-call(bf16[1024,768]{1,0:T(8,128)(2,1)} %get-tuple-element.139.refs_0_, ...), custom_call_target="tpu_custom_call" | custom-call | flops 5637144576 | bytes 25000000 | tf_op jit(solution)/shard_map/pallas_call | solution.py:629
  467.0 1.3 add.132.refs_28_
  468.3 0.9 slice.224
  469.2 0.9 slice.222
  470.8 2.7 reshape.194.refs_4_
  473.5 0.8 constant_dynamic-slice_fusion.refs_5_
  474.4 3.2 fusion.27
  478.2 0.9 convolution_bitcast_fusion.refs_24_
  479.1 90.7 %shard_map.362 = (f32[2,8,96,384]{3,2,1,0:T(8,128)}, f32[8,128]{1,0:T(8,128)}, f32[1,8,96,384]{3,2,1,0:T(8,128)}, f32[8,128]{1,0:T(8,128)}, f32[2,96,4608]{2,1,0...) custom-call(bf16[1024,768]{1,0:T(8,128)(2,1)} %get-tuple-element.107, ...), custom_call_target="tpu_custom_call" | custom-call | tf_op jit(solution)/shard_map/pallas_call | solution.py:673
  569.8 1.3 fusion.30
  572.5 1.5 fusion.17
  574.0 3.4 fusion.20
  577.4 2.2 fusion.23
  579.6 8.1 %shard_map.364 = (f32[2,96,3086]{2,1,0:T(8,128)}, f32[2,96,3086]{2,1,0:T(8,128)}, f32[2,96,3086]{2,1,0:T(8,128)}, bf16[2,96,3086]{2,1,0:T(8,128)(2,1)}) custom-call(f32[1]{0:T(128)} %bitcast.28.f_ref, f32[2,8,96,384]{3,2,1,0:T(8,128)} %get-tuple-element.170.m0_ref.g0_ref, f32[2,8,96,384]{3,2,1,0:T(8,128)} %get-tuple-element.172.m1_ref.g1_ref, ...), custom_call_target="tpu_custom_call" | custom-call | tf_op jit(solution)/shard_map/pallas_call | solution.py:972
  587.7 26.6 %shard_map.363 = (f32[2,96,10752]{2,1,0:T(8,128)}, f32[2,96,10752]{2,1,0:T(8,128)}, f32[2,96,10752]{2,1,0:T(8,128)}, bf16[2,96,10752]{2,1,0:T(8,128)(2,1)}) custom-call(f32[1]{0:T(128)} %bitcast.28.f_ref, f32[1,8,96,384]{3,2,1,0:T(8,128)} %get-tuple-element.169.a0_ref, f32[2,8,96,384]{3,2,1,0:T(8,128)} %get-tuple-element.170.m0_ref.g0_ref, ...), custom_call_target="tpu_custom_call" | custom-call | tf_op jit(solution)/shard_map/pallas_call | solution.py:948
  (87 shorter events, 12.2 us)
Async XLA Ops:
  0.7 10.0 %copy-start.2 = (f32[2043,96]{0,1:T(8,128)S(1)}, f32[2043,96]{0,1:T(8,128)}, u32[]{:S(2)}) copy-start(f32[2043,96]{0,1:T(8,128)} %param.25) | copy-start | bytes 2353540
  10.7 2.3 copy-start.4
  10.7 8.0 %copy-start = (f32[2,3086,96]{1,2,0:T(8,128)S(1)}, f32[2,3086,96]{1,2,0:T(8,128)}, u32[]{:S(2)}) copy-start(f32[2,3086,96]{1,2,0:T(8,128)} %param.24) | copy-start | bytes 7110148
  18.7 0.7 slice-start
  109.7 6.0 copy-start.10
  109.7 6.9 %copy-start.9 = (bf16[4,2,128,96]{3,2,1,0:T(8,128)(2,1)S(1)}, bf16[4,2,128,96]{3,2,1,0:T(8,128)(2,1)}, u32[]{:S(2)}) copy-start(bf16[4,2,128,96]{3,2,1,0:T(8,128)(2,1)} %get-tuple-element.154) | copy-start | bytes 589828
  109.7 7.9 %copy-start.3 = (f32[256,768]{1,0:T(8,128)S(1)}, f32[256,768]{1,0:T(8,128)}, u32[]{:S(2)}) copy-start(f32[256,768]{1,0:T(8,128)} %pad_maximum_fusion.2) | copy-start | bytes 2359300
  258.0 70.1 %copy-start.12 = (f32[4,2,768]{2,1,0:T(2,128)S(1)}, f32[4,2,768]{2,1,0:T(2,128)}, u32[]{:S(2)}) copy-start(f32[4,2,768]{2,1,0:T(2,128)} %get-tuple-element.138.refs_26_) | copy-start | bytes 73732
  396.5 70.5 %copy-start.15 = (f32[8,128]{1,0:T(8,128)S(1)}, f32[8,128]{1,0:T(8,128)}, u32[]{:S(2)}) copy-start(f32[8,128]{1,0:T(8,128)} %get-tuple-element.166) | copy-start | bytes 12292
  473.5 5.6 copy-start.1
  479.1 93.3 %copy-start.11 = (f32[769,16]{0,1:T(8,128)S(1)}, f32[769,16]{0,1:T(8,128)}, u32[]{:S(2)}) copy-start(f32[769,16]{0,1:T(8,128)} %param.27) | copy-start | bytes 147652
  479.1 93.3 %copy-start.13 = (f32[769,16]{0,1:T(8,128)S(1)}, f32[769,16]{0,1:T(8,128)}, u32[]{:S(2)}) copy-start(f32[769,16]{0,1:T(8,128)} %param.36) | copy-start | bytes 147652
  479.1 93.4 %copy-start.14 = (f32[769,16]{0,1:T(8,128)S(1)}, f32[769,16]{0,1:T(8,128)}, u32[]{:S(2)}) copy-start(f32[769,16]{0,1:T(8,128)} %param.37) | copy-start | bytes 147652
  479.1 94.9 %copy-start.5 = (f32[769,192]{0,1:T(8,128)S(1)}, f32[769,192]{0,1:T(8,128)}, u32[]{:S(2)}) copy-start(f32[769,192]{0,1:T(8,128)} %param.26) | copy-start | bytes 1771780
  574.0 3.4 copy-start.6
  574.0 3.4 copy-start.7
  574.0 3.4 copy-start.8
